TPU v7x, 32 devices: a whole 2x2x4 slice. The times are simulated.
32 devices in a mesh: ens: 2 (over y), lat: 4 (over z), lon: 2 (over x), lev: 2 (over core).
Axes of the slice: x: 2, y: 2, z: 4, core: 2. Of those that a mesh axis runs over, the one named last changes fastest.
Arguments:
- tracers: float32 [4, 64, 16, 256], P('lev', 'ens', 'lat', 'lon'), parts along dimension 1, may hold values from -6 to 6
- face_winds: float32 [2, 64, 16, 256], P(None, 'ens', 'lat', 'lon'), parts along dimension 1, may hold values from -0.25 to 0.25
- inverse_mass: float32 [64, 16, 256], P('ens', 'lat', 'lon'), parts along dimension 0, may hold values from 0.5 to 1
- span_owner: int32 [16, 256], P('lat', 'lon'), may hold values from 0 to 7, as said below
- span_slot: int32 [16, 256], P('lat', 'lon'), may hold values from 0 to 639, as said below
- span_column_count: int32 [40], P(('lat', 'lon')), may hold values from 1 to 128, as said below
- diffusivity: float32 [62, 5120], P('ens', ('lat', 'lon')), parts along dimension 0, may hold values from 0.2 to 2
Outputs:
- tracers_out: float32 [4, 64, 16, 256], P('lev', 'ens', 'lat', 'lon'), parts along dimension 1
- diffusivity_out: float32 [62, 5120], P('ens', ('lat', 'lon')), parts along dimension 0
There are 2 independent parts, one for each index of `ens`. A program takes and returns all parts, laid end to end along the dimension named above; an argument that names none is the same for every part. Nothing has to cross between parts.
Inputs may be any that keep to these rules, and one draw needn't show every extreme that they name: `span_owner`: owners are numbered over lat+lon with lat slowest. Each device's block sends columns to exactly 4 distinct owners, exactly 128 columns to each, and every owner takes 4 * 128 columns in all. `span_slot`: slot s of an owner lies in its span s // 128 at position s % 128, below that span's count; no two columns share an owner and slot, and every slot below its span's count holds a column. `span_column_count`: span c belongs to owner c // 5; every owner's counts sum to 512, and every owner's last span holds exactly 128 columns.
All inputs are finite; a program needn't handle non-finite values.
Results may differ from a plain program's by a relative error of at most 0.00002.
Values sent between devices are 32-bit elements; how exact they have to be, the bound alone decides.
No kernel may reach another device: no remote copies, remote signals or barrier semaphores. Data moves between devices by JAX's collectives and lax.ppermute only.
A program may use at most 64 MiB of HBM per device.

v0:
```python
import jax
import jax.numpy as jnp
from jax import lax
from jax.sharding import PartitionSpec as P


def with_halo(block, sides, width):
    for axis, dim in sides:
        count = lax.axis_size(axis)
        forward = [(i, i + 1) for i in range(count - 1)]
        forward.append((count - 1, 0))
        backward = [(target, source) for source, target in forward]
        low = lax.ppermute(
            lax.slice_in_dim(block, block.shape[dim] - width, None, axis=dim), axis, forward
        )
        high = lax.ppermute(lax.slice_in_dim(block, 0, width, axis=dim), axis, backward)
        block = jnp.concatenate([low, block, high], axis=dim)
    return block


def advect(tracer_field, east_wind, north_wind, inverse_mass, open_rows):
    east_flux = (
        jnp.maximum(east_wind[..., :-1], 0.0) * tracer_field[..., :-1]
        + jnp.minimum(east_wind[..., :-1], 0.0) * tracer_field[..., 1:]
    )
    north_flux = (
        jnp.maximum(north_wind[..., :-1, :], 0.0) * tracer_field[..., :-1, :]
        + jnp.minimum(north_wind[..., :-1, :], 0.0) * tracer_field[..., 1:, :]
    ) * open_rows[:-1, None]
    zonal_div = east_flux[..., 1:-1, 1:] - east_flux[..., 1:-1, :-1]
    merid_div = north_flux[..., 1:, 1:-1] - north_flux[..., :-1, 1:-1]
    return tracer_field[..., 1:-1, 1:-1] - inverse_mass[..., 1:-1, 1:-1] * (zonal_div + merid_div)


def new_diffusivity(previous, wind_shear, active):
    return jnp.where(active, 0.5 * previous + 2.0 * wind_shear / (0.05 + wind_shear), previous)


def implicit_diffusion(tracer_field, diffus, active):
    layers = tracer_field.shape[-2]
    ratios = []
    sweeps = []
    lower_kv = jnp.zeros_like(diffus[0])
    for layer_idx in range(layers):
        upper_kv = diffus[layer_idx] if layer_idx < layers - 1 else jnp.zeros_like(diffus[0])
        pivot_sum = 1.0 + lower_kv + upper_kv
        rhs_value = tracer_field[..., layer_idx, :]
        if layer_idx > 0:
            pivot_sum = pivot_sum - lower_kv * ratios[-1]
            rhs_value = rhs_value + lower_kv * sweeps[-1]
        ratios.append(upper_kv / pivot_sum)
        sweeps.append(rhs_value / pivot_sum)
        lower_kv = upper_kv
    result = [sweeps[-1]]
    for layer_idx in range(layers - 2, -1, -1):
        result.append(sweeps[layer_idx] + ratios[layer_idx] * result[-1])
    solved = jnp.stack(result[::-1], axis=-2)
    return jnp.where(active, solved, tracer_field)


def regroup(send_block):
    return lax.all_to_all(send_block, ("lat", "lon"), split_axis=1, concat_axis=1, tiled=True)


def on_device(
    tracers, face_winds, inverse_mass, span_owner, span_slot, span_column_count, diffusivity
):
    own_count = tracers.shape[0]
    level_stack = tracers.shape[1]
    lat_rows = tracers.shape[2]
    lon_cols = tracers.shape[3]
    lat_count = lax.axis_size("lat")
    devices = lat_count * lax.axis_size("lon")
    per_device = lat_rows * lon_cols
    group_size = per_device * 2 // devices
    buffer_len = devices * group_size
    slot_total = diffusivity.shape[1]
    span_cols = slot_total // span_column_count.shape[0]

    def open_for(margin):
        first_row = lax.axis_index("lat") * lat_rows - margin
        glob_rows = first_row + jnp.arange(lat_rows + 2 * margin, dtype=jnp.int32)
        return ((glob_rows >= 0) & (glob_rows < lat_rows * lat_count - 1)).astype(jnp.float32)

    stacked = jnp.concatenate([tracers, face_winds, inverse_mass[None]], axis=0)
    padded = with_halo(stacked, (("lat", 2), ("lon", 3)), 1)
    advected = advect(
        padded[:own_count],
        padded[own_count],
        padded[own_count + 1],
        padded[own_count + 2],
        open_for(1),
    )
    bordered = with_halo(advected, (("lat", 2), ("lon", 3)), 1)
    advected = advect(
        bordered, padded[own_count], padded[own_count + 1], padded[own_count + 2], open_for(1)
    )
    east_step = face_winds[0, 1:] - face_winds[0, :-1]
    north_step = face_winds[1, 1:] - face_winds[1, :-1]
    wind_shear = (east_step * east_step + north_step * north_step).reshape(
        level_stack - 1, per_device
    )
    columns = advected.reshape(own_count * level_stack, per_device)
    owner_flat = span_owner.reshape(-1)
    sorted_order = jnp.argsort(owner_flat, stable=True)
    sorted_owner = owner_flat[sorted_order]
    per_owner = jnp.sum(
        (owner_flat[:, None] == jnp.arange(devices, dtype=jnp.int32)[None, :]).astype(jnp.int32),
        axis=0,
    )
    owner_start = jnp.cumsum(per_owner) - per_owner
    sorted_pos = (
        sorted_owner * group_size
        + jnp.arange(per_device, dtype=jnp.int32)
        - owner_start[sorted_owner]
    )
    buffer_pos = jnp.zeros((per_device,), jnp.int32).at[sorted_order].set(sorted_pos)
    slot_row = (
        jnp.full((1, buffer_len), -1.0, jnp.float32)
        .at[0, buffer_pos]
        .set(span_slot.reshape(-1).astype(jnp.float32))
    )
    slot_position_index = jnp.arange(slot_total, dtype=jnp.int32)
    slot_is_active = slot_position_index % span_cols < jnp.repeat(
        span_column_count, span_cols, total_repeat_length=slot_total
    )
    payload = jnp.concatenate([columns, wind_shear], axis=0)
    outgoing = jnp.concatenate(
        [
            jnp.zeros((payload.shape[0], buffer_len), jnp.float32).at[:, buffer_pos].set(payload),
            slot_row,
        ],
        axis=0,
    )
    arrived = regroup(outgoing)
    target_slot = jnp.where(arrived[-1] < 0.0, slot_total, arrived[-1]).astype(jnp.int32)
    in_spans = (
        jnp.zeros((arrived.shape[0] - 1, slot_total), jnp.float32)
        .at[:, target_slot]
        .set(arrived[:-1], mode="drop")
    )
    span_kv = new_diffusivity(diffusivity, in_spans[own_count * level_stack :], slot_is_active)
    span_fields = in_spans[: own_count * level_stack].reshape(own_count, level_stack, slot_total)
    span_diffused = implicit_diffusion(span_fields, span_kv, slot_is_active)
    lookup_slot = jnp.clip(target_slot, 0, slot_total - 1)
    returned = regroup(span_diffused.reshape(own_count * level_stack, slot_total)[:, lookup_slot])
    tracers_out = returned[:, buffer_pos].reshape(own_count, level_stack, per_device)
    return (tracers_out.reshape(own_count, level_stack, lat_rows, lon_cols), span_kv)


def solution(mesh):
    placed = (
        P("lev", "ens", "lat", "lon"),
        P(None, "ens", "lat", "lon"),
        P("ens", "lat", "lon"),
        P("lat", "lon"),
        P("lat", "lon"),
        P(("lat", "lon")),
        P("ens", ("lat", "lon")),
    )
    return jax.shard_map(
        on_device,
        mesh=mesh,
        in_specs=placed,
        out_specs=(P("lev", "ens", "lat", "lon"), P("ens", ("lat", "lon"))),
        check_vma=False,
    )
```

profile of v0, /device:TPU:0, one launch (start us, length us, event | category | flops | bytes accessed | tf_op | source)
XLA Modules:
  0.0 101.3 jit_solution(5122609256926340873)
XLA Ops:
  0.6 0.9 copy.344
  1.6 0.9 copy-done.2
  2.5 5.1 %collective-permute-start.1 = (f32[5,32,1,128]{3,1,2,0:T(8,128)S(1)}, f32[5,32,1,128]{3,1,2,0:T(8,128)S(1)}, u32[]{:S(2)}, u32[]{:S(2)}) collective-permute-start(f32[5,32,1,128]{3,1,2,0:T(8,128)S(1)} %get-tuple-element.226), channel_id=1, source_target_pairs={{4,0},{8,4},{12,8},{0,12},{5,1},{9,5},{13,9},{1,13},{6,2},{10,6},{... | collective-permute-start | bytes 245768 | tf_op jit(solution)/shard_map/ppermute | solution.py:16
  7.7 0.7 copy-done
  8.4 3.8 %sort.17 = (s32[512]{0:T(512)}, s32[512]{0:T(512)S(1)}) sort(s32[512]{0:T(512)S(1)} %bitcast.107, s32[512]{0:T(512)S(1)} %iota.26), dimensions={0}, to_apply=%region_0.0 | sort | flops 4608 | bytes 8192 | tf_op jit(solution)/shard_map/jit(argsort)/sort | solution.py:105
  12.2 3.5 %gather_fusion = s32[512]{0:T(512)S(1)} fusion(s32[512]{0:T(512)S(1)} %bitcast.108, s32[1024]{0:T(1024)S(1)} %pad_clamp_fusion.1), kind=kCustom, calls=%fused_computation | custom fusion | bytes 6144 | tf_op jit(solution)/shard_map/gather | solution.py:106
  15.9 0.7 fusion.135
  16.6 4.4 %compare_select_fusion.10 = s32[512,1]{0,1:T(1,128)S(1)} fusion(s32[]{:T(128)} %bitcast.12, s32[]{:T(128)} %bitcast.13, s32[]{:T(128)} %bitcast.14, s32[]{:T(128)} %bitcast.15, s32[]{:T(128)} %bitcast.16, s32[]{:T(128)} %bitcast.18, s32[]{:T(128)} %bitcast.17, s32[512,1]{0,1:T(1,128)S(1)} %bitcast.129), kind=kLoop, calls=%fused_computation.207 | loop fusion | flops 7680 | bytes 4124 | tf_op jit(solution)/shard_map/gather | solution.py:115
  21.0 0.7 select_subtract_fusion
  22.0 0.3 copy.170
  22.3 1.5 %collective-permute-start.3 = (f32[5,32,6,1]{1,2,3,0:T(8,128)S(1)}, f32[5,32,6,1]{1,2,3,0:T(8,128)S(1)}, u32[]{:S(2)}, u32[]{:S(2)}) collective-permute-start(f32[5,32,6,1]{1,2,3,0:T(8,128)S(1)} %copy.170), channel_id=1, source_target_pairs={{2,0},{0,2},{3,1},{1,3},{6,4},{4,6},{7,5},{5,7},{10,8},{8,10},{11,... | collective-permute-start | bytes 11528 | tf_op jit(solution)/shard_map/ppermute | solution.py:16
  23.8 0.3 copy.169
  24.1 0.6 collective-permute-start.2
  24.7 2.4 %scatter_custom_fusion = s32[512]{0:T(512)S(1)} fusion(s32[512]{0:T(512)S(1)} %compare_select_fusion.17, s32[512]{0:T(512)S(1)} %select_subtract_fusion, s32[]{:T(128)} %constant.120.clone.1), kind=kCustom, calls=%fused_computation.334 | custom fusion | bytes 2052 | tf_op jit(solution)/shard_map/scatter | solution.py:117
  27.4 0.5 collective-permute-done.2
  28.2 0.4 pad_maximum_fusion
  29.3 3.9 %collective-permute-start.5 = (f32[2,32,1,128]{3,1,2,0:T(8,128)S(1)}, f32[2,32,1,128]{3,1,2,0:T(8,128)S(1)}, u32[]{:S(2)}, u32[]{:S(2)}) collective-permute-start(f32[2,32,1,128]{3,1,2,0:T(8,128)S(1)} %get-tuple-element.266), channel_id=1, source_target_pairs={{4,0},{8,4},{12,8},{0,12},{5,1},{9,5},{13,9},{1,13},{6,2},{10,6},{... | collective-permute-start | bytes 98312 | tf_op jit(solution)/shard_map/ppermute | solution.py:16
  33.2 1.6 %collective-permute-done.5 = f32[2,32,1,128]{3,1,2,0:T(8,128)S(1)} collective-permute-done((f32[2,32,1,128]{3,1,2,0:T(8,128)S(1)}, f32[2,32,1,128]{3,1,2,0:T(8,128)S(1)}, u32[]{:S(2)}, u32[]{:S(2)}) %collective-permute-start.5) | collective-permute-done | bytes 32800 | tf_op jit(solution)/shard_map/ppermute | solution.py:16
  34.8 4.1 %collective-permute-done.4 = f32[2,32,1,128]{3,1,2,0:T(8,128)S(1)} collective-permute-done((f32[2,32,1,128]{3,1,2,0:T(8,128)S(1)}, f32[2,32,1,128]{3,1,2,0:T(8,128)S(1)}, u32[]{:S(2)}, u32[]{:S(2)}) %collective-permute-start.4) | collective-permute-done | bytes 32800 | tf_op jit(solution)/shard_map/ppermute | solution.py:13
  39.1 1.0 %collective-permute-start.7 = (f32[2,32,6,1]{3,1,2,0:T(8,128)S(1)}, f32[2,32,6,1]{3,1,2,0:T(8,128)S(1)}, u32[]{:S(2)}, u32[]{:S(2)}) collective-permute-start(f32[2,32,6,1]{3,1,2,0:T(8,128)S(1)} %get-tuple-element.228), channel_id=1, source_target_pairs={{2,0},{0,2},{3,1},{1,3},{6,4},{4,6},{7,5},{5,7},{10,8},{8,10},{11,... | collective-permute-start | bytes 4616 | tf_op jit(solution)/shard_map/ppermute | solution.py:16
  40.1 1.1 %collective-permute-start.6 = (f32[2,32,6,1]{3,1,2,0:T(8,128)S(1)}, f32[2,32,6,1]{3,1,2,0:T(8,128)S(1)}, u32[]{:S(2)}, u32[]{:S(2)}) collective-permute-start(f32[2,32,6,1]{3,1,2,0:T(8,128)S(1)} %get-tuple-element.227), channel_id=1, source_target_pairs={{0,2},{2,0},{1,3},{3,1},{4,6},{6,4},{5,7},{7,5},{8,10},{10,8},{9,1... | collective-permute-start | bytes 4616 | tf_op jit(solution)/shard_map/ppermute | solution.py:13
  41.2 2.4 %scatter_custom_fusion.2 = f32[1024]{0:T(1024)S(1)} fusion(s32[512]{0:T(512)S(1)} %compare_select_fusion.16, f32[512]{0:T(512)S(1)} %convert_bitcast_fusion, f32[]{:T(128)} %constant.133.clone.1), kind=kCustom, calls=%fused_computation.328 | custom fusion | bytes 4100 | tf_op jit(solution)/shard_map/scatter | solution.py:121
  43.9 1.0 collective-permute-done.7
  44.8 2.1 %collective-permute-done.6 = f32[2,32,6,1]{3,1,2,0:T(8,128)S(1)} collective-permute-done((f32[2,32,6,1]{3,1,2,0:T(8,128)S(1)}, f32[2,32,6,1]{3,1,2,0:T(8,128)S(1)}, u32[]{:S(2)}, u32[]{:S(2)}) %collective-permute-start.6) | collective-permute-done | bytes 1568 | tf_op jit(solution)/shard_map/ppermute | solution.py:13
  47.9 1.8 %scatter_custom_fusion.1 = f32[95,1024]{0,1:T(8,128)S(1)} fusion(s32[512]{0:T(512)S(1)} %compare_select_fusion.16, f32[512,95]{1,0:T(8,128)S(1)} %copy.122, f32[]{:T(128)} %constant.126.clone.1), kind=kCustom, calls=%fused_computation.132 | custom fusion | bytes 389124 | tf_op jit(solution)/shard_map/scatter | solution.py:130
  50.0 0.9 copy.124
  50.9 3.6 %all-to-all-start = ((f32[96,8,128]{2,0,1:T(8,128)}), f32[96,8,128]{2,0,1:T(8,128)S(1)}, u32[]{:S(2)}, u32[]{:S(2)}) async-start(f32[96,8,128]{2,0,1:T(8,128)} %copy.124), calls=%async_computation | async-start | bytes 786432 | tf_op jit(solution)/shard_map/all_to_all | solution.py:62
  54.7 0.5 copy-done.4
  55.1 0.7 fusion.134
  55.8 3.2 %fusion.63 = s32[640]{0:T(1024)S(1)} fusion(s32[1,1,5,128]{3,2,1,0:T(8,128)S(1)} %get-tuple-element.281, s32[1,1,5,128]{3,2,1,0:T(8,128)S(1)} %get-tuple-element.280, s32[]{:T(128)} %bitcast.2, s32[]{:T(128)} %bitcast.3, s32[]{:T(128)} %bitcast.4, s32[]{:T(128)} %bitcast.6, s32[]{:T(128)} %bitcast.5), kind=kLoop, calls=%fused_computation.326 | loop fusion | flops 6400 | bytes 7700 | tf_op jit(solution)/shard_map/jit(_take)/gather | solution.py:124
  59.1 4.5 %all-to-all-done = f32[96,8,128]{2,0,1:T(8,128)S(1)} async-done(((f32[96,8,128]{2,0,1:T(8,128)}), f32[96,8,128]{2,0,1:T(8,128)S(1)}, u32[]{:S(2)}, u32[]{:S(2)}) %all-to-all-start) | async-done | bytes 393248 | tf_op jit(solution)/shard_map/all_to_all | solution.py:62
  64.2 3.4 %scatter_custom_fusion.3 = f32[95,640]{0,1:T(8,128)S(1)} fusion(s32[1024]{0:T(1024)S(1)} %bitcast.133, f32[1024,95]{1,0:T(8,128)S(1)} %copy.127, f32[]{:T(128)} %constant.126.clone.1), kind=kCustom, calls=%fused_computation.141 | custom fusion | bytes 243204 | tf_op jit(solution)/shard_map/scatter | solution.py:140
  68.1 1.0 multiply_subtract_fusion.20
  69.1 2.2 %fusion.73 = (f32[640]{0:T(1024)S(1)}, f32[640]{0:T(1024)S(1)}, f32[640]{0:T(1024)S(1)}, f32[640]{0:T(1024)S(1)}, f32[640]{0:T(1024)S(1)}, /*index=5*/f32[640]{0...) fusion(f32[1,640]{0,1:T(8,128)S(1)} %get-tuple-element.194, ...), kind=kLoop, calls=%fused_computation.342 | loop fusion | flops 6400 | bytes 79360 | tf_op jit(solution)/shard_map/div | solution.py:51
  71.3 0.6 multiply_subtract_fusion.14
  71.9 2.2 %fusion.79 = (f32[640]{0:T(1024)S(1)}, f32[640]{0:T(1024)S(1)}, f32[640]{0:T(1024)S(1)}, f32[640]{0:T(1024)S(1)}, f32[640]{0:T(1024)S(1)}, /*index=5*/f32[640]{0...) fusion(f32[1,640]{0,1:T(8,128)S(1)} %get-tuple-element.189, ...), kind=kLoop, calls=%fused_computation.348 | loop fusion | flops 6400 | bytes 79360 | tf_op jit(solution)/shard_map/div | solution.py:51
  74.1 0.6 multiply_subtract_fusion.8
  74.7 2.2 %fusion.85 = (f32[640]{0:T(1024)S(1)}, f32[640]{0:T(1024)S(1)}, f32[640]{0:T(1024)S(1)}, f32[640]{0:T(1024)S(1)}, f32[640]{0:T(1024)S(1)}, /*index=5*/f32[640]{0...) fusion(f32[1,640]{0,1:T(8,128)S(1)} %get-tuple-element.184, ...), kind=kLoop, calls=%fused_computation.354 | loop fusion | flops 6400 | bytes 79360 | tf_op jit(solution)/shard_map/div | solution.py:51
  77.0 0.6 multiply_subtract_fusion.2
  77.6 2.2 %fusion.91 = (f32[640]{0:T(1024)S(1)}, f32[640]{0:T(1024)S(1)}, f32[640]{0:T(1024)S(1)}, f32[640]{0:T(1024)S(1)}, f32[640]{0:T(1024)S(1)}, /*index=5*/f32[640]{0...) fusion(f32[1,640]{0,1:T(8,128)S(1)} %get-tuple-element.179, ...), kind=kLoop, calls=%fused_computation.360 | loop fusion | flops 6400 | bytes 79360 | tf_op jit(solution)/shard_map/div | solution.py:51
  79.8 2.9 %fusion.97 = (f32[640]{0:T(1024)S(1)}, f32[640]{0:T(1024)S(1)}, f32[640]{0:T(1024)S(1)}, f32[640]{0:T(1024)S(1)}, f32[640]{0:T(1024)S(1)}, /*index=5*/f32[640]{0...) fusion(f32[31,640]{0,1:T(8,128)S(1)} %add_select_fusion, ...), kind=kLoop, calls=%fused_computation.366 | loop fusion | flops 10240 | bytes 94720 | tf_op jit(solution)/shard_map/div | solution.py:51
  84.0 2.8 %gather_fusion.1 = f32[1024,64]{1,0:T(8,128)S(1)} fusion(f32[64,640]{0,1:T(8,128)S(1)} %broadcast_select_fusion, s32[1024]{0:T(1024)S(1)} %broadcast_clamp_fusion), kind=kCustom, calls=%fused_computation.1 | custom fusion | bytes 528384 | tf_op jit(solution)/shard_map/gather | solution.py:146
  86.8 0.9 copy.165
  87.6 3.4 %all-to-all-start.1 = ((f32[64,8,128]{2,0,1:T(8,128)}), f32[64,8,128]{2,0,1:T(8,128)S(1)}, u32[]{:S(2)}, u32[]{:S(2)}) async-start(f32[64,8,128]{2,0,1:T(8,128)} %copy.165), calls=%async_computation.1 | async-start | bytes 524288 | tf_op jit(solution)/shard_map/all_to_all | solution.py:62
  91.1 0.8 copy.168
  91.9 7.4 %all-to-all-done.1 = f32[64,8,128]{2,0,1:T(8,128)S(1)} async-done(((f32[64,8,128]{2,0,1:T(8,128)}), f32[64,8,128]{2,0,1:T(8,128)S(1)}, u32[]{:S(2)}, u32[]{:S(2)}) %all-to-all-start.1) | async-done | bytes 262176 | tf_op jit(solution)/shard_map/all_to_all | solution.py:62
  99.4 1.0 %gather_fusion.2 = f32[512,64]{1,0:T(8,128)S(1)} fusion(f32[64,1024]{0,1:T(8,128)S(1)} %bitcast.110, s32[1024]{0:T(1024)S(1)} %pad_clamp_fusion), kind=kCustom, calls=%fused_computation.2 | custom fusion | bytes 264192 | tf_op jit(solution)/shard_map/gather | solution.py:147
  100.6 0.7 reshape_reshape.3
  (107 shorter events, 6.1 us)
Async XLA Ops:
  0.6 0.9 copy-start.1
  1.6 0.9 copy-start.2
  2.5 19.2 %collective-permute-start.1 = (f32[5,32,1,128]{3,1,2,0:T(8,128)S(1)}, f32[5,32,1,128]{3,1,2,0:T(8,128)S(1)}, u32[]{:S(2)}, u32[]{:S(2)}) collective-permute-start(f32[5,32,1,128]{3,1,2,0:T(8,128)S(1)} %get-tuple-element.226), channel_id=1, source_target_pairs={{4,0},{8,4},{12,8},{0,12},{5,1},{9,5},{13,9},{1,13},{6,2},{10,6},{... | collective-permute-start | bytes 245768 | tf_op jit(solution)/shard_map/ppermute | solution.py:16
  7.6 14.1 %collective-permute-start = (f32[5,32,1,128]{3,1,2,0:T(8,128)S(1)}, f32[5,32,1,128]{3,1,2,0:T(8,128)S(1)}, u32[]{:S(2)}, u32[]{:S(2)}) collective-permute-start(f32[5,32,1,128]{3,1,2,0:T(8,128)S(1)} %get-tuple-element.225), channel_id=1, source_target_pairs={{0,4},{4,8},{8,12},{12,0},{1,5},{5,9},{9,13},{13,1},{2,6},{6,10},{... | collective-permute-start | bytes 245768 | tf_op jit(solution)/shard_map/ppermute | solution.py:13
  7.6 0.7 copy-start
  22.3 4.9 %collective-permute-start.3 = (f32[5,32,6,1]{1,2,3,0:T(8,128)S(1)}, f32[5,32,6,1]{1,2,3,0:T(8,128)S(1)}, u32[]{:S(2)}, u32[]{:S(2)}) collective-permute-start(f32[5,32,6,1]{1,2,3,0:T(8,128)S(1)} %copy.170), channel_id=1, source_target_pairs={{2,0},{0,2},{3,1},{1,3},{6,4},{4,6},{7,5},{5,7},{10,8},{8,10},{11,... | collective-permute-start | bytes 11528 | tf_op jit(solution)/shard_map/ppermute | solution.py:16
  24.1 3.8 %collective-permute-start.2 = (f32[5,32,6,1]{1,2,3,0:T(8,128)S(1)}, f32[5,32,6,1]{1,2,3,0:T(8,128)S(1)}, u32[]{:S(2)}, u32[]{:S(2)}) collective-permute-start(f32[5,32,6,1]{1,2,3,0:T(8,128)S(1)} %copy.169), channel_id=1, source_target_pairs={{0,2},{2,0},{1,3},{3,1},{4,6},{6,4},{5,7},{7,5},{8,10},{10,8},{9,1... | collective-permute-start | bytes 11528 | tf_op jit(solution)/shard_map/ppermute | solution.py:13
  29.3 5.5 %collective-permute-start.5 = (f32[2,32,1,128]{3,1,2,0:T(8,128)S(1)}, f32[2,32,1,128]{3,1,2,0:T(8,128)S(1)}, u32[]{:S(2)}, u32[]{:S(2)}) collective-permute-start(f32[2,32,1,128]{3,1,2,0:T(8,128)S(1)} %get-tuple-element.266), channel_id=1, source_target_pairs={{4,0},{8,4},{12,8},{0,12},{5,1},{9,5},{13,9},{1,13},{6,2},{10,6},{... | collective-permute-start | bytes 98312 | tf_op jit(solution)/shard_map/ppermute | solution.py:16
  33.2 5.7 %collective-permute-start.4 = (f32[2,32,1,128]{3,1,2,0:T(8,128)S(1)}, f32[2,32,1,128]{3,1,2,0:T(8,128)S(1)}, u32[]{:S(2)}, u32[]{:S(2)}) collective-permute-start(f32[2,32,1,128]{3,1,2,0:T(8,128)S(1)} %get-tuple-element.265), channel_id=1, source_target_pairs={{0,4},{4,8},{8,12},{12,0},{1,5},{5,9},{9,13},{13,1},{2,6},{6,10},{... | collective-permute-start | bytes 98312 | tf_op jit(solution)/shard_map/ppermute | solution.py:13
  39.1 2.1 %copy-start.5 = (s32[4,128]{1,0:T(4,128)S(1)}, s32[4,128]{1,0:T(4,128)}, u32[]{:S(2)}) copy-start(s32[4,128]{1,0:T(4,128)} %param.13) | copy-start | bytes 6148
  39.1 5.8 %collective-permute-start.7 = (f32[2,32,6,1]{3,1,2,0:T(8,128)S(1)}, f32[2,32,6,1]{3,1,2,0:T(8,128)S(1)}, u32[]{:S(2)}, u32[]{:S(2)}) collective-permute-start(f32[2,32,6,1]{3,1,2,0:T(8,128)S(1)} %get-tuple-element.228), channel_id=1, source_target_pairs={{2,0},{0,2},{3,1},{1,3},{6,4},{4,6},{7,5},{5,7},{10,8},{8,10},{11,... | collective-permute-start | bytes 4616 | tf_op jit(solution)/shard_map/ppermute | solution.py:16
  40.1 6.8 %collective-permute-start.6 = (f32[2,32,6,1]{3,1,2,0:T(8,128)S(1)}, f32[2,32,6,1]{3,1,2,0:T(8,128)S(1)}, u32[]{:S(2)}, u32[]{:S(2)}) collective-permute-start(f32[2,32,6,1]{3,1,2,0:T(8,128)S(1)} %get-tuple-element.227), channel_id=1, source_target_pairs={{0,2},{2,0},{1,3},{3,1},{4,6},{6,4},{5,7},{7,5},{8,10},{10,8},{9,1... | collective-permute-start | bytes 4616 | tf_op jit(solution)/shard_map/ppermute | solution.py:13
  50.9 3.6 %copy-start.3 = (f32[31,640]{1,0:T(8,128)S(1)}, f32[31,640]{1,0:T(8,128)}, u32[]{:S(2)}) copy-start(f32[31,640]{1,0:T(8,128)} %param.15) | copy-start | bytes 238084
  50.9 12.7 %all-to-all-start = ((f32[96,8,128]{2,0,1:T(8,128)}), f32[96,8,128]{2,0,1:T(8,128)S(1)}, u32[]{:S(2)}, u32[]{:S(2)}) async-start(f32[96,8,128]{2,0,1:T(8,128)} %copy.124), calls=%async_computation | async-start | bytes 786432 | tf_op jit(solution)/shard_map/all_to_all | solution.py:62
  54.5 0.7 copy-start.4
  87.6 11.6 %all-to-all-start.1 = ((f32[64,8,128]{2,0,1:T(8,128)}), f32[64,8,128]{2,0,1:T(8,128)S(1)}, u32[]{:S(2)}, u32[]{:S(2)}) async-start(f32[64,8,128]{2,0,1:T(8,128)} %copy.165), calls=%async_computation.1 | async-start | bytes 524288 | tf_op jit(solution)/shard_map/all_to_all | solution.py:62
where the time goes:
time: 102 us; the launch traced here: 101 us
  other arithmetic  30 us (29%)
  local copies, waits for them, and re-layouts  28.7 us (28%)
  waiting for transfers between devices  21.2 us (21%)
  starting transfers between devices  20.2 us (20%)
  between operations  1.28 us (1%)
    all_to_all x2, waiting for transfers between devices, regroup(): lax.all_to_all(send_block, ('lat', 'lon'), split_axis=1, concat_axis=1, t...  11.9 us
    div x5, other arithmetic, implicit_diffusion(): ratios.append(upper_kv / pivot_sum)  11.8 us
    ppermute x4, starting transfers between devices, with_halo(): lax.ppermute(lax.slice_in_dim(block, 0, width, axis=dim), axis, backward)  11.5 us
    all_to_all x2, starting transfers between devices, regroup(): lax.all_to_all(send_block, ('lat', 'lon'), split_axis=1, concat_axis=1, t...  6.99 us
    ppermute x4, waiting for transfers between devices, with_halo(): lax.ppermute(lax.slice_in_dim(block, block.shape[dim] - width, None, axis...  6.76 us
    unnamed x39, local copies, waits for them, and re-layouts  4.81 us
    gather x2, other arithmetic, on_device(): owner_start[sorted_owner]  4.42 us
    sort x1, other arithmetic, on_device(): sorted_order = jnp.argsort(owner_flat, stable=True)  3.77 us
  transfers between devices with their start and end apart: 10, of which 7 were waited for; matrix products, arithmetic and copies ran while one was open for 24% of the time, Pallas kernels for 0%

commit v1 on v0

v1 whole, which is shorter than its diff:
```python
import functools

import jax
import jax.numpy as jnp
from jax import lax
from jax.experimental import pallas as pl
from jax.experimental.pallas import tpu as pltpu
from jax.sharding import PartitionSpec as P

LANES = 128
EDGE = 16
VMEM_LIMIT = 48 * 1024 * 1024
NT = (((1,), (1,)), ((), ()))


def lane_iota(shape):
    return lax.broadcasted_iota(jnp.int32, shape, len(shape) - 1)


def split3(values):
    top = values.astype(jnp.bfloat16)
    rest = values - top.astype(jnp.float32)
    mid = rest.astype(jnp.bfloat16)
    low = (rest - mid.astype(jnp.float32)).astype(jnp.bfloat16)
    return jnp.concatenate([top, mid, low], axis=0)


def pick_columns(values, hot):
    rows = values.shape[0]
    out = lax.dot_general(split3(values), hot, NT, preferred_element_type=jnp.float32)
    return out[:rows] + out[rows : 2 * rows] + out[2 * rows :]


def hot_matrix(row_of, size, base=0):
    cols = row_of.shape[-1]
    index = lax.broadcasted_iota(jnp.int32, (size, cols), 0) + base
    return jnp.where(index == row_of, 1.0, 0.0).astype(jnp.bfloat16)


def loop_over(count, body):
    if count <= 8:
        for index in range(count):
            body(index)
    else:
        pl.loop(0, count)(body)


def half_levels(first, second):
    return jnp.where(lax.axis_index("lev") == 0, first, second)


def pack_kernel(
    levels, rows, devices, tr_ref, wind_ref, mass_ref, owner_ref, slot_ref, diff_ref,
    send_ref, north_ref, south_ref, shear_ref, rank_ref,
):
    faces = levels - 1
    half = levels // 2
    spans = diff_ref.shape[1] // LANES

    def tracer_row(j):
        return tr_ref[pl.ds(j, 2 * levels, stride=rows), :]

    def east_row(j):
        return wind_ref[pl.ds(j, levels, stride=rows), :]

    def north_row(j):
        return wind_ref[pl.ds(levels * rows + j, levels, stride=rows), :]

    def mass_row(j):
        return mass_ref[pl.ds(j, levels, stride=rows), :]

    two, lev = 2 * levels, levels
    last = rows - 1
    north_ref[0:two] = tracer_row(last - 1)
    north_ref[two : 2 * two] = tracer_row(last)
    north_ref[2 * two : 2 * two + lev] = east_row(last)
    north_ref[2 * two + lev : 2 * two + 2 * lev] = north_row(last - 1)
    north_ref[2 * two + 2 * lev : 2 * two + 3 * lev] = north_row(last)
    north_ref[2 * two + 3 * lev : 2 * two + 4 * lev] = mass_row(last)
    south_ref[0:two] = tracer_row(0)
    south_ref[two : 2 * two] = tracer_row(1)
    south_ref[2 * two : 2 * two + lev] = east_row(0)
    south_ref[2 * two + lev : 2 * two + 2 * lev] = north_row(0)
    south_ref[2 * two + 2 * lev : 2 * two + 3 * lev] = mass_row(0)

    shears = []
    for j in range(rows):
        east, north = east_row(j), north_row(j)
        east_step = east[1:] - east[:-1]
        north_step = north[1:] - north[:-1]
        shear = east_step * east_step + north_step * north_step
        shears.append(half_levels(shear[:half], shear[faces - half :]))
    shear = jnp.concatenate(shears, axis=1)
    shear_ref[...] = shear

    owner_index = lax.broadcasted_iota(jnp.int32, (devices, LANES), 0)
    owned = [owner_index == owner_ref[j : j + 1, :] for j in range(rows)]
    upto = lax.broadcasted_iota(jnp.int32, (LANES, LANES), 0) <= lane_iota((LANES, LANES))
    counted = lax.dot_general(
        jnp.concatenate([jnp.where(hit, 1.0, 0.0) for hit in owned], axis=0).astype(jnp.bfloat16),
        jnp.where(upto, 1.0, 0.0).astype(jnp.bfloat16),
        (((1,), (0,)), ((), ())),
        preferred_element_type=jnp.float32,
    )
    before = jnp.full((devices, 1), -1.0, jnp.float32)
    for j in range(rows):
        count = counted[j * devices : (j + 1) * devices]
        rank_ref[:, j * LANES : (j + 1) * LANES] = jnp.where(owned[j], count + before, -1.0).astype(
            jnp.int32
        )
        before = before + count[:, LANES - 1 :]

    lane_row = lane_iota((1, LANES))
    masses = jnp.transpose(jnp.concatenate([mass_row(j) for j in range(rows)], axis=0))
    edge_rows = [[], [], [], []]
    for j in range(rows):
        turned = jnp.transpose(jnp.concatenate([tracer_row(j), east_row(j), north_row(j)], axis=0))
        west_mass = pltpu.roll(masses[0:1], (2 * levels - j * levels) % LANES, 1)
        east_mass = pltpu.roll(masses[LANES - 1 :], (3 * levels - j * levels) % LANES, 1)
        edge_rows[0].append(
            jnp.where(lane_row >= 3 * levels, east_mass, turned[LANES - 2 : LANES - 1])
        )
        edge_rows[1].append(turned[LANES - 1 :])
        edge_rows[2].append(turned[0:1])
        edge_rows[3].append(jnp.where(lane_row >= 2 * levels, west_mass, turned[1:2]))
    edges = jnp.concatenate([row for group in edge_rows for row in group], axis=0)

    diffs = half_levels(diff_ref[0:half], diff_ref[faces - half :])
    slots = jnp.concatenate([slot_ref[j : j + 1, :] for j in range(rows)], axis=1)
    extra = jnp.concatenate(
        [slots.astype(jnp.float32) + 1.0, jnp.zeros((7, rows * LANES), jnp.float32)], axis=0
    )
    payload = jnp.concatenate([shear, extra], axis=0)

    def fill(dest):
        hot = hot_matrix(rank_ref[pl.ds(dest, 1), :], LANES)
        grouped = pick_columns(payload, hot)
        slot_row = grouped[half : half + 1] - 1.0
        tail = jnp.concatenate(
            [pltpu.roll(slot_row, (3 * levels - j * levels) % LANES, 1) for j in range(rows)], axis=0
        )
        send_ref[dest, 0 : EDGE - rows] = edges[: EDGE - rows]
        send_ref[dest, EDGE - rows : EDGE] = jnp.where(
            lane_row >= 3 * levels, tail, edges[EDGE - rows :]
        )
        send_ref[dest, EDGE : EDGE + half] = grouped[:half]
        for span in range(spans):
            send_ref[dest, EDGE + half * (span + 1) : EDGE + half * (span + 2)] = diffs[
                :, span * LANES : (span + 1) * LANES
            ]

    loop_over(devices, fill)


def source_term(shear):
    return 2.0 * shear / (0.05 + shear)


def select_kernel(
    levels, rows, devices, recv_ref, owner_ref, slot_ref, diff_ref, count_ref, shear_ref,
    mine_ref, place_ref, arrived_ref,
):
    faces = levels - 1
    half = levels // 2
    slot_total = diff_ref.shape[1]
    spans = slot_total // LANES
    cols = rows * LANES
    lane_row = lane_iota((1, LANES))

    for j in range(rows):
        mine_ref[:, j * LANES : (j + 1) * LANES] = jnp.zeros((half, LANES), jnp.float32)
    span_of = []
    position = []
    for j in range(rows):
        slot = slot_ref[j : j + 1, :]
        span = slot // LANES
        span_of.append(owner_ref[j : j + 1, :] * spans + span)
        position.append(jnp.broadcast_to(slot - span * LANES, (half, LANES)))

    def gather(source):
        for j in range(rows):
            found = mine_ref[:, j * LANES : (j + 1) * LANES]
            for span in range(spans):
                held = recv_ref[source, EDGE + half * (span + 1) : EDGE + half * (span + 2), :]
                taken = jnp.take_along_axis(held, position[j], axis=1)
                found = jnp.where(span_of[j] == source * spans + span, taken, found)
            mine_ref[:, j * LANES : (j + 1) * LANES] = found

    loop_over(devices, gather)
    mine_ref[:, 0:cols] = 0.5 * mine_ref[:, 0:cols] + source_term(shear_ref[...])

    def unpack(source):
        tail = recv_ref[source, EDGE - rows : EDGE, :]
        slot_row = jnp.zeros((1, LANES), jnp.float32)
        for j in range(rows):
            back = pltpu.roll(tail[j : j + 1], (levels + j * levels) % LANES, 1)
            slot_row = jnp.where(lane_row // levels == j, back, slot_row)
        place_ref[source] = slot_row.astype(jnp.int32)

    loop_over(devices, unpack)
    if devices <= 8:
        slot_row = jnp.concatenate([place_ref[source] for source in range(devices)], axis=1)
        arrived = jnp.concatenate(
            [recv_ref[source, EDGE : EDGE + half, :] for source in range(devices)], axis=1
        )
        arrived_ref[...] = pick_columns(arrived, hot_matrix(slot_row, slot_total))
    else:
        arrived_ref[...] = jnp.zeros((half, slot_total), jnp.float32)

        def place(source):
            arrived_ref[...] += pick_columns(
                recv_ref[source, EDGE : EDGE + half, :], hot_matrix(place_ref[source], slot_total)
            )

        loop_over(devices, place)
    for span in range(spans):
        here = slice(span * LANES, (span + 1) * LANES)
        old = half_levels(diff_ref[0:half, here], diff_ref[faces - half :, here])
        new = 0.5 * old + source_term(arrived_ref[:, here])
        active = lane_row < count_ref[span]
        mine_ref[:, cols + span * LANES : cols + (span + 1) * LANES] = jnp.where(active, new, old)


def advect_kernel(
    levels, rows, lat_count, lon_count, tr_ref, wind_ref, mass_ref, low_ref, high_ref, edge_ref,
    out_ref,
):
    lev, two = levels, 2 * levels
    lat, lon = lax.axis_index("lat"), lax.axis_index("lon")
    first, final = lat == 0, lat == lat_count - 1
    lane_row = lane_iota((1, LANES))

    def block(lat_index, lon_index):
        return lat_index * lon_count + lon_index

    west_lon = lax.rem(lon + lon_count - 1, lon_count)
    east_lon = lax.rem(lon + 1, lon_count)
    south_lat = jnp.maximum(lat - 1, 0)
    north_lat = jnp.minimum(lat + 1, lat_count - 1)

    def edge(lat_index, lon_index, group):
        return edge_ref[block(lat_index, lon_index), group * rows : (group + 1) * rows, :]

    def east_of(row):
        return jnp.where(lane_row < lev, pltpu.roll(row, 2 * lev, 1), pltpu.roll(row, 3 * lev, 1))

    def north_of(row):
        return jnp.where(lane_row < lev, pltpu.roll(row, lev, 1), pltpu.roll(row, 2 * lev, 1))

    def upwind(wind, here, ahead):
        return jnp.maximum(wind, 0.0) * here + jnp.minimum(wind, 0.0) * ahead

    def beside(column, west_east, west_value, here_east, east_value, mass):
        fluxes = upwind(north_of(column[: rows + 1]), column[: rows + 1], column[1:])
        index = lax.broadcasted_iota(jnp.int32, (rows + 1, LANES), 0)
        closed = ((index == 0) & first) | ((index == rows) & final)
        fluxes = jnp.where(closed, 0.0, fluxes)
        here = column[1 : rows + 1]
        zonal = upwind(here_east, here, east_value) - upwind(west_east, west_value, here)
        return here - mass * (zonal + fluxes[1:] - fluxes[:-1])

    far_west = edge(lat, west_lon, 0)
    west = jnp.concatenate(
        [
            edge(south_lat, west_lon, 1)[rows - 1 :],
            edge(lat, west_lon, 1),
            edge(north_lat, west_lon, 1)[0:1],
        ],
        axis=0,
    )
    east = jnp.concatenate(
        [
            edge(south_lat, east_lon, 2)[rows - 1 :],
            edge(lat, east_lon, 2),
            edge(north_lat, east_lon, 2)[0:1],
        ],
        axis=0,
    )
    far_east = edge(lat, east_lon, 3)
    own_first, own_last = edge(lat, lon, 2), edge(lat, lon, 1)
    west_mid, east_mid = west[1 : rows + 1], east[1 : rows + 1]
    west_new = beside(
        west, east_of(far_west), far_west, east_of(west_mid), own_first, north_of(far_west)
    )
    east_new = beside(
        east, east_of(own_last), own_last, east_of(east_mid), far_east, east_of(far_east)
    )
    filler = jnp.zeros((LANES - 2 * (rows + 2) - 2 * rows, LANES), jnp.float32)
    turned = jnp.transpose(jnp.concatenate([west, east, west_new, east_new, filler], axis=0))

    def column(index, start, size):
        return jnp.broadcast_to(turned[start : start + size, index : index + 1], (size, LANES))

    def place(value, lane, index, start, size):
        return jnp.where(lane_row == lane, column(index, start, size), value)

    tracer = {-2: low_ref[0:two], -1: low_ref[two : 2 * two]}
    east_wind = {-1: low_ref[2 * two : 2 * two + lev]}
    north_wind = {
        -2: low_ref[2 * two + lev : 2 * two + 2 * lev],
        -1: low_ref[2 * two + 2 * lev : 2 * two + 3 * lev],
    }
    mass = {-1: low_ref[2 * two + 3 * lev : 2 * two + 4 * lev]}
    for j in range(rows):
        tracer[j] = tr_ref[pl.ds(j, two, stride=rows), :]
        east_wind[j] = wind_ref[pl.ds(j, lev, stride=rows), :]
        north_wind[j] = wind_ref[pl.ds(levels * rows + j, lev, stride=rows), :]
        mass[j] = mass_ref[pl.ds(j, lev, stride=rows), :]
    tracer[rows] = high_ref[0:two]
    tracer[rows + 1] = high_ref[two : 2 * two]
    east_wind[rows] = high_ref[2 * two : 2 * two + lev]
    north_wind[rows] = high_ref[2 * two + lev : 2 * two + 2 * lev]
    mass[rows] = high_ref[2 * two + 2 * lev : 2 * two + 3 * lev]

    west_wind = {
        j: place(pltpu.roll(east_wind[j], 1, 1), 0, j + 1, two, lev) for j in range(-1, rows + 1)
    }

    def substep(field, row_range, west_index, east_index, start):
        fluxes = {}
        for j in range(row_range[0] - 1, row_range[-1] + 1):
            flux = upwind(north_wind[j], field[j], field[j + 1])
            if j == -1:
                flux = jnp.where(first, 0.0, flux)
            if j == rows - 1:
                flux = jnp.where(final, 0.0, flux)
            fluxes[j] = flux
        result = {}
        for j in row_range:
            here = field[j]
            ahead = place(pltpu.roll(here, LANES - 1, 1), LANES - 1, east_index(j), start, lev)
            behind = place(pltpu.roll(here, 1, 1), 0, west_index(j), start, lev)
            zonal = upwind(east_wind[j], here, ahead) - upwind(west_wind[j], behind, here)
            result[j] = here - mass[j] * (zonal + fluxes[j] - fluxes[j - 1])
        return result

    for t in range(2):
        start = t * lev
        field = {j: value[start : start + lev] for j, value in tracer.items()}
        once = substep(
            field, range(-1, rows + 1), lambda j: j + 1, lambda j: rows + 2 + j + 1, start
        )
        base = 2 * (rows + 2)
        twice = substep(once, range(rows), lambda j: base + j, lambda j: base + rows + j, start)
        for j in range(rows):
            out_ref[pl.ds(t * rows + j, lev, stride=2 * rows), :] = twice[j]


def solve_kernel(levels, rows, adv_ref, mine_ref, other_ref, out_ref, diff_ref, kv_ref):
    faces = levels - 1
    half = levels // 2
    slot_total = diff_ref.shape[1]
    cols = rows * LANES
    width = 2 * rows
    low = half_levels(mine_ref[...], other_ref[...])
    high = half_levels(other_ref[...], mine_ref[...])
    diff_ref[0:half] = low[:, cols:]
    diff_ref[half:] = high[1:, cols:]
    for j in range(rows):
        here = slice(j * LANES, (j + 1) * LANES)
        for t in range(2):
            kv_ref[pl.ds(t * rows + j, half, stride=width), :] = low[:, here]
            kv_ref[pl.ds((faces - half) * width + t * rows + j, half, stride=width), :] = high[:, here]

    ratios, sweeps = [], []
    lower = None
    for level in range(levels):
        rhs = adv_ref[level * width : (level + 1) * width]
        pivot = 1.0
        upper = None
        if level < levels - 1:
            upper = kv_ref[level * width : (level + 1) * width]
            pivot = pivot + upper
        if level > 0:
            pivot = pivot + lower - lower * ratios[-1]
            rhs = rhs + lower * sweeps[-1]
        inverse = 1.0 / pivot
        if upper is not None:
            ratios.append(upper * inverse)
        sweeps.append(rhs * inverse)
        lower = upper
    value = sweeps[-1]
    for level in range(levels - 1, -1, -1):
        if level < levels - 1:
            value = sweeps[level] + ratios[level] * value
        for t in range(2):
            out_ref[(t * levels + level) * rows : (t * levels + level + 1) * rows] = value[
                t * rows : (t + 1) * rows
            ]


def call(kernel, outs, in_specs, scratch=()):
    vmem = pl.BlockSpec(memory_space=pltpu.VMEM)
    return pl.pallas_call(
        kernel,
        out_shape=[jax.ShapeDtypeStruct(shape, jnp.float32) for shape in outs],
        in_specs=in_specs,
        out_specs=[vmem] * len(outs),
        scratch_shapes=list(scratch),
        compiler_params=pltpu.CompilerParams(vmem_limit_bytes=VMEM_LIMIT),
    )


def on_device(
    tracers, face_winds, inverse_mass, span_owner, span_slot, span_column_count, diffusivity
):
    own_count, levels, rows, cols = tracers.shape
    lat_count, lon_count = lax.axis_size("lat"), lax.axis_size("lon")
    devices = lat_count * lon_count
    half = levels // 2
    slot_total = diffusivity.shape[1]
    spans = span_column_count.shape[0]
    block_rows = EDGE + half * (1 + spans)
    vmem = pl.BlockSpec(memory_space=pltpu.VMEM)
    smem = pl.BlockSpec(memory_space=pltpu.SMEM)

    tr = tracers.reshape(own_count * levels * rows, cols)
    winds = face_winds.reshape(2 * levels * rows, cols)
    mass = inverse_mass.reshape(levels * rows, cols)

    send, north, south, shear = call(
        functools.partial(pack_kernel, levels, rows, devices),
        [
            (devices, block_rows, LANES),
            (8 * levels, LANES),
            (7 * levels, LANES),
            (half, rows * LANES),
        ],
        [vmem] * 6,
        [pltpu.VMEM((devices, rows * LANES), jnp.int32)],
    )(tr, winds, mass, span_owner, span_slot, diffusivity)
    recv = lax.all_to_all(send, ("lat", "lon"), split_axis=0, concat_axis=0, tiled=True)
    up = [(i, (i + 1) % lat_count) for i in range(lat_count)]
    down = [(target, source) for source, target in up]
    low = lax.ppermute(north, "lat", up)
    high = lax.ppermute(south, "lat", down)
    (mine,) = call(
        functools.partial(select_kernel, levels, rows, devices),
        [(half, rows * LANES + slot_total)],
        [vmem, vmem, vmem, vmem, smem, vmem],
        [
            pltpu.VMEM((devices, 1, LANES), jnp.int32),
            pltpu.VMEM((half, slot_total), jnp.float32),
        ],
    )(recv, span_owner, span_slot, diffusivity, span_column_count, shear)
    other = lax.ppermute(mine, "lev", [(0, 1), (1, 0)])
    (advected,) = call(
        functools.partial(advect_kernel, levels, rows, lat_count, lon_count),
        [(levels * own_count * rows, LANES)],
        [vmem] * 6,
    )(tr, winds, mass, low, high, recv)
    out, diff_out = call(
        functools.partial(solve_kernel, levels, rows),
        [(own_count * levels * rows, cols), (levels - 1, slot_total)],
        [vmem] * 3,
        [pltpu.VMEM((levels * 2 * rows, LANES), jnp.float32)],
    )(advected, mine, other)
    return out.reshape(own_count, levels, rows, cols), diff_out


def solution(mesh):
    placed = (
        P("lev", "ens", "lat", "lon"),
        P(None, "ens", "lat", "lon"),
        P("ens", "lat", "lon"),
        P("lat", "lon"),
        P("lat", "lon"),
        P(("lat", "lon")),
        P("ens", ("lat", "lon")),
    )
    return jax.shard_map(
        on_device,
        mesh=mesh,
        in_specs=placed,
        out_specs=(P("lev", "ens", "lat", "lon"), P("ens", ("lat", "lon"))),
        check_vma=False,
    )
```

time: 102 us -> 35 us (0.34)
  other arithmetic: 30 us -> 0 us
  local copies, waits for them, and re-layouts: 28.7 us -> 4.24 us
  starting transfers between devices: 20.2 us -> 11.3 us
  waiting for transfers between devices: 21.2 us -> 13.7 us
  Pallas kernels: 0 us -> 4.56 us
    div x6 -> x0, other arithmetic: 12.1 us -> none  [the longest x5 11.8 us: implicit_diffusion(): ratios.append(upper_kv / pivot_sum)]
    scatter x5 -> x0, local copies, waits for them, and re-layouts: 10.3 us -> none  [the longest x1 3.35 us: on_device(): in_spans = jnp.zeros((arrived.shape[0] - 1, slot_total), jnp.float32).at[...]
    ppermute x8 -> x3, starting transfers between devices: 13.2 us -> 3.95 us  [the longest x1 2.02 us: on_device(): low = lax.ppermute(north, 'lat', up)]
    gather x6 -> x0, local copies, waits for them, and re-layouts: 8.82 us -> none  [the longest x1 3.49 us: on_device(): sorted_owner = owner_flat[sorted_order]]
    ppermute x8 -> x3, waiting for transfers between devices: 9.3 us -> 0.51 us  [the longest x1 0.5 us: on_device(): other = lax.ppermute(mine, 'lev', [(0, 1), (1, 0)])]
    gather x6 -> x0, other arithmetic: 7.68 us -> none  [the longest x2 4.42 us: on_device(): owner_start[sorted_owner]]
    pallas_call x0 -> x4, Pallas kernels: none -> 4.56 us  [the longest x1 1.56 us: on_device(): call(functools.partial(pack_kernel, levels, rows, devices), [(devices, bl...]
    sort x1 -> x0, other arithmetic: 3.77 us -> none  [on_device(): sorted_order = jnp.argsort(owner_flat, stable=True)]
  transfers between devices with their start and end apart: 10 -> 4, of which waited for: 7 -> 2; matrix products, arithmetic and copies ran while one was open for 24% -> 0% of each run, Pallas kernels for 0% -> 6%
where the time goes in v1:
time: 35 us; the launch traced here: 34.6 us
  waiting for transfers between devices  13.7 us (39%)
  starting transfers between devices  11.3 us (32%)
  Pallas kernels  4.56 us (13%)
  local copies, waits for them, and re-layouts  4.24 us (12%)
  between operations  0.73 us (2%)
    all_to_all x1, waiting for transfers between devices, on_device(): lax.all_to_all(send, ('lat', 'lon'), split_axis=0, concat_axis=0, tiled=T...  13.2 us
    all_to_all x1, starting transfers between devices, on_device(): lax.all_to_all(send, ('lat', 'lon'), split_axis=0, concat_axis=0, tiled=T...  7.39 us
    unnamed x22, local copies, waits for them, and re-layouts  4.24 us
    ppermute x1, starting transfers between devices, on_device(): low = lax.ppermute(north, 'lat', up)  2.02 us
    ppermute x1, starting transfers between devices, on_device(): high = lax.ppermute(south, 'lat', down)  1.86 us
    pallas_call x1, Pallas kernels, on_device(): call(functools.partial(pack_kernel, levels, rows, devices), [(devices, bl...  1.56 us
    pallas_call x1, Pallas kernels, on_device(): call(functools.partial(select_kernel, levels, rows, devices), [(half, row...  1.29 us
    pallas_call x1, Pallas kernels, on_device(): call(functools.partial(solve_kernel, levels, rows), [(own_count * levels...  1.03 us
  transfers between devices with their start and end apart: 4, of which 2 were waited for; matrix products, arithmetic and copies ran while one was open for 0% of the time, Pallas kernels for 6%

profile of v1, /device:TPU:0, one launch (start us, length us, event | category | flops | bytes accessed | tf_op | source)
XLA Modules:
  0.0 34.6 jit_solution(15742774127840080706)
XLA Ops:
  0.6 0.0 copy-start.9
  0.6 0.0 copy-start.8
  0.6 0.7 %copy-done.9 = s32[4,128]{1,0:T(4,128)S(1)} copy-done((s32[4,128]{1,0:T(4,128)S(1)}, s32[4,128]{1,0:T(4,128)}, u32[]{:S(2)}) %copy-start.9) | copy-done | bytes 2072
  1.3 0.0 copy-done.8
  1.3 0.0 copy-start
  1.3 0.9 %copy-done = f32[2,32,4,128]{3,2,1,0:T(4,128)S(1)} copy-done((f32[2,32,4,128]{3,2,1,0:T(4,128)S(1)}, f32[2,32,4,128]{3,2,1,0:T(4,128)}, u32[]{:S(2)}) %copy-start) | copy-done | bytes 131096
  2.2 0.0 copy-start.2
  2.2 0.9 %copy-done.2 = f32[2,32,4,128]{3,2,1,0:T(4,128)S(1)} copy-done((f32[2,32,4,128]{3,2,1,0:T(4,128)S(1)}, f32[2,32,4,128]{3,2,1,0:T(4,128)}, u32[]{:S(2)}) %copy-start.2) | copy-done | bytes 131096
  3.1 0.0 copy-start.4
  3.1 0.9 %copy-done.4 = f32[31,640]{1,0:T(8,128)S(1)} copy-done((f32[31,640]{1,0:T(8,128)S(1)}, f32[31,640]{1,0:T(8,128)}, u32[]{:S(2)}) %copy-start.4) | copy-done | bytes 79384
  4.0 0.0 copy-start.6
  4.0 0.8 %copy-done.6 = f32[32,4,128]{2,1,0:T(4,128)S(1)} copy-done((f32[32,4,128]{2,1,0:T(4,128)S(1)}, f32[32,4,128]{2,1,0:T(4,128)}, u32[]{:S(2)}) %copy-start.6) | copy-done | bytes 65560
  4.9 1.6 %shard_map.86 = (f32[8,112,128]{2,1,0:T(8,128)}, f32[256,128]{1,0:T(8,128)S(1)}, f32[224,128]{1,0:T(8,128)S(1)}, f32[16,512]{1,0:T(8,128)S(1)}) custom-call(f32[256,128]{1,0:T(8,128)S(1)} %bitcast.4, f32[256,128]{1,0:T(8,128)S(1)} %bitcast.6, f32[128,128]{1,0:T(8,128)S(1)} %bitcast.8, s32[4,128]{1,0:T(4,128)S(1)} %copy-done.8, s32[4,128]{1,0:T(4,128)S(1)} %copy-done.9, ...), custom_call_target="tpu_custom_call" | custom-call | tf_op jit(solution)/shard_map/pallas_call | solution.py:421
  6.4 0.0 copy-start.5
  6.4 7.4 %all-to-all-start = ((f32[8,112,128]{2,1,0:T(8,128)}), f32[8,112,128]{2,1,0:T(8,128)S(1)}, u32[]{:S(2)}, u32[]{:S(2)}) async-start(f32[8,112,128]{2,1,0:T(8,128)} %get-tuple-element.10), calls=%async_computation | async-start | bytes 917504 | tf_op jit(solution)/shard_map/all_to_all | solution.py:432
  13.8 2.0 %collective-permute-start = (f32[256,128]{1,0:T(8,128)S(1)}, f32[256,128]{1,0:T(8,128)S(1)}, u32[]{:S(2)}, u32[]{:S(2)}) collective-permute-start(f32[256,128]{1,0:T(8,128)S(1)} %get-tuple-element.8), channel_id=1, source_target_pairs={{0,4},{4,8},{8,12},{12,0},{1,5},{5,9},{9,13},{13,1},{2,6},{6,10},{... | collective-permute-start | bytes 393224 | tf_op jit(solution)/shard_map/ppermute | solution.py:435
  15.8 0.0 copy-start.10
  15.8 1.9 %collective-permute-start.1 = (f32[224,128]{1,0:T(8,128)S(1)}, f32[224,128]{1,0:T(8,128)S(1)}, u32[]{:S(2)}, u32[]{:S(2)}) collective-permute-start(f32[224,128]{1,0:T(8,128)S(1)} %get-tuple-element.9), channel_id=1, source_target_pairs={{4,0},{8,4},{12,8},{0,12},{5,1},{9,5},{13,9},{1,13},{6,2},{10,6},{... | collective-permute-start | bytes 344072 | tf_op jit(solution)/shard_map/ppermute | solution.py:436
  17.7 13.2 %all-to-all-done.edge_ref.recv_ref = f32[8,112,128]{2,1,0:T(8,128)S(1)} async-done(((f32[8,112,128]{2,1,0:T(8,128)}), f32[8,112,128]{2,1,0:T(8,128)S(1)}, u32[]{:S(2)}, u32[]{:S(2)}) %all-to-all-start) | async-done | bytes 458784 | tf_op jit(solution)/shard_map/all_to_all | solution.py:432
  30.9 0.0 copy-done.5
  30.9 0.0 copy-done.10
  30.9 0.0 copy-start.1
  30.9 0.0 copy-start.3
  30.9 0.0 copy-start.7
  31.0 1.3 %shard_map.88.mine_ref = f32[16,1152]{1,0:T(8,128)S(1)} custom-call(f32[8,112,128]{2,1,0:T(8,128)S(1)} %all-to-all-done.edge_ref.recv_ref, s32[4,128]{1,0:T(4,128)S(1)} %copy-done.8, s32[4,128]{1,0:T(4,128)S(1)} %copy-done.9, f32[31,640]{1,0:T(8,128)S(1)} %copy-done.5, s32[5]{0:T(128)S(1)} %copy-done.10, f32[16,512]{1,0:T(8,128)S(1)} %get-tuple-element.11.shear_ref), custom_call_target="tpu_custom_call" | custom-call | tf_op jit(solution)/shard_map/pallas_call | solution.py:437
  32.3 0.1 collective-permute-start.2
  32.3 0.0 collective-permute-done.1.high_ref
  32.3 0.0 collective-permute-done.low_ref
  32.4 0.0 copy-done.1
  32.4 0.0 copy-done.3
  32.4 0.0 copy-done.7
  32.4 0.7 %shard_map.87.adv_ref = f32[256,128]{1,0:T(8,128)S(1)} custom-call(f32[256,128]{1,0:T(8,128)S(1)} %bitcast.5, f32[256,128]{1,0:T(8,128)S(1)} %bitcast.7, f32[128,128]{1,0:T(8,128)S(1)} %bitcast.9, f32[256,128]{1,0:T(8,128)S(1)} %collective-permute-done.low_ref, f32[224,128]{1,0:T(8,128)S(1)} %collective-permute-done.1.high_ref, ...), custom_call_target="tpu_custom_call" | custom-call | tf_op jit(solution)/shard_map/pallas_call | solution.py:447
  33.1 0.5 %collective-permute-done.2.other_ref = f32[16,1152]{1,0:T(8,128)S(1)} collective-permute-done((f32[16,1152]{1,0:T(8,128)S(1)}, f32[16,1152]{1,0:T(8,128)S(1)}, u32[]{:S(2)}, u32[]{:S(2)}) %collective-permute-start.2) | collective-permute-done | bytes 73760 | tf_op jit(solution)/shard_map/ppermute | solution.py:446
  33.6 1.0 %shard_map.89 = (f32[256,128]{1,0:T(8,128)}, f32[31,640]{1,0:T(8,128)}) custom-call(f32[256,128]{1,0:T(8,128)S(1)} %shard_map.87.adv_ref, f32[16,1152]{1,0:T(8,128)S(1)} %shard_map.88.mine_ref, f32[16,1152]{1,0:T(8,128)S(1)} %collective-permute-done.2.other_ref), custom_call_target="tpu_custom_call" | custom-call | tf_op jit(solution)/shard_map/pallas_call | solution.py:452
Async XLA Ops:
  0.6 0.7 %copy-start.9 = (s32[4,128]{1,0:T(4,128)S(1)}, s32[4,128]{1,0:T(4,128)}, u32[]{:S(2)}) copy-start(s32[4,128]{1,0:T(4,128)} %slot_ref.3) | copy-start | bytes 6148
  0.6 0.7 %copy-start.8 = (s32[4,128]{1,0:T(4,128)S(1)}, s32[4,128]{1,0:T(4,128)}, u32[]{:S(2)}) copy-start(s32[4,128]{1,0:T(4,128)} %owner_ref.3) | copy-start | bytes 6148
  1.3 0.9 %copy-start = (f32[2,32,4,128]{3,2,1,0:T(4,128)S(1)}, f32[2,32,4,128]{3,2,1,0:T(4,128)}, u32[]{:S(2)}) copy-start(f32[2,32,4,128]{3,2,1,0:T(4,128)} %param.7) | copy-start | bytes 393220
  2.2 0.9 %copy-start.2 = (f32[2,32,4,128]{3,2,1,0:T(4,128)S(1)}, f32[2,32,4,128]{3,2,1,0:T(4,128)}, u32[]{:S(2)}) copy-start(f32[2,32,4,128]{3,2,1,0:T(4,128)} %param.8) | copy-start | bytes 393220
  3.1 0.9 %copy-start.4 = (f32[31,640]{1,0:T(8,128)S(1)}, f32[31,640]{1,0:T(8,128)}, u32[]{:S(2)}) copy-start(f32[31,640]{1,0:T(8,128)} %diff_ref.3) | copy-start | bytes 238084
  4.0 0.8 %copy-start.6 = (f32[32,4,128]{2,1,0:T(4,128)S(1)}, f32[32,4,128]{2,1,0:T(4,128)}, u32[]{:S(2)}) copy-start(f32[32,4,128]{2,1,0:T(4,128)} %param.9) | copy-start | bytes 196612
  6.4 24.5 %copy-start.5 = (f32[31,640]{1,0:T(8,128)S(1)}, f32[31,640]{1,0:T(8,128)}, u32[]{:S(2)}) copy-start(f32[31,640]{1,0:T(8,128)} %diff_ref.3) | copy-start | bytes 238084
  6.4 24.5 %all-to-all-start = ((f32[8,112,128]{2,1,0:T(8,128)}), f32[8,112,128]{2,1,0:T(8,128)S(1)}, u32[]{:S(2)}, u32[]{:S(2)}) async-start(f32[8,112,128]{2,1,0:T(8,128)} %get-tuple-element.10), calls=%async_computation | async-start | bytes 917504 | tf_op jit(solution)/shard_map/all_to_all | solution.py:432
  13.8 18.5 %collective-permute-start = (f32[256,128]{1,0:T(8,128)S(1)}, f32[256,128]{1,0:T(8,128)S(1)}, u32[]{:S(2)}, u32[]{:S(2)}) collective-permute-start(f32[256,128]{1,0:T(8,128)S(1)} %get-tuple-element.8), channel_id=1, source_target_pairs={{0,4},{4,8},{8,12},{12,0},{1,5},{5,9},{9,13},{13,1},{2,6},{6,10},{... | collective-permute-start | bytes 393224 | tf_op jit(solution)/shard_map/ppermute | solution.py:435
  15.8 15.1 %copy-start.10 = (s32[5]{0:T(128)S(1)}, s32[5]{0:T(128)}, u32[]{:S(2)}) copy-start(s32[5]{0:T(128)} %count_ref.1) | copy-start | bytes 64
  15.8 16.5 %collective-permute-start.1 = (f32[224,128]{1,0:T(8,128)S(1)}, f32[224,128]{1,0:T(8,128)S(1)}, u32[]{:S(2)}, u32[]{:S(2)}) collective-permute-start(f32[224,128]{1,0:T(8,128)S(1)} %get-tuple-element.9), channel_id=1, source_target_pairs={{4,0},{8,4},{12,8},{0,12},{5,1},{9,5},{13,9},{1,13},{6,2},{10,6},{... | collective-permute-start | bytes 344072 | tf_op jit(solution)/shard_map/ppermute | solution.py:436
  30.9 1.4 %copy-start.1 = (f32[2,32,4,128]{3,2,1,0:T(4,128)S(1)}, f32[2,32,4,128]{3,2,1,0:T(4,128)}, u32[]{:S(2)}) copy-start(f32[2,32,4,128]{3,2,1,0:T(4,128)} %param.7) | copy-start | bytes 393220
  30.9 1.4 %copy-start.3 = (f32[2,32,4,128]{3,2,1,0:T(4,128)S(1)}, f32[2,32,4,128]{3,2,1,0:T(4,128)}, u32[]{:S(2)}) copy-start(f32[2,32,4,128]{3,2,1,0:T(4,128)} %param.8) | copy-start | bytes 393220
  30.9 1.4 %copy-start.7 = (f32[32,4,128]{2,1,0:T(4,128)S(1)}, f32[32,4,128]{2,1,0:T(4,128)}, u32[]{:S(2)}) copy-start(f32[32,4,128]{2,1,0:T(4,128)} %param.9) | copy-start | bytes 196612
  32.3 1.3 %collective-permute-start.2 = (f32[16,1152]{1,0:T(8,128)S(1)}, f32[16,1152]{1,0:T(8,128)S(1)}, u32[]{:S(2)}, u32[]{:S(2)}) collective-permute-start(f32[16,1152]{1,0:T(8,128)S(1)} %shard_map.88.mine_ref), channel_id=1, source_target_pairs={{0,1},{1,0},{2,3},{3,2},{4,5},{5,4},{6,7},{7,6},{8,9},{9,8},{10,11... | collective-permute-start | bytes 221192 | tf_op jit(solution)/shard_map/ppermute | solution.py:446

commit v2 on v1

--- a/solution.py
+++ b/solution.py
@@ -8,7 +8,7 @@
 from jax.sharding import PartitionSpec as P
 
 LANES = 128
-EDGE = 16
+MISC = 8
 VMEM_LIMIT = 48 * 1024 * 1024
 NT = (((1,), (1,)), ((), ()))
 
@@ -50,12 +50,23 @@
 
 
 def pack_kernel(
-    levels, rows, devices, tr_ref, wind_ref, mass_ref, owner_ref, slot_ref, diff_ref,
-    send_ref, north_ref, south_ref, shear_ref, rank_ref,
+    levels, rows, devices, tr_hbm, wind_hbm, mass_hbm, owner_hbm, slot_hbm, diff_hbm, count_hbm,
+    send_ref, north_ref, south_ref, shear_ref, edge_ref,
+    tr_ref, wind_ref, mass_ref, owner_ref, slot_ref, diff_ref, count_ref, rank_ref, sems,
 ):
     faces = levels - 1
     half = levels // 2
     spans = diff_ref.shape[1] // LANES
+    pairs = [
+        (owner_hbm, owner_ref), (slot_hbm, slot_ref), (wind_hbm, wind_ref), (count_hbm, count_ref),
+        (diff_hbm, diff_ref), (mass_hbm, mass_ref), (tr_hbm, tr_ref),
+    ]
+    copies = [
+        pltpu.make_async_copy(source, target, sems.at[index])
+        for index, (source, target) in enumerate(pairs)
+    ]
+    for copy in copies:
+        copy.start()
 
     def tracer_row(j):
         return tr_ref[pl.ds(j, 2 * levels, stride=rows), :]
@@ -69,6 +80,64 @@
     def mass_row(j):
         return mass_ref[pl.ds(j, levels, stride=rows), :]
 
+    copies[0].wait()
+    owner_index = lax.broadcasted_iota(jnp.int32, (devices, LANES), 0)
+    owned = [owner_index == owner_ref[j : j + 1, :] for j in range(rows)]
+    upto = lax.broadcasted_iota(jnp.int32, (LANES, LANES), 0) <= lane_iota((LANES, LANES))
+    counted = lax.dot_general(
+        jnp.concatenate([jnp.where(hit, 1.0, 0.0) for hit in owned], axis=0).astype(jnp.bfloat16),
+        jnp.where(upto, 1.0, 0.0).astype(jnp.bfloat16),
+        (((1,), (0,)), ((), ())),
+        preferred_element_type=jnp.float32,
+    )
+    before = jnp.full((devices, 1), -1.0, jnp.float32)
+    for j in range(rows):
+        count = counted[j * devices : (j + 1) * devices]
+        rank_ref[:, j * LANES : (j + 1) * LANES] = jnp.where(owned[j], count + before, -1.0).astype(
+            jnp.int32
+        )
+        before = before + count[:, LANES - 1 :]
+
+    copies[1].wait()
+    copies[2].wait()
+    shears = []
+    for j in range(rows):
+        east, north = east_row(j), north_row(j)
+        east_step = east[1:] - east[:-1]
+        north_step = north[1:] - north[:-1]
+        shear = east_step * east_step + north_step * north_step
+        shears.append(half_levels(shear[:half], shear[faces - half :]))
+    shear = jnp.concatenate(shears, axis=1)
+    shear_ref[...] = shear
+
+    copies[3].wait()
+    copies[4].wait()
+    diffs = half_levels(diff_ref[0:half], diff_ref[faces - half :])
+    lane_half = lane_iota((half, LANES))
+    lane_row = lane_iota((1, LANES))
+    starts, start = [], 0
+    for span in range(spans):
+        starts.append(start)
+        start = start + count_ref[span]
+    packed = []
+    for group in range(rows - 1):
+        value = jnp.zeros((half, LANES), jnp.float32)
+        for span in range(spans - 1):
+            spot = lane_half + (group * LANES - starts[span])
+            taken = jnp.take_along_axis(
+                diffs[:, span * LANES : (span + 1) * LANES], spot & (LANES - 1), axis=1
+            )
+            value = jnp.where((spot >= 0) & (spot < count_ref[span]), taken, value)
+        packed.append(value)
+    packed.append(diffs[:, (spans - 1) * LANES :])
+    start_row = jnp.zeros((1, LANES), jnp.float32)
+    for span in range(spans):
+        start_row = jnp.where(
+            lane_row == span, lax.convert_element_type(starts[span], jnp.float32), start_row
+        )
+
+    copies[5].wait()
+    copies[6].wait()
     two, lev = 2 * levels, levels
     last = rows - 1
     north_ref[0:two] = tracer_row(last - 1)
@@ -83,34 +152,6 @@
     south_ref[2 * two + lev : 2 * two + 2 * lev] = north_row(0)
     south_ref[2 * two + 2 * lev : 2 * two + 3 * lev] = mass_row(0)
 
-    shears = []
-    for j in range(rows):
-        east, north = east_row(j), north_row(j)
-        east_step = east[1:] - east[:-1]
-        north_step = north[1:] - north[:-1]
-        shear = east_step * east_step + north_step * north_step
-        shears.append(half_levels(shear[:half], shear[faces - half :]))
-    shear = jnp.concatenate(shears, axis=1)
-    shear_ref[...] = shear
-
-    owner_index = lax.broadcasted_iota(jnp.int32, (devices, LANES), 0)
-    owned = [owner_index == owner_ref[j : j + 1, :] for j in range(rows)]
-    upto = lax.broadcasted_iota(jnp.int32, (LANES, LANES), 0) <= lane_iota((LANES, LANES))
-    counted = lax.dot_general(
-        jnp.concatenate([jnp.where(hit, 1.0, 0.0) for hit in owned], axis=0).astype(jnp.bfloat16),
-        jnp.where(upto, 1.0, 0.0).astype(jnp.bfloat16),
-        (((1,), (0,)), ((), ())),
-        preferred_element_type=jnp.float32,
-    )
-    before = jnp.full((devices, 1), -1.0, jnp.float32)
-    for j in range(rows):
-        count = counted[j * devices : (j + 1) * devices]
-        rank_ref[:, j * LANES : (j + 1) * LANES] = jnp.where(owned[j], count + before, -1.0).astype(
-            jnp.int32
-        )
-        before = before + count[:, LANES - 1 :]
-
-    lane_row = lane_iota((1, LANES))
     masses = jnp.transpose(jnp.concatenate([mass_row(j) for j in range(rows)], axis=0))
     edge_rows = [[], [], [], []]
     for j in range(rows):
@@ -123,31 +164,34 @@
         edge_rows[1].append(turned[LANES - 1 :])
         edge_rows[2].append(turned[0:1])
         edge_rows[3].append(jnp.where(lane_row >= 2 * levels, west_mass, turned[1:2]))
-    edges = jnp.concatenate([row for group in edge_rows for row in group], axis=0)
-
-    diffs = half_levels(diff_ref[0:half], diff_ref[faces - half :])
+    edge_ref[...] = jnp.concatenate([row for group in edge_rows for row in group], axis=0)
+
     slots = jnp.concatenate([slot_ref[j : j + 1, :] for j in range(rows)], axis=1)
     extra = jnp.concatenate(
         [slots.astype(jnp.float32) + 1.0, jnp.zeros((7, rows * LANES), jnp.float32)], axis=0
     )
     payload = jnp.concatenate([shear, extra], axis=0)
+    misc = jnp.concatenate(
+        [
+            jnp.zeros((1, LANES), jnp.float32),
+            start_row,
+            edge_rows[1][last],
+            edge_rows[2][last],
+            edge_rows[1][0],
+            edge_rows[2][0],
+            jnp.zeros((2, LANES), jnp.float32),
+        ],
+        axis=0,
+    )
 
     def fill(dest):
         hot = hot_matrix(rank_ref[pl.ds(dest, 1), :], LANES)
         grouped = pick_columns(payload, hot)
-        slot_row = grouped[half : half + 1] - 1.0
-        tail = jnp.concatenate(
-            [pltpu.roll(slot_row, (3 * levels - j * levels) % LANES, 1) for j in range(rows)], axis=0
-        )
-        send_ref[dest, 0 : EDGE - rows] = edges[: EDGE - rows]
-        send_ref[dest, EDGE - rows : EDGE] = jnp.where(
-            lane_row >= 3 * levels, tail, edges[EDGE - rows :]
-        )
-        send_ref[dest, EDGE : EDGE + half] = grouped[:half]
-        for span in range(spans):
-            send_ref[dest, EDGE + half * (span + 1) : EDGE + half * (span + 2)] = diffs[
-                :, span * LANES : (span + 1) * LANES
-            ]
+        send_ref[dest, 0:MISC] = misc
+        send_ref[dest, 0:1] = grouped[half : half + 1] - 1.0
+        send_ref[dest, MISC : MISC + half] = grouped[:half]
+        for group in range(rows):
+            send_ref[dest, MISC + half * (group + 1) : MISC + half * (group + 2)] = packed[group]
 
     loop_over(devices, fill)
 
@@ -158,7 +202,7 @@
 
 def select_kernel(
     levels, rows, devices, recv_ref, owner_ref, slot_ref, diff_ref, count_ref, shear_ref,
-    mine_ref, place_ref, arrived_ref,
+    after_ref, mine_ref, start_ref, arrived_ref,
 ):
     faces = levels - 1
     half = levels // 2
@@ -167,63 +211,66 @@
     cols = rows * LANES
     lane_row = lane_iota((1, LANES))
 
-    for j in range(rows):
-        mine_ref[:, j * LANES : (j + 1) * LANES] = jnp.zeros((half, LANES), jnp.float32)
-    span_of = []
-    position = []
-    for j in range(rows):
-        slot = slot_ref[j : j + 1, :]
-        span = slot // LANES
-        span_of.append(owner_ref[j : j + 1, :] * spans + span)
-        position.append(jnp.broadcast_to(slot - span * LANES, (half, LANES)))
+    owner = owner_ref[...]
+    slot = slot_ref[...]
+    span = slot // LANES
+    start_ref[...] = jnp.zeros((rows, LANES), jnp.float32)
+
+    def look_up(source):
+        table = jnp.broadcast_to(recv_ref[source, 1:2, :], (rows, LANES))
+        start_ref[...] = jnp.where(
+            owner == source, jnp.take_along_axis(table, span, axis=1), start_ref[...]
+        )
+
+    loop_over(devices, look_up)
+    place = start_ref[...].astype(jnp.int32) + (slot - span * LANES)
+    group_of = owner * rows + place // LANES
+    position = place & (LANES - 1)
+
+    mine_ref[:, 0:cols] = jnp.zeros((half, cols), jnp.float32)
 
     def gather(source):
         for j in range(rows):
+            spot = jnp.broadcast_to(position[j : j + 1], (half, LANES))
             found = mine_ref[:, j * LANES : (j + 1) * LANES]
-            for span in range(spans):
-                held = recv_ref[source, EDGE + half * (span + 1) : EDGE + half * (span + 2), :]
-                taken = jnp.take_along_axis(held, position[j], axis=1)
-                found = jnp.where(span_of[j] == source * spans + span, taken, found)
+            for group in range(rows):
+                held = recv_ref[source, MISC + half * (group + 1) : MISC + half * (group + 2), :]
+                taken = jnp.take_along_axis(held, spot, axis=1)
+                found = jnp.where(group_of[j : j + 1] == source * rows + group, taken, found)
             mine_ref[:, j * LANES : (j + 1) * LANES] = found
 
     loop_over(devices, gather)
     mine_ref[:, 0:cols] = 0.5 * mine_ref[:, 0:cols] + source_term(shear_ref[...])
 
-    def unpack(source):
-        tail = recv_ref[source, EDGE - rows : EDGE, :]
-        slot_row = jnp.zeros((1, LANES), jnp.float32)
-        for j in range(rows):
-            back = pltpu.roll(tail[j : j + 1], (levels + j * levels) % LANES, 1)
-            slot_row = jnp.where(lane_row // levels == j, back, slot_row)
-        place_ref[source] = slot_row.astype(jnp.int32)
-
-    loop_over(devices, unpack)
+    def slots_of(source):
+        return recv_ref[source, 0:1, :].astype(jnp.int32)
+
     if devices <= 8:
-        slot_row = jnp.concatenate([place_ref[source] for source in range(devices)], axis=1)
+        slot_row = jnp.concatenate([slots_of(source) for source in range(devices)], axis=1)
         arrived = jnp.concatenate(
-            [recv_ref[source, EDGE : EDGE + half, :] for source in range(devices)], axis=1
+            [recv_ref[source, MISC : MISC + half, :] for source in range(devices)], axis=1
         )
         arrived_ref[...] = pick_columns(arrived, hot_matrix(slot_row, slot_total))
     else:
         arrived_ref[...] = jnp.zeros((half, slot_total), jnp.float32)
 
-        def place(source):
+        def add(source):
             arrived_ref[...] += pick_columns(
-                recv_ref[source, EDGE : EDGE + half, :], hot_matrix(place_ref[source], slot_total)
+                recv_ref[source, MISC : MISC + half, :], hot_matrix(slots_of(source), slot_total)
             )
 
-        loop_over(devices, place)
-    for span in range(spans):
-        here = slice(span * LANES, (span + 1) * LANES)
+        loop_over(devices, add)
+    for index in range(spans):
+        here = slice(index * LANES, (index + 1) * LANES)
         old = half_levels(diff_ref[0:half, here], diff_ref[faces - half :, here])
         new = 0.5 * old + source_term(arrived_ref[:, here])
-        active = lane_row < count_ref[span]
-        mine_ref[:, cols + span * LANES : cols + (span + 1) * LANES] = jnp.where(active, new, old)
+        active = lane_row < count_ref[index]
+        mine_ref[:, cols + index * LANES : cols + (index + 1) * LANES] = jnp.where(active, new, old)
 
 
 def advect_kernel(
-    levels, rows, lat_count, lon_count, tr_ref, wind_ref, mass_ref, low_ref, high_ref, edge_ref,
-    out_ref,
+    levels, rows, lat_count, lon_count, tr_ref, wind_ref, mass_ref, low_ref, high_ref, recv_ref,
+    own_ref, west_ref, east_ref, out_ref,
 ):
     lev, two = levels, 2 * levels
     lat, lon = lax.axis_index("lat"), lax.axis_index("lon")
@@ -238,8 +285,11 @@
     south_lat = jnp.maximum(lat - 1, 0)
     north_lat = jnp.minimum(lat + 1, lat_count - 1)
 
-    def edge(lat_index, lon_index, group):
-        return edge_ref[block(lat_index, lon_index), group * rows : (group + 1) * rows, :]
+    def edge(ref, group):
+        return ref[group * rows : (group + 1) * rows, :]
+
+    def corner(lat_index, lon_index, row):
+        return recv_ref[block(lat_index, lon_index), row : row + 1, :]
 
     def east_of(row):
         return jnp.where(lane_row < lev, pltpu.roll(row, 2 * lev, 1), pltpu.roll(row, 3 * lev, 1))
@@ -259,25 +309,14 @@
         zonal = upwind(here_east, here, east_value) - upwind(west_east, west_value, here)
         return here - mass * (zonal + fluxes[1:] - fluxes[:-1])
 
-    far_west = edge(lat, west_lon, 0)
+    far_west, far_east = edge(west_ref, 0), edge(east_ref, 3)
+    own_first, own_last = edge(own_ref, 2), edge(own_ref, 1)
     west = jnp.concatenate(
-        [
-            edge(south_lat, west_lon, 1)[rows - 1 :],
-            edge(lat, west_lon, 1),
-            edge(north_lat, west_lon, 1)[0:1],
-        ],
-        axis=0,
+        [corner(south_lat, west_lon, 2), edge(west_ref, 1), corner(north_lat, west_lon, 4)], axis=0
     )
     east = jnp.concatenate(
-        [
-            edge(south_lat, east_lon, 2)[rows - 1 :],
-            edge(lat, east_lon, 2),
-            edge(north_lat, east_lon, 2)[0:1],
-        ],
-        axis=0,
-    )
-    far_east = edge(lat, east_lon, 3)
-    own_first, own_last = edge(lat, lon, 2), edge(lat, lon, 1)
+        [corner(south_lat, east_lon, 3), edge(east_ref, 2), corner(north_lat, east_lon, 5)], axis=0
+    )
     west_mid, east_mid = west[1 : rows + 1], east[1 : rows + 1]
     west_new = beside(
         west, east_of(far_west), far_west, east_of(west_mid), own_first, north_of(far_west)
@@ -409,46 +448,66 @@
     devices = lat_count * lon_count
     half = levels // 2
     slot_total = diffusivity.shape[1]
-    spans = span_column_count.shape[0]
-    block_rows = EDGE + half * (1 + spans)
+    block_rows = MISC + half * (1 + rows)
     vmem = pl.BlockSpec(memory_space=pltpu.VMEM)
     smem = pl.BlockSpec(memory_space=pltpu.SMEM)
+    hbm = pl.BlockSpec(memory_space=pltpu.HBM)
 
     tr = tracers.reshape(own_count * levels * rows, cols)
     winds = face_winds.reshape(2 * levels * rows, cols)
     mass = inverse_mass.reshape(levels * rows, cols)
 
-    send, north, south, shear = call(
+    send, north, south, shear, edges = call(
         functools.partial(pack_kernel, levels, rows, devices),
         [
             (devices, block_rows, LANES),
             (8 * levels, LANES),
             (7 * levels, LANES),
             (half, rows * LANES),
+            (4 * rows, LANES),
         ],
-        [vmem] * 6,
-        [pltpu.VMEM((devices, rows * LANES), jnp.int32)],
-    )(tr, winds, mass, span_owner, span_slot, diffusivity)
+        [hbm] * 7,
+        [
+            pltpu.VMEM(tr.shape, jnp.float32),
+            pltpu.VMEM(winds.shape, jnp.float32),
+            pltpu.VMEM(mass.shape, jnp.float32),
+            pltpu.VMEM(span_owner.shape, jnp.int32),
+            pltpu.VMEM(span_slot.shape, jnp.int32),
+            pltpu.VMEM(diffusivity.shape, jnp.float32),
+            pltpu.SMEM(span_column_count.shape, jnp.int32),
+            pltpu.VMEM((devices, rows * LANES), jnp.int32),
+            pltpu.SemaphoreType.DMA((7,)),
+        ],
+    )(
+        *(
+            pltpu.with_memory_space_constraint(value, pltpu.HBM)
+            for value in (tr, winds, mass, span_owner, span_slot, diffusivity, span_column_count)
+        )
+    )
     recv = lax.all_to_all(send, ("lat", "lon"), split_axis=0, concat_axis=0, tiled=True)
-    up = [(i, (i + 1) % lat_count) for i in range(lat_count)]
+    up = [(i, i + 1) for i in range(lat_count - 1)]
     down = [(target, source) for source, target in up]
     low = lax.ppermute(north, "lat", up)
     high = lax.ppermute(south, "lat", down)
+    to_east = [(i, (i + 1) % lon_count) for i in range(lon_count)]
+    to_west = [(target, source) for source, target in to_east]
+    west_edges = lax.ppermute(edges, "lon", to_east)
+    east_edges = west_edges if lon_count == 2 else lax.ppermute(edges, "lon", to_west)
     (mine,) = call(
         functools.partial(select_kernel, levels, rows, devices),
         [(half, rows * LANES + slot_total)],
-        [vmem, vmem, vmem, vmem, smem, vmem],
+        [vmem, vmem, vmem, vmem, smem, vmem, pl.BlockSpec(memory_space=pl.ANY)],
         [
-            pltpu.VMEM((devices, 1, LANES), jnp.int32),
+            pltpu.VMEM((rows, LANES), jnp.float32),
             pltpu.VMEM((half, slot_total), jnp.float32),
         ],
-    )(recv, span_owner, span_slot, diffusivity, span_column_count, shear)
+    )(recv, span_owner, span_slot, diffusivity, span_column_count, shear, west_edges)
     other = lax.ppermute(mine, "lev", [(0, 1), (1, 0)])
     (advected,) = call(
         functools.partial(advect_kernel, levels, rows, lat_count, lon_count),
         [(levels * own_count * rows, LANES)],
-        [vmem] * 6,
-    )(tr, winds, mass, low, high, recv)
+        [vmem] * 9,
+    )(tr, winds, mass, low, high, recv, edges, west_edges, east_edges)
     out, diff_out = call(
         functools.partial(solve_kernel, levels, rows),
         [(own_count * levels * rows, cols), (levels - 1, slot_total)],

time: 35 us -> 26.5 us (0.76)
  waiting for transfers between devices: 13.7 us -> 5.81 us
  local copies, waits for them, and re-layouts: 4.24 us -> 0.04 us
  starting transfers between devices: 11.3 us -> 14.2 us
  Pallas kernels: 4.56 us -> 5.31 us
    all_to_all x1, waiting for transfers between devices: 13.2 us -> 3.11 us  [on_device(): lax.all_to_all(send, ('lat', 'lon'), split_axis=0, concat_axis=0, tiled=T...]
    unnamed x22 -> x14, local copies, waits for them, and re-layouts: 4.24 us -> 0.04 us
    ppermute x0 -> x1, waiting for transfers between devices: none -> 2.19 us  [on_device(): west_edges = lax.ppermute(edges, 'lon', to_east)]
    ppermute x1, starting transfers between devices: 2.02 us -> 3.92 us  [on_device(): low = lax.ppermute(north, 'lat', up)]
    ppermute x0 -> x1, starting transfers between devices: none -> 1.53 us  [on_device(): west_edges = lax.ppermute(edges, 'lon', to_east)]
    pallas_call x1, Pallas kernels: 1.56 us -> 2.43 us  [on_device(): call(functools.partial(pack_kernel, levels, rows, devices), [(devices, bl...]
    ppermute x1, starting transfers between devices: 1.86 us -> 1.29 us  [on_device(): high = lax.ppermute(south, 'lat', down)]
  transfers between devices with their start and end apart: 4 -> 5, of which waited for: 2 -> 3; matrix products, arithmetic and copies ran while one was open for 0% -> 0% of each run, Pallas kernels for 6% -> 7%
where the time goes in v2:
time: 26.5 us; the launch traced here: 26.2 us
  starting transfers between devices  14.2 us (54%)
  waiting for transfers between devices  5.81 us (22%)
  Pallas kernels  5.31 us (20%)
  between operations  0.78 us (3%)
    all_to_all x1, starting transfers between devices, on_device(): lax.all_to_all(send, ('lat', 'lon'), split_axis=0, concat_axis=0, tiled=T...  7.4 us
    ppermute x1, starting transfers between devices, on_device(): low = lax.ppermute(north, 'lat', up)  3.92 us
    all_to_all x1, waiting for transfers between devices, on_device(): lax.all_to_all(send, ('lat', 'lon'), split_axis=0, concat_axis=0, tiled=T...  3.11 us
    pallas_call x1, Pallas kernels, on_device(): call(functools.partial(pack_kernel, levels, rows, devices), [(devices, bl...  2.43 us
    ppermute x1, waiting for transfers between devices, on_device(): west_edges = lax.ppermute(edges, 'lon', to_east)  2.19 us
    ppermute x1, starting transfers between devices, on_device(): west_edges = lax.ppermute(edges, 'lon', to_east)  1.53 us
    ppermute x1, starting transfers between devices, on_device(): high = lax.ppermute(south, 'lat', down)  1.29 us
    pallas_call x1, Pallas kernels, on_device(): call(functools.partial(select_kernel, levels, rows, devices), [(half, row...  1.17 us
  transfers between devices with their start and end apart: 5, of which 3 were waited for; matrix products, arithmetic and copies ran while one was open for 0% of the time, Pallas kernels for 7%

profile of v2, /device:TPU:0, one launch (start us, length us, event | category | flops | bytes accessed | tf_op | source)
XLA Modules:
  0.0 26.2 jit_solution(2060723522314244515)
XLA Ops:
  0.6 2.4 %shard_map.86 = (f32[8,88,128]{2,1,0:T(8,128)}, f32[256,128]{1,0:T(8,128)S(1)}, f32[224,128]{1,0:T(8,128)S(1)}, f32[16,512]{1,0:T(8,128)S(1)}, f32[16,128]{1,0:T(8,128)S(1)}) custom-call(f32[256,128]{1,0:T(8,128)} %bitcast.4, f32[256,128]{1,0:T(8,128)} %bitcast.6, f32[128,128]{1,0:T(8,128)} %bitcast.8, s32[4,128]{1,0:T(4,128)} %owner_ref.1, ...), custom_call_target="tpu_custom_call" | custom-call | tf_op jit(solution)/shard_map/pallas_call | solution.py:460
  3.1 0.0 copy-start.2
  3.1 7.4 %all-to-all-start = ((f32[8,88,128]{2,1,0:T(8,128)}), f32[8,88,128]{2,1,0:T(8,128)S(1)}, u32[]{:S(2)}, u32[]{:S(2)}) async-start(f32[8,88,128]{2,1,0:T(8,128)} %get-tuple-element.11), calls=%async_computation | async-start | bytes 720896 | tf_op jit(solution)/shard_map/all_to_all | solution.py:487
  10.5 3.9 %collective-permute-start = (f32[256,128]{1,0:T(8,128)S(1)}, f32[256,128]{1,0:T(8,128)S(1)}, u32[]{:S(2)}, u32[]{:S(2)}) collective-permute-start(f32[256,128]{1,0:T(8,128)S(1)} %get-tuple-element.9), channel_id=1, source_target_pairs={{0,4},{4,8},{8,12},{1,5},{5,9},{9,13},{2,6},{6,10},{10,14},{3,7},{... | collective-permute-start | bytes 393224 | tf_op jit(solution)/shard_map/ppermute | solution.py:490
  14.4 0.0 copy-start.5
  14.4 0.0 copy-start.4
  14.4 1.3 %collective-permute-start.1 = (f32[224,128]{1,0:T(8,128)S(1)}, f32[224,128]{1,0:T(8,128)S(1)}, u32[]{:S(2)}, u32[]{:S(2)}) collective-permute-start(f32[224,128]{1,0:T(8,128)S(1)} %get-tuple-element.10), channel_id=1, source_target_pairs={{4,0},{8,4},{12,8},{5,1},{9,5},{13,9},{6,2},{10,6},{14,10},{7,3},{... | collective-permute-start | bytes 344072 | tf_op jit(solution)/shard_map/ppermute | solution.py:491
  15.7 0.0 copy-start.6
  15.7 1.5 %collective-permute-start.2 = (f32[16,128]{1,0:T(8,128)S(1)}, f32[16,128]{1,0:T(8,128)S(1)}, u32[]{:S(2)}, u32[]{:S(2)}) collective-permute-start(f32[16,128]{1,0:T(8,128)S(1)} %get-tuple-element.12.own_ref), channel_id=1, source_target_pairs={{0,2},{2,0},{1,3},{3,1},{4,6},{6,4},{5,7},{7,5},{8,10},{10,8},{9,1... | collective-permute-start | bytes 24584 | tf_op jit(solution)/shard_map/ppermute | solution.py:494
  17.3 2.2 %collective-permute-done.2.west_ref.east_ref.after_ref = f32[16,128]{1,0:T(8,128)S(1)} collective-permute-done((f32[16,128]{1,0:T(8,128)S(1)}, f32[16,128]{1,0:T(8,128)S(1)}, u32[]{:S(2)}, u32[]{:S(2)}) %collective-permute-start.2) | collective-permute-done | bytes 8224 | tf_op jit(solution)/shard_map/ppermute | solution.py:494
  19.5 3.1 %all-to-all-done.recv_ref = f32[8,88,128]{2,1,0:T(8,128)S(1)} async-done(((f32[8,88,128]{2,1,0:T(8,128)}), f32[8,88,128]{2,1,0:T(8,128)S(1)}, u32[]{:S(2)}, u32[]{:S(2)}) %all-to-all-start) | async-done | bytes 360480 | tf_op jit(solution)/shard_map/all_to_all | solution.py:487
  22.6 0.0 copy-done.2
  22.6 0.0 copy-done.5
  22.6 0.0 copy-done.4
  22.6 0.0 copy-done.6
  22.6 0.0 copy-start
  22.6 0.0 copy-start.1
  22.6 0.0 copy-start.3
  22.6 1.2 %shard_map.88.mine_ref = f32[16,1152]{1,0:T(8,128)S(1)} custom-call(f32[8,88,128]{2,1,0:T(8,128)S(1)} %all-to-all-done.recv_ref, s32[4,128]{1,0:T(4,128)S(1)} %copy-done.4, s32[4,128]{1,0:T(4,128)S(1)} %copy-done.5, f32[31,640]{1,0:T(8,128)S(1)} %copy-done.2, s32[5]{0:T(128)S(1)} %copy-done.6, f32[16,512]{1,0:T(8,128)S(1)} %get-tuple-element.13.shear_ref, ...), custom_call_target="tpu_custom_call" | custom-call | tf_op jit(solution)/shard_map/pallas_call | solution.py:496
  23.8 0.1 collective-permute-start.3
  23.9 0.0 collective-permute-done.1.high_ref
  23.9 0.0 collective-permute-done.low_ref
  23.9 0.0 copy-done
  23.9 0.0 copy-done.1
  23.9 0.0 copy-done.3
  23.9 0.7 %shard_map.87.adv_ref = f32[256,128]{1,0:T(8,128)S(1)} custom-call(f32[256,128]{1,0:T(8,128)S(1)} %bitcast.5, f32[256,128]{1,0:T(8,128)S(1)} %bitcast.7, f32[128,128]{1,0:T(8,128)S(1)} %bitcast.9, f32[256,128]{1,0:T(8,128)S(1)} %collective-permute-done.low_ref, f32[224,128]{1,0:T(8,128)S(1)} %collective-permute-done.1.high_ref, ...), custom_call_target="tpu_custom_call" | custom-call | tf_op jit(solution)/shard_map/pallas_call | solution.py:506
  24.6 0.5 %collective-permute-done.3.other_ref = f32[16,1152]{1,0:T(8,128)S(1)} collective-permute-done((f32[16,1152]{1,0:T(8,128)S(1)}, f32[16,1152]{1,0:T(8,128)S(1)}, u32[]{:S(2)}, u32[]{:S(2)}) %collective-permute-start.3) | collective-permute-done | bytes 73760 | tf_op jit(solution)/shard_map/ppermute | solution.py:505
  25.1 1.0 %shard_map.89 = (f32[256,128]{1,0:T(8,128)}, f32[31,640]{1,0:T(8,128)}) custom-call(f32[256,128]{1,0:T(8,128)S(1)} %shard_map.87.adv_ref, f32[16,1152]{1,0:T(8,128)S(1)} %shard_map.88.mine_ref, f32[16,1152]{1,0:T(8,128)S(1)} %collective-permute-done.3.other_ref), custom_call_target="tpu_custom_call" | custom-call | tf_op jit(solution)/shard_map/pallas_call | solution.py:511
Async XLA Ops:
  3.1 19.5 %copy-start.2 = (f32[31,640]{1,0:T(8,128)S(1)}, f32[31,640]{1,0:T(8,128)}, u32[]{:S(2)}) copy-start(f32[31,640]{1,0:T(8,128)} %diff_ref.1) | copy-start | bytes 238084
  3.1 19.5 %all-to-all-start = ((f32[8,88,128]{2,1,0:T(8,128)}), f32[8,88,128]{2,1,0:T(8,128)S(1)}, u32[]{:S(2)}, u32[]{:S(2)}) async-start(f32[8,88,128]{2,1,0:T(8,128)} %get-tuple-element.11), calls=%async_computation | async-start | bytes 720896 | tf_op jit(solution)/shard_map/all_to_all | solution.py:487
  10.5 13.4 %collective-permute-start = (f32[256,128]{1,0:T(8,128)S(1)}, f32[256,128]{1,0:T(8,128)S(1)}, u32[]{:S(2)}, u32[]{:S(2)}) collective-permute-start(f32[256,128]{1,0:T(8,128)S(1)} %get-tuple-element.9), channel_id=1, source_target_pairs={{0,4},{4,8},{8,12},{1,5},{5,9},{9,13},{2,6},{6,10},{10,14},{3,7},{... | collective-permute-start | bytes 393224 | tf_op jit(solution)/shard_map/ppermute | solution.py:490
  14.4 8.2 %copy-start.5 = (s32[4,128]{1,0:T(4,128)S(1)}, s32[4,128]{1,0:T(4,128)}, u32[]{:S(2)}) copy-start(s32[4,128]{1,0:T(4,128)} %slot_ref.1) | copy-start | bytes 6148
  14.4 8.2 %copy-start.4 = (s32[4,128]{1,0:T(4,128)S(1)}, s32[4,128]{1,0:T(4,128)}, u32[]{:S(2)}) copy-start(s32[4,128]{1,0:T(4,128)} %owner_ref.1) | copy-start | bytes 6148
  14.4 9.5 %collective-permute-start.1 = (f32[224,128]{1,0:T(8,128)S(1)}, f32[224,128]{1,0:T(8,128)S(1)}, u32[]{:S(2)}, u32[]{:S(2)}) collective-permute-start(f32[224,128]{1,0:T(8,128)S(1)} %get-tuple-element.10), channel_id=1, source_target_pairs={{4,0},{8,4},{12,8},{5,1},{9,5},{13,9},{6,2},{10,6},{14,10},{7,3},{... | collective-permute-start | bytes 344072 | tf_op jit(solution)/shard_map/ppermute | solution.py:491
  15.7 6.9 %copy-start.6 = (s32[5]{0:T(128)S(1)}, s32[5]{0:T(128)}, u32[]{:S(2)}) copy-start(s32[5]{0:T(128)} %count_ref.1) | copy-start | bytes 64
  15.7 3.7 %collective-permute-start.2 = (f32[16,128]{1,0:T(8,128)S(1)}, f32[16,128]{1,0:T(8,128)S(1)}, u32[]{:S(2)}, u32[]{:S(2)}) collective-permute-start(f32[16,128]{1,0:T(8,128)S(1)} %get-tuple-element.12.own_ref), channel_id=1, source_target_pairs={{0,2},{2,0},{1,3},{3,1},{4,6},{6,4},{5,7},{7,5},{8,10},{10,8},{9,1... | collective-permute-start | bytes 24584 | tf_op jit(solution)/shard_map/ppermute | solution.py:494
  22.6 1.3 %copy-start = (f32[2,32,4,128]{3,2,1,0:T(4,128)S(1)}, f32[2,32,4,128]{3,2,1,0:T(4,128)}, u32[]{:S(2)}) copy-start(f32[2,32,4,128]{3,2,1,0:T(4,128)} %param.7) | copy-start | bytes 393220
  22.6 1.3 %copy-start.1 = (f32[2,32,4,128]{3,2,1,0:T(4,128)S(1)}, f32[2,32,4,128]{3,2,1,0:T(4,128)}, u32[]{:S(2)}) copy-start(f32[2,32,4,128]{3,2,1,0:T(4,128)} %param.8) | copy-start | bytes 393220
  22.6 1.3 %copy-start.3 = (f32[32,4,128]{2,1,0:T(4,128)S(1)}, f32[32,4,128]{2,1,0:T(4,128)}, u32[]{:S(2)}) copy-start(f32[32,4,128]{2,1,0:T(4,128)} %param.9) | copy-start | bytes 196612
  23.8 1.3 %collective-permute-start.3 = (f32[16,1152]{1,0:T(8,128)S(1)}, f32[16,1152]{1,0:T(8,128)S(1)}, u32[]{:S(2)}, u32[]{:S(2)}) collective-permute-start(f32[16,1152]{1,0:T(8,128)S(1)} %shard_map.88.mine_ref), channel_id=1, source_target_pairs={{0,1},{1,0},{2,3},{3,2},{4,5},{5,4},{6,7},{7,6},{8,9},{9,8},{10,11... | collective-permute-start | bytes 221192 | tf_op jit(solution)/shard_map/ppermute | solution.py:505

commit v3 on v2

v3 whole, which is shorter than its diff:
```python
import functools

import jax
import jax.numpy as jnp
from jax import lax
from jax.experimental import pallas as pl
from jax.experimental.pallas import tpu as pltpu
from jax.sharding import PartitionSpec as P

LANES = 128
MISC = 8
VMEM_LIMIT = 48 * 1024 * 1024
NT = (((1,), (1,)), ((), ()))


def lane_iota(shape):
    return lax.broadcasted_iota(jnp.int32, shape, len(shape) - 1)


def split3(values):
    top = values.astype(jnp.bfloat16)
    rest = values - top.astype(jnp.float32)
    mid = rest.astype(jnp.bfloat16)
    low = (rest - mid.astype(jnp.float32)).astype(jnp.bfloat16)
    return jnp.concatenate([top, mid, low], axis=0)


def hot_matrix(row_of, size):
    index = lax.broadcasted_iota(jnp.int32, (size, row_of.shape[-1]), 0)
    return jnp.where(index == row_of, 1.0, 0.0).astype(jnp.bfloat16)


def pick_columns(masked, hot, rows):
    out = lax.dot_general(masked, hot, NT, preferred_element_type=jnp.float32)
    return [
        out[at : at + rows] + out[at + rows : at + 2 * rows] + out[at + 2 * rows : at + 3 * rows]
        for at in range(0, masked.shape[0], 3 * rows)
    ]


def only_where(split, key, wanted):
    return split * jnp.where(key == wanted, 1.0, 0.0).astype(jnp.bfloat16)


def loop_over(count, body):
    if count <= 8:
        for index in range(count):
            body(index)
    else:
        pl.loop(0, count)(body)


def half_levels(first, second):
    return jnp.where(lax.axis_index("lev") == 0, first, second)


def pack_kernel(
    levels, rows, devices, tr_hbm, wind_hbm, mass_hbm, owner_hbm, slot_hbm, diff_hbm, count_hbm,
    send_hbm, even_ref, odd_ref, shear_ref, edge_ref, active_ref,
    tr_ref, wind_ref, mass_ref, owner_ref, slot_ref, diff_ref, count_ref, send_ref, sems,
):
    faces = levels - 1
    half = levels // 2
    spans = diff_ref.shape[1] // LANES
    last = rows - 1
    head = MISC + half
    pairs = [
        (owner_hbm, owner_ref), (slot_hbm, slot_ref), (count_hbm, count_ref), (diff_hbm, diff_ref),
        (wind_hbm, wind_ref), (tr_hbm, tr_ref), (mass_hbm, mass_ref),
    ]
    copies = [
        pltpu.make_async_copy(source, target, sems.at[index])
        for index, (source, target) in enumerate(pairs)
    ]
    for copy in copies:
        copy.start()

    def tracer_row(j):
        return tr_ref[pl.ds(j, 2 * levels, stride=rows), :]

    def east_row(j):
        return wind_ref[pl.ds(j, levels, stride=rows), :]

    def north_row(j):
        return wind_ref[pl.ds(levels * rows + j, levels, stride=rows), :]

    def mass_row(j):
        return mass_ref[pl.ds(j, levels, stride=rows), :]

    copies[0].wait()
    owner_index = lax.broadcasted_iota(jnp.int32, (devices, LANES), 0)
    owned = [owner_index == owner_ref[j : j + 1, :] for j in range(rows)]
    upto = lax.broadcasted_iota(jnp.int32, (LANES, LANES), 0) <= lane_iota((LANES, LANES))
    counted = lax.dot_general(
        jnp.concatenate([jnp.where(hit, 1.0, 0.0) for hit in owned], axis=0).astype(jnp.bfloat16),
        jnp.where(upto, 1.0, 0.0).astype(jnp.bfloat16),
        (((1,), (0,)), ((), ())),
        preferred_element_type=jnp.float32,
    )
    before = jnp.full((devices, 1), -1.0, jnp.float32)
    ranks = []
    for j in range(rows):
        count = counted[j * devices : (j + 1) * devices]
        ranks.append(jnp.sum(jnp.where(owned[j], count + before, 0.0), axis=0, keepdims=True))
        before = before + count[:, LANES - 1 :]
    rank = jnp.concatenate(ranks, axis=1).astype(jnp.int32)
    owner = jnp.concatenate([owner_ref[j : j + 1, :] for j in range(rows)], axis=1)
    copies[1].wait()
    slots = jnp.concatenate([slot_ref[j : j + 1, :] for j in range(rows)], axis=1)

    copies[2].wait()
    copies[3].wait()
    diffs = half_levels(diff_ref[0:half], diff_ref[faces - half :])
    lane_half = lane_iota((half, LANES))
    lane_row = lane_iota((1, LANES))
    starts, start = [], 0
    for span in range(spans):
        starts.append(start)
        start = start + count_ref[span]
    for group in range(rows):
        if group < last:
            value = jnp.zeros((half, LANES), jnp.float32)
            for span in range(spans - 1):
                spot = lane_half + (group * LANES - starts[span])
                taken = jnp.take_along_axis(
                    diffs[:, span * LANES : (span + 1) * LANES], spot & (LANES - 1), axis=1
                )
                value = jnp.where((spot >= 0) & (spot < count_ref[span]), taken, value)
        else:
            value = diffs[:, (spans - 1) * LANES :]

        def store(dest):
            send_ref[dest, head + half * group : head + half * (group + 1)] = value

        loop_over(devices, store)
    put_diffs = pltpu.make_async_copy(
        send_ref.at[:, pl.ds(head, half * rows)],
        send_hbm.at[:, pl.ds(head, half * rows)],
        sems.at[len(pairs)],
    )
    put_diffs.start()
    start_row = jnp.zeros((1, LANES), jnp.float32)
    for span in range(spans):
        here = lax.convert_element_type(starts[span], jnp.float32)
        start_row = jnp.where(lane_row == span, here, start_row)
        active_ref[:, span * LANES : (span + 1) * LANES] = jnp.where(
            lane_row < count_ref[span], 1.0, 0.0
        )

    copies[4].wait()
    shears = []
    for j in range(rows):
        east, north = east_row(j), north_row(j)
        east_step = east[1:] - east[:-1]
        north_step = north[1:] - north[:-1]
        shear = east_step * east_step + north_step * north_step
        shears.append(half_levels(shear[:half], shear[faces - half :]))
    shear = jnp.concatenate(shears, axis=1)
    shear_ref[...] = shear

    copies[5].wait()
    turned = [
        jnp.transpose(jnp.concatenate([tracer_row(j), east_row(j), north_row(j)], axis=0))
        for j in range(rows)
    ]
    misc = jnp.concatenate(
        [
            start_row,
            turned[last][LANES - 1 :],
            turned[last][0:1],
            turned[0][LANES - 1 :],
            turned[0][0:1],
            jnp.zeros((2, LANES), jnp.float32),
        ],
        axis=0,
    )

    extra = jnp.concatenate(
        [slots.astype(jnp.float32) + 1.0, jnp.zeros((7, rows * LANES), jnp.float32)], axis=0
    )
    split = split3(jnp.concatenate([shear, extra], axis=0))
    hot = hot_matrix(rank, LANES)

    def fill(dest, grouped):
        send_ref[dest, 0:1] = grouped[half : half + 1] - 1.0
        send_ref[dest, 1:MISC] = misc
        send_ref[dest, MISC:head] = grouped[:half]

    if devices <= 8:
        masked = [only_where(split, owner, dest) for dest in range(devices)]
        for dest, grouped in enumerate(
            pick_columns(jnp.concatenate(masked, axis=0), hot, half + 8)
        ):
            fill(dest, grouped)
    else:
        pl.loop(0, devices)(
            lambda dest: fill(dest, pick_columns(only_where(split, owner, dest), hot, half + 8)[0])
        )
    put_head = pltpu.make_async_copy(
        send_ref.at[:, pl.ds(0, head)], send_hbm.at[:, pl.ds(0, head)], sems.at[len(pairs) + 1]
    )
    put_head.start()

    copies[6].wait()
    masses = jnp.transpose(jnp.concatenate([mass_row(j) for j in range(rows)], axis=0))
    edge_rows = [[], [], [], []]
    for j in range(rows):
        west_mass = pltpu.roll(masses[0:1], (2 * levels - j * levels) % LANES, 1)
        east_mass = pltpu.roll(masses[LANES - 1 :], (3 * levels - j * levels) % LANES, 1)
        edge_rows[0].append(
            jnp.where(lane_row >= 3 * levels, east_mass, turned[j][LANES - 2 : LANES - 1])
        )
        edge_rows[1].append(turned[j][LANES - 1 :])
        edge_rows[2].append(turned[j][0:1])
        edge_rows[3].append(jnp.where(lane_row >= 2 * levels, west_mass, turned[j][1:2]))
    edge_ref[...] = jnp.concatenate([row for group in edge_rows for row in group], axis=0)

    def put_rows(ref, far, near):
        two, lev = 2 * levels, levels
        ref[0:two] = tracer_row(far)
        ref[two : 2 * two] = tracer_row(near)
        ref[2 * two : 2 * two + lev] = east_row(near)
        ref[2 * two + lev : 2 * two + 2 * lev] = north_row(far)
        ref[2 * two + 2 * lev : 2 * two + 3 * lev] = north_row(near)
        ref[2 * two + 3 * lev : 2 * two + 4 * lev] = mass_row(near)

    even = lax.rem(lax.axis_index("lat"), 2) == 0

    @pl.when(even)
    def _():
        put_rows(even_ref, last - 1, last)
        put_rows(odd_ref, 1, 0)

    @pl.when(jnp.logical_not(even))
    def _():
        put_rows(even_ref, 1, 0)
        put_rows(odd_ref, last - 1, last)

    put_diffs.wait()
    put_head.wait()


def source_term(shear):
    return 2.0 * shear / (0.05 + shear)


def select_kernel(
    levels, rows, devices, recv_ref, owner_ref, slot_ref, diff_ref, active_ref, shear_ref,
    after_ref, mine_ref, start_ref, arrived_ref,
):
    faces = levels - 1
    half = levels // 2
    slot_total = diff_ref.shape[1]
    spans = slot_total // LANES
    cols = rows * LANES

    owner = owner_ref[...]
    slot = slot_ref[...]
    span = slot // LANES
    start_ref[...] = jnp.zeros((rows, LANES), jnp.float32)

    def look_up(source):
        table = jnp.broadcast_to(recv_ref[source, 1:2, :], (rows, LANES))
        start_ref[...] = jnp.where(
            owner == source, jnp.take_along_axis(table, span, axis=1), start_ref[...]
        )

    loop_over(devices, look_up)
    place = start_ref[...].astype(jnp.int32) + (slot - span * LANES)
    group_of = owner * rows + place // LANES
    position = place & (LANES - 1)

    mine_ref[:, 0:cols] = jnp.zeros((half, cols), jnp.float32)

    def gather(source):
        for j in range(rows):
            spot = jnp.broadcast_to(position[j : j + 1], (half, LANES))
            found = mine_ref[:, j * LANES : (j + 1) * LANES]
            for group in range(rows):
                held = recv_ref[source, MISC + half * (group + 1) : MISC + half * (group + 2), :]
                taken = jnp.take_along_axis(held, spot, axis=1)
                found = jnp.where(group_of[j : j + 1] == source * rows + group, taken, found)
            mine_ref[:, j * LANES : (j + 1) * LANES] = found

    loop_over(devices, gather)
    mine_ref[:, 0:cols] = 0.5 * mine_ref[:, 0:cols] + source_term(shear_ref[...])

    def place(slot_row, values):
        split = split3(values)
        masked = [only_where(split, slot_row >> 7, index) for index in range(spans)]
        hot = hot_matrix(slot_row & (LANES - 1), LANES)
        return jnp.concatenate(
            pick_columns(jnp.concatenate(masked, axis=0), hot, half), axis=1
        )

    def slots_of(source):
        return recv_ref[source, 0:1, :].astype(jnp.int32)

    def shears_of(source):
        return recv_ref[source, MISC : MISC + half, :]

    if devices <= 8:
        arrived_ref[...] = place(
            jnp.concatenate([slots_of(source) for source in range(devices)], axis=1),
            jnp.concatenate([shears_of(source) for source in range(devices)], axis=1),
        )
    else:
        arrived_ref[...] = jnp.zeros((half, slot_total), jnp.float32)

        @pl.loop(0, devices)
        def _(source):
            arrived_ref[...] += place(slots_of(source), shears_of(source))

    old = half_levels(diff_ref[0:half], diff_ref[faces - half :])
    new = 0.5 * old + source_term(arrived_ref[...])
    mine_ref[:, cols:] = jnp.where(active_ref[...] > 0.0, new, old)


def advect_kernel(
    levels, rows, lat_count, lon_count, tr_ref, wind_ref, mass_ref, even_ref, odd_ref, recv_ref,
    own_ref, west_ref, east_ref, out_ref,
):
    lev, two = levels, 2 * levels
    lat, lon = lax.axis_index("lat"), lax.axis_index("lon")
    first, final = lat == 0, lat == lat_count - 1
    lane_row = lane_iota((1, LANES))

    def block(lat_index, lon_index):
        return lat_index * lon_count + lon_index

    west_lon = lax.rem(lon + lon_count - 1, lon_count)
    east_lon = lax.rem(lon + 1, lon_count)
    south_lat = jnp.maximum(lat - 1, 0)
    north_lat = jnp.minimum(lat + 1, lat_count - 1)

    def edge(ref, group):
        return ref[group * rows : (group + 1) * rows, :]

    def corner(lat_index, lon_index, row):
        return recv_ref[block(lat_index, lon_index), row : row + 1, :]

    def east_of(row):
        return jnp.where(lane_row < lev, pltpu.roll(row, 2 * lev, 1), pltpu.roll(row, 3 * lev, 1))

    def north_of(row):
        return jnp.where(lane_row < lev, pltpu.roll(row, lev, 1), pltpu.roll(row, 2 * lev, 1))

    def upwind(wind, here, ahead):
        return jnp.maximum(wind, 0.0) * here + jnp.minimum(wind, 0.0) * ahead

    def beside(column, west_east, west_value, here_east, east_value, mass):
        fluxes = upwind(north_of(column[: rows + 1]), column[: rows + 1], column[1:])
        index = lax.broadcasted_iota(jnp.int32, (rows + 1, LANES), 0)
        closed = ((index == 0) & first) | ((index == rows) & final)
        fluxes = jnp.where(closed, 0.0, fluxes)
        here = column[1 : rows + 1]
        zonal = upwind(here_east, here, east_value) - upwind(west_east, west_value, here)
        return here - mass * (zonal + fluxes[1:] - fluxes[:-1])

    far_west, far_east = edge(west_ref, 0), edge(east_ref, 3)
    own_first, own_last = edge(own_ref, 2), edge(own_ref, 1)
    west = jnp.concatenate(
        [corner(south_lat, west_lon, 2), edge(west_ref, 1), corner(north_lat, west_lon, 4)], axis=0
    )
    east = jnp.concatenate(
        [corner(south_lat, east_lon, 3), edge(east_ref, 2), corner(north_lat, east_lon, 5)], axis=0
    )
    west_mid, east_mid = west[1 : rows + 1], east[1 : rows + 1]
    west_new = beside(
        west, east_of(far_west), far_west, east_of(west_mid), own_first, north_of(far_west)
    )
    east_new = beside(
        east, east_of(own_last), own_last, east_of(east_mid), far_east, east_of(far_east)
    )
    filler = jnp.zeros((LANES - 2 * (rows + 2) - 2 * rows, LANES), jnp.float32)
    turned = jnp.transpose(jnp.concatenate([west, east, west_new, east_new, filler], axis=0))

    def column(index, start, size):
        return jnp.broadcast_to(turned[start : start + size, index : index + 1], (size, LANES))

    def place(value, lane, index, start, size):
        return jnp.where(lane_row == lane, column(index, start, size), value)

    even = lax.rem(lat, 2) == 0

    def low(start, size):
        return jnp.where(even, odd_ref[start : start + size], even_ref[start : start + size])

    def high(start, size):
        return jnp.where(even, even_ref[start : start + size], odd_ref[start : start + size])

    tracer = {-2: low(0, two), -1: low(two, two)}
    east_wind = {-1: low(2 * two, lev)}
    north_wind = {-2: low(2 * two + lev, lev), -1: low(2 * two + 2 * lev, lev)}
    mass = {-1: low(2 * two + 3 * lev, lev)}
    for j in range(rows):
        tracer[j] = tr_ref[pl.ds(j, two, stride=rows), :]
        east_wind[j] = wind_ref[pl.ds(j, lev, stride=rows), :]
        north_wind[j] = wind_ref[pl.ds(levels * rows + j, lev, stride=rows), :]
        mass[j] = mass_ref[pl.ds(j, lev, stride=rows), :]
    tracer[rows], tracer[rows + 1] = high(two, two), high(0, two)
    east_wind[rows] = high(2 * two, lev)
    north_wind[rows] = high(2 * two + 2 * lev, lev)
    mass[rows] = high(2 * two + 3 * lev, lev)

    west_wind = {
        j: place(pltpu.roll(east_wind[j], 1, 1), 0, j + 1, two, lev) for j in range(-1, rows + 1)
    }

    def substep(field, row_range, west_index, east_index, start):
        fluxes = {}
        for j in range(row_range[0] - 1, row_range[-1] + 1):
            flux = upwind(north_wind[j], field[j], field[j + 1])
            if j == -1:
                flux = jnp.where(first, 0.0, flux)
            if j == rows - 1:
                flux = jnp.where(final, 0.0, flux)
            fluxes[j] = flux
        result = {}
        for j in row_range:
            here = field[j]
            ahead = place(pltpu.roll(here, LANES - 1, 1), LANES - 1, east_index(j), start, lev)
            behind = place(pltpu.roll(here, 1, 1), 0, west_index(j), start, lev)
            zonal = upwind(east_wind[j], here, ahead) - upwind(west_wind[j], behind, here)
            result[j] = here - mass[j] * (zonal + fluxes[j] - fluxes[j - 1])
        return result

    for t in range(2):
        start = t * lev
        field = {j: value[start : start + lev] for j, value in tracer.items()}
        once = substep(
            field, range(-1, rows + 1), lambda j: j + 1, lambda j: rows + 2 + j + 1, start
        )
        base = 2 * (rows + 2)
        twice = substep(once, range(rows), lambda j: base + j, lambda j: base + rows + j, start)
        for j in range(rows):
            out_ref[pl.ds(t * rows + j, lev, stride=2 * rows), :] = twice[j]


def solve_kernel(
    levels, rows, adv_ref, mine_ref, other_ref, out_hbm, diff_hbm, out_ref, diff_ref, kv_ref, sems
):
    faces = levels - 1
    half = levels // 2
    cols = rows * LANES
    width = 2 * rows
    low = half_levels(mine_ref[...], other_ref[...])
    high = half_levels(other_ref[...], mine_ref[...])
    diff_ref[0:half] = low[:, cols:]
    diff_ref[half:] = high[1:, cols:]
    put_diff = pltpu.make_async_copy(diff_ref, diff_hbm, sems.at[0])
    put_diff.start()
    for j in range(rows):
        here = slice(j * LANES, (j + 1) * LANES)
        for t in range(2):
            kv_ref[pl.ds(t * rows + j, half, stride=width), :] = low[:, here]
            kv_ref[pl.ds((faces - half) * width + t * rows + j, half, stride=width), :] = high[:, here]

    def face(level):
        return kv_ref[level * width : (level + 1) * width]

    def eliminate(order, outer_face, inner_face):
        ratios, sweeps = {}, {}
        last_level = None
        for level in order:
            rhs = adv_ref[level * width : (level + 1) * width]
            inner = inner_face(level)
            pivot = 1.0 + inner
            if last_level is not None:
                outer = outer_face(level)
                pivot = pivot + outer - outer * ratios[last_level]
                rhs = rhs + outer * sweeps[last_level]
            inverse = 1.0 / pivot
            ratios[level] = inner * inverse
            sweeps[level] = rhs * inverse
            last_level = level
        return ratios, sweeps

    down, down_sweep = eliminate(range(half), lambda k: face(k - 1), face)
    up, up_sweep = eliminate(range(levels - 1, half - 1, -1), face, lambda k: face(k - 1))

    def put(level, value):
        for t in range(2):
            out_ref[(t * levels + level) * rows : (t * levels + level + 1) * rows] = value[
                t * rows : (t + 1) * rows
            ]

    below = (down_sweep[half - 1] + down[half - 1] * up_sweep[half]) / (
        1.0 - down[half - 1] * up[half]
    )
    above = up_sweep[half] + up[half] * below
    put(half - 1, below)
    put(half, above)
    for step in range(1, half):
        below = down_sweep[half - 1 - step] + down[half - 1 - step] * below
        above = up_sweep[half + step] + up[half + step] * above
        put(half - 1 - step, below)
        put(half + step, above)
    put_out = pltpu.make_async_copy(out_ref, out_hbm, sems.at[1])
    put_out.start()
    put_diff.wait()
    put_out.wait()


def call(kernel, outs, in_specs, out_specs, scratch=()):
    return pl.pallas_call(
        kernel,
        out_shape=[jax.ShapeDtypeStruct(shape, jnp.float32) for shape in outs],
        in_specs=in_specs,
        out_specs=out_specs,
        scratch_shapes=list(scratch),
        compiler_params=pltpu.CompilerParams(vmem_limit_bytes=VMEM_LIMIT),
    )


def on_device(
    tracers, face_winds, inverse_mass, span_owner, span_slot, span_column_count, diffusivity
):
    own_count, levels, rows, cols = tracers.shape
    lat_count, lon_count = lax.axis_size("lat"), lax.axis_size("lon")
    devices = lat_count * lon_count
    half = levels // 2
    slot_total = diffusivity.shape[1]
    block_rows = MISC + half * (1 + rows)
    vmem = pl.BlockSpec(memory_space=pltpu.VMEM)
    hbm = pl.BlockSpec(memory_space=pltpu.HBM)

    tr = tracers.reshape(own_count * levels * rows, cols)
    winds = face_winds.reshape(2 * levels * rows, cols)
    mass = inverse_mass.reshape(levels * rows, cols)

    send, to_even, to_odd, shear, edges, active = call(
        functools.partial(pack_kernel, levels, rows, devices),
        [
            (devices, block_rows, LANES),
            (8 * levels, LANES),
            (8 * levels, LANES),
            (half, rows * LANES),
            (4 * rows, LANES),
            (1, slot_total),
        ],
        [hbm] * 7,
        [hbm] + [vmem] * 5,
        [
            pltpu.VMEM(tr.shape, jnp.float32),
            pltpu.VMEM(winds.shape, jnp.float32),
            pltpu.VMEM(mass.shape, jnp.float32),
            pltpu.VMEM(span_owner.shape, jnp.int32),
            pltpu.VMEM(span_slot.shape, jnp.int32),
            pltpu.VMEM(diffusivity.shape, jnp.float32),
            pltpu.SMEM(span_column_count.shape, jnp.int32),
            pltpu.VMEM((devices, block_rows, LANES), jnp.float32),
            pltpu.SemaphoreType.DMA((9,)),
        ],
    )(
        *(
            pltpu.with_memory_space_constraint(value, pltpu.HBM)
            for value in (tr, winds, mass, span_owner, span_slot, diffusivity, span_column_count)
        )
    )
    recv = lax.all_to_all(send, ("lat", "lon"), split_axis=0, concat_axis=0, tiled=True)
    even_pairs = [(i, i + 1) for i in range(0, lat_count - 1, 2)]
    odd_pairs = [(i, i + 1) for i in range(1, lat_count - 1, 2)]
    from_even = lax.ppermute(to_even, "lat", even_pairs + [(b, a) for a, b in even_pairs])
    from_odd = lax.ppermute(to_odd, "lat", odd_pairs + [(b, a) for a, b in odd_pairs])
    to_east = [(i, (i + 1) % lon_count) for i in range(lon_count)]
    to_west = [(target, source) for source, target in to_east]
    west_edges = lax.ppermute(edges, "lon", to_east)
    east_edges = west_edges if lon_count == 2 else lax.ppermute(edges, "lon", to_west)
    (mine,) = call(
        functools.partial(select_kernel, levels, rows, devices),
        [(half, rows * LANES + slot_total)],
        [vmem] * 6 + [pl.BlockSpec(memory_space=pl.ANY)],
        [vmem],
        [
            pltpu.VMEM((rows, LANES), jnp.float32),
            pltpu.VMEM((half, slot_total), jnp.float32),
        ],
    )(recv, span_owner, span_slot, diffusivity, active, shear, west_edges)
    other = lax.ppermute(mine, "lev", [(0, 1), (1, 0)])
    (advected,) = call(
        functools.partial(advect_kernel, levels, rows, lat_count, lon_count),
        [(levels * own_count * rows, LANES)],
        [vmem] * 9,
        [vmem],
    )(tr, winds, mass, from_even, from_odd, recv, edges, west_edges, east_edges)
    out, diff_out = call(
        functools.partial(solve_kernel, levels, rows),
        [(own_count * levels * rows, cols), (levels - 1, slot_total)],
        [vmem] * 3,
        [hbm] * 2,
        [
            pltpu.VMEM((own_count * levels * rows, cols), jnp.float32),
            pltpu.VMEM((levels - 1, slot_total), jnp.float32),
            pltpu.VMEM((levels * 2 * rows, LANES), jnp.float32),
            pltpu.SemaphoreType.DMA((2,)),
        ],
    )(advected, mine, other)
    return out.reshape(own_count, levels, rows, cols), diff_out


def solution(mesh):
    placed = (
        P("lev", "ens", "lat", "lon"),
        P(None, "ens", "lat", "lon"),
        P("ens", "lat", "lon"),
        P("lat", "lon"),
        P("lat", "lon"),
        P(("lat", "lon")),
        P("ens", ("lat", "lon")),
    )
    return jax.shard_map(
        on_device,
        mesh=mesh,
        in_specs=placed,
        out_specs=(P("lev", "ens", "lat", "lon"), P("ens", ("lat", "lon"))),
        check_vma=False,
    )
```

time: 26.5 us -> 25.8 us (0.974)
  waiting for transfers between devices: 5.81 us -> 8.48 us
  starting transfers between devices: 14.2 us -> 11.7 us
  Pallas kernels: 5.31 us -> 4.34 us
    all_to_all x1, waiting for transfers between devices: 3.11 us -> 5.98 us  [on_device(): lax.all_to_all(send, ('lat', 'lon'), split_axis=0, concat_axis=0, tiled=T...]
    ppermute x2, starting transfers between devices: 5.21 us -> 2.68 us  [the longest x1 2.02 us: on_device(): lax.ppermute(to_even, 'lat', even_pairs + [(b, a) for a, b in even_pairs])]
    pallas_call x1, Pallas kernels: 1.17 us -> 0.61 us  [on_device(): call(functools.partial(select_kernel, levels, rows, devices), [(half, row...]
    pallas_call x1, Pallas kernels: 2.43 us -> 2.15 us  [on_device(): call(functools.partial(pack_kernel, levels, rows, devices), [(devices, bl...]
  transfers between devices with their start and end apart: 5 -> 5, of which waited for: 3 -> 3; matrix products, arithmetic and copies ran while one was open for 0% -> 0% of each run, Pallas kernels for 7% -> 5%
where the time goes in v3:
time: 25.8 us; the launch traced here: 25.5 us
  starting transfers between devices  11.7 us (45%)
  waiting for transfers between devices  8.48 us (33%)
  Pallas kernels  4.34 us (17%)
  between operations  0.74 us (3%)
  local copies, waits for them, and re-layouts  0.26 us (1%)
    all_to_all x1, starting transfers between devices, on_device(): lax.all_to_all(send, ('lat', 'lon'), split_axis=0, concat_axis=0, tiled=T...  7.4 us
    all_to_all x1, waiting for transfers between devices, on_device(): lax.all_to_all(send, ('lat', 'lon'), split_axis=0, concat_axis=0, tiled=T...  5.98 us
    ppermute x1, waiting for transfers between devices, on_device(): west_edges = lax.ppermute(edges, 'lon', to_east)  2.19 us
    pallas_call x1, Pallas kernels, on_device(): call(functools.partial(pack_kernel, levels, rows, devices), [(devices, bl...  2.15 us
    ppermute x1, starting transfers between devices, on_device(): lax.ppermute(to_even, 'lat', even_pairs + [(b, a) for a, b in even_pairs])  2.02 us
    ppermute x1, starting transfers between devices, on_device(): west_edges = lax.ppermute(edges, 'lon', to_east)  1.53 us
    pallas_call x1, Pallas kernels, on_device(): call(functools.partial(solve_kernel, levels, rows), [(own_count * levels...  0.89 us
    pallas_call x1, Pallas kernels, on_device(): call(functools.partial(advect_kernel, levels, rows, lat_count, lon_count)...  0.69 us
  transfers between devices with their start and end apart: 5, of which 3 were waited for; matrix products, arithmetic and copies ran while one was open for 0% of the time, Pallas kernels for 5%

profile of v3, /device:TPU:0, one launch (start us, length us, event | category | flops | bytes accessed | tf_op | source)
XLA Modules:
  0.0 25.5 jit_solution(4378361578348344034)
XLA Ops:
  0.6 2.1 %shard_map.86 = (f32[8,88,128]{2,1,0:T(8,128)}, f32[256,128]{1,0:T(8,128)S(1)}, f32[256,128]{1,0:T(8,128)S(1)}, f32[16,512]{1,0:T(8,128)S(1)}, f32[16,128]{1,0:T(8,128)S(1)}, /*index=5*/f32[1,640]{1,0:T(1,128)S(1)}) custom-call(f32[256,128]{1,0:T(8,128)} %bitcast.4, f32[256,128]{1,0:T(8,128)} %bitcast.6, f32[128,128]{1,0:T(8,128)} %bitcast.8, ...), custom_call_target="tpu_custom_call" | custom-call | tf_op jit(solution)/shard_map/pallas_call | solution.py:532
  2.8 0.0 copy-start.2
  2.8 7.4 %all-to-all-start = ((f32[8,88,128]{2,1,0:T(8,128)}), f32[8,88,128]{2,1,0:T(8,128)S(1)}, u32[]{:S(2)}, u32[]{:S(2)}) async-start(f32[8,88,128]{2,1,0:T(8,128)} %get-tuple-element.12), calls=%async_computation | async-start | bytes 720896 | tf_op jit(solution)/shard_map/all_to_all | solution.py:561
  10.2 2.0 %collective-permute-start = (f32[256,128]{1,0:T(8,128)S(1)}, f32[256,128]{1,0:T(8,128)S(1)}, u32[]{:S(2)}, u32[]{:S(2)}) collective-permute-start(f32[256,128]{1,0:T(8,128)S(1)} %get-tuple-element.10), channel_id=1, source_target_pairs={{0,4},{8,12},{4,0},{12,8},{1,5},{9,13},{5,1},{13,9},{2,6},{10,14},... | collective-permute-start | bytes 393224 | tf_op jit(solution)/shard_map/ppermute | solution.py:564
  12.2 0.7 %collective-permute-start.1 = (f32[256,128]{1,0:T(8,128)S(1)}, f32[256,128]{1,0:T(8,128)S(1)}, u32[]{:S(2)}, u32[]{:S(2)}) collective-permute-start(f32[256,128]{1,0:T(8,128)S(1)} %get-tuple-element.11), channel_id=1, source_target_pairs={{4,8},{8,4},{5,9},{9,5},{6,10},{10,6},{7,11},{11,7},{20,24},{24,20... | collective-permute-start | bytes 393224 | tf_op jit(solution)/shard_map/ppermute | solution.py:565
  12.9 0.0 copy-start.5
  12.9 0.0 copy-start.4
  12.9 1.5 %collective-permute-start.2 = (f32[16,128]{1,0:T(8,128)S(1)}, f32[16,128]{1,0:T(8,128)S(1)}, u32[]{:S(2)}, u32[]{:S(2)}) collective-permute-start(f32[16,128]{1,0:T(8,128)S(1)} %get-tuple-element.13.own_ref), channel_id=1, source_target_pairs={{0,2},{2,0},{1,3},{3,1},{4,6},{6,4},{5,7},{7,5},{8,10},{10,8},{9,1... | collective-permute-start | bytes 24584 | tf_op jit(solution)/shard_map/ppermute | solution.py:568
  14.4 2.2 %collective-permute-done.2.west_ref.east_ref.after_ref = f32[16,128]{1,0:T(8,128)S(1)} collective-permute-done((f32[16,128]{1,0:T(8,128)S(1)}, f32[16,128]{1,0:T(8,128)S(1)}, u32[]{:S(2)}, u32[]{:S(2)}) %collective-permute-start.2) | collective-permute-done | bytes 8224 | tf_op jit(solution)/shard_map/ppermute | solution.py:568
  16.6 6.0 %all-to-all-done.recv_ref = f32[8,88,128]{2,1,0:T(8,128)S(1)} async-done(((f32[8,88,128]{2,1,0:T(8,128)}), f32[8,88,128]{2,1,0:T(8,128)S(1)}, u32[]{:S(2)}, u32[]{:S(2)}) %all-to-all-start) | async-done | bytes 360480 | tf_op jit(solution)/shard_map/all_to_all | solution.py:561
  22.6 0.0 copy-done.2
  22.6 0.0 copy-done.5
  22.6 0.0 copy-done.4
  22.6 0.0 copy-start
  22.6 0.0 copy-start.1
  22.6 0.0 copy-start.3
  22.7 0.6 %shard_map.88.mine_ref = f32[16,1152]{1,0:T(8,128)S(1)} custom-call(f32[8,88,128]{2,1,0:T(8,128)S(1)} %all-to-all-done.recv_ref, s32[4,128]{1,0:T(4,128)S(1)} %copy-done.4, s32[4,128]{1,0:T(4,128)S(1)} %copy-done.5, f32[31,640]{1,0:T(8,128)S(1)} %copy-done.2, f32[1,640]{1,0:T(1,128)S(1)} %get-tuple-element.14.active_ref, ...), custom_call_target="tpu_custom_call" | custom-call | tf_op jit(solution)/shard_map/pallas_call | solution.py:570
  23.3 0.1 collective-permute-start.3
  23.3 0.0 collective-permute-done.even_ref
  23.4 0.0 collective-permute-done.1.odd_ref
  23.4 0.2 copy-done
  23.5 0.1 copy-done.1
  23.6 0.0 copy-done.3
  23.6 0.7 %shard_map.87.adv_ref = f32[256,128]{1,0:T(8,128)S(1)} custom-call(f32[256,128]{1,0:T(8,128)S(1)} %bitcast.5, f32[256,128]{1,0:T(8,128)S(1)} %bitcast.7, f32[128,128]{1,0:T(8,128)S(1)} %bitcast.9, f32[256,128]{1,0:T(8,128)S(1)} %collective-permute-done.even_ref, f32[256,128]{1,0:T(8,128)S(1)} %collective-permute-done.1.odd_ref, ...), custom_call_target="tpu_custom_call" | custom-call | tf_op jit(solution)/shard_map/pallas_call | solution.py:581
  24.3 0.3 %collective-permute-done.3.other_ref = f32[16,1152]{1,0:T(8,128)S(1)} collective-permute-done((f32[16,1152]{1,0:T(8,128)S(1)}, f32[16,1152]{1,0:T(8,128)S(1)}, u32[]{:S(2)}, u32[]{:S(2)}) %collective-permute-start.3) | collective-permute-done | bytes 73760 | tf_op jit(solution)/shard_map/ppermute | solution.py:580
  24.6 0.9 %shard_map.89 = (f32[256,128]{1,0:T(8,128)}, f32[31,640]{1,0:T(8,128)}) custom-call(f32[256,128]{1,0:T(8,128)S(1)} %shard_map.87.adv_ref, f32[16,1152]{1,0:T(8,128)S(1)} %shard_map.88.mine_ref, f32[16,1152]{1,0:T(8,128)S(1)} %collective-permute-done.3.other_ref), custom_call_target="tpu_custom_call" | custom-call | tf_op jit(solution)/shard_map/pallas_call | solution.py:587
Async XLA Ops:
  2.8 19.8 %copy-start.2 = (f32[31,640]{1,0:T(8,128)S(1)}, f32[31,640]{1,0:T(8,128)}, u32[]{:S(2)}) copy-start(f32[31,640]{1,0:T(8,128)} %diff_ref.1) | copy-start | bytes 238084
  2.8 19.8 %all-to-all-start = ((f32[8,88,128]{2,1,0:T(8,128)}), f32[8,88,128]{2,1,0:T(8,128)S(1)}, u32[]{:S(2)}, u32[]{:S(2)}) async-start(f32[8,88,128]{2,1,0:T(8,128)} %get-tuple-element.12), calls=%async_computation | async-start | bytes 720896 | tf_op jit(solution)/shard_map/all_to_all | solution.py:561
  10.2 13.1 %collective-permute-start = (f32[256,128]{1,0:T(8,128)S(1)}, f32[256,128]{1,0:T(8,128)S(1)}, u32[]{:S(2)}, u32[]{:S(2)}) collective-permute-start(f32[256,128]{1,0:T(8,128)S(1)} %get-tuple-element.10), channel_id=1, source_target_pairs={{0,4},{8,12},{4,0},{12,8},{1,5},{9,13},{5,1},{13,9},{2,6},{10,14},... | collective-permute-start | bytes 393224 | tf_op jit(solution)/shard_map/ppermute | solution.py:564
  12.2 11.1 %collective-permute-start.1 = (f32[256,128]{1,0:T(8,128)S(1)}, f32[256,128]{1,0:T(8,128)S(1)}, u32[]{:S(2)}, u32[]{:S(2)}) collective-permute-start(f32[256,128]{1,0:T(8,128)S(1)} %get-tuple-element.11), channel_id=1, source_target_pairs={{4,8},{8,4},{5,9},{9,5},{6,10},{10,6},{7,11},{11,7},{20,24},{24,20... | collective-permute-start | bytes 393224 | tf_op jit(solution)/shard_map/ppermute | solution.py:565
  12.9 9.7 %copy-start.5 = (s32[4,128]{1,0:T(4,128)S(1)}, s32[4,128]{1,0:T(4,128)}, u32[]{:S(2)}) copy-start(s32[4,128]{1,0:T(4,128)} %slot_ref.1) | copy-start | bytes 6148
  12.9 9.7 %copy-start.4 = (s32[4,128]{1,0:T(4,128)S(1)}, s32[4,128]{1,0:T(4,128)}, u32[]{:S(2)}) copy-start(s32[4,128]{1,0:T(4,128)} %owner_ref.1) | copy-start | bytes 6148
  12.9 3.7 %collective-permute-start.2 = (f32[16,128]{1,0:T(8,128)S(1)}, f32[16,128]{1,0:T(8,128)S(1)}, u32[]{:S(2)}, u32[]{:S(2)}) collective-permute-start(f32[16,128]{1,0:T(8,128)S(1)} %get-tuple-element.13.own_ref), channel_id=1, source_target_pairs={{0,2},{2,0},{1,3},{3,1},{4,6},{6,4},{5,7},{7,5},{8,10},{10,8},{9,1... | collective-permute-start | bytes 24584 | tf_op jit(solution)/shard_map/ppermute | solution.py:568
  22.6 0.9 %copy-start = (f32[2,32,4,128]{3,2,1,0:T(4,128)S(1)}, f32[2,32,4,128]{3,2,1,0:T(4,128)}, u32[]{:S(2)}) copy-start(f32[2,32,4,128]{3,2,1,0:T(4,128)} %param.7) | copy-start | bytes 393220
  22.6 1.0 %copy-start.1 = (f32[2,32,4,128]{3,2,1,0:T(4,128)S(1)}, f32[2,32,4,128]{3,2,1,0:T(4,128)}, u32[]{:S(2)}) copy-start(f32[2,32,4,128]{3,2,1,0:T(4,128)} %param.8) | copy-start | bytes 393220
  22.6 1.0 %copy-start.3 = (f32[32,4,128]{2,1,0:T(4,128)S(1)}, f32[32,4,128]{2,1,0:T(4,128)}, u32[]{:S(2)}) copy-start(f32[32,4,128]{2,1,0:T(4,128)} %param.9) | copy-start | bytes 196612
  23.3 1.3 %collective-permute-start.3 = (f32[16,1152]{1,0:T(8,128)S(1)}, f32[16,1152]{1,0:T(8,128)S(1)}, u32[]{:S(2)}, u32[]{:S(2)}) collective-permute-start(f32[16,1152]{1,0:T(8,128)S(1)} %shard_map.88.mine_ref), channel_id=1, source_target_pairs={{0,1},{1,0},{2,3},{3,2},{4,5},{5,4},{6,7},{7,6},{8,9},{9,8},{10,11... | collective-permute-start | bytes 221192 | tf_op jit(solution)/shard_map/ppermute | solution.py:580

commit v4 on v3

--- a/solution.py
+++ b/solution.py
@@ -38,6 +38,14 @@
     ]
 
 
+def fold(count, body, start):
+    if count > 8:
+        return lax.fori_loop(0, count, body, start)
+    for index in range(count):
+        start = body(index, start)
+    return start
+
+
 def only_where(split, key, wanted):
     return split * jnp.where(key == wanted, 1.0, 0.0).astype(jnp.bfloat16)
 
@@ -48,6 +56,10 @@
             body(index)
     else:
         pl.loop(0, count)(body)
+
+
+def upwind(wind, here, ahead):
+    return jnp.maximum(wind, 0.0) * here + jnp.minimum(wind, 0.0) * ahead
 
 
 def half_levels(first, second):
@@ -159,10 +171,11 @@
     shear_ref[...] = shear
 
     copies[5].wait()
-    turned = [
-        jnp.transpose(jnp.concatenate([tracer_row(j), east_row(j), north_row(j)], axis=0))
-        for j in range(rows)
-    ]
+
+    def turn(j):
+        return jnp.transpose(jnp.concatenate([tracer_row(j), east_row(j), north_row(j)], axis=0))
+
+    turned = {j: turn(j) for j in (0, last)}
     misc = jnp.concatenate(
         [
             start_row,
@@ -203,6 +216,7 @@
 
     copies[6].wait()
     masses = jnp.transpose(jnp.concatenate([mass_row(j) for j in range(rows)], axis=0))
+    turned.update({j: turn(j) for j in range(1, last)})
     edge_rows = [[], [], [], []]
     for j in range(rows):
         west_mass = pltpu.roll(masses[0:1], (2 * levels - j * levels) % LANES, 1)
@@ -215,26 +229,34 @@
         edge_rows[3].append(jnp.where(lane_row >= 2 * levels, west_mass, turned[j][1:2]))
     edge_ref[...] = jnp.concatenate([row for group in edge_rows for row in group], axis=0)
 
-    def put_rows(ref, far, near):
-        two, lev = 2 * levels, levels
-        ref[0:two] = tracer_row(far)
-        ref[two : 2 * two] = tracer_row(near)
-        ref[2 * two : 2 * two + lev] = east_row(near)
-        ref[2 * two + lev : 2 * two + 2 * lev] = north_row(far)
-        ref[2 * two + 2 * lev : 2 * two + 3 * lev] = north_row(near)
-        ref[2 * two + 3 * lev : 2 * two + 4 * lev] = mass_row(near)
-
+    lane_level = lane_iota((levels, LANES))
+
+    def partly_advected(t, near, beyond, sign):
+        here = tr_ref[pl.ds(t * levels * rows + near, levels, stride=rows), :]
+        other = tr_ref[pl.ds(t * levels * rows + beyond, levels, stride=rows), :]
+        ahead = jnp.where(lane_level == LANES - 1, 0.0, pltpu.roll(here, LANES - 1, 1))
+        flux = upwind(east_row(near), here, ahead)
+        zonal = flux - jnp.where(lane_level == 0, 0.0, pltpu.roll(flux, 1, 1))
+        if sign > 0:
+            merid = upwind(north_row(near), here, other)
+        else:
+            merid = -upwind(north_row(beyond), other, here)
+        return here, here - mass_row(near) * (zonal + merid)
+
+    wind = north_row(last)
+    ahead_wind = jnp.maximum(wind, 0.0)
+    to_north, to_south = [], []
+    for t in range(2):
+        here, new = partly_advected(t, last, last - 1, -1)
+        to_north += [ahead_wind * here, ahead_wind * new]
+        to_south += partly_advected(t, 0, 1, 1)
+    to_north.append(jnp.where(wind < 0.0, wind, ahead_wind * mass_row(last)))
+    to_south.append(mass_row(0))
     even = lax.rem(lax.axis_index("lat"), 2) == 0
-
-    @pl.when(even)
-    def _():
-        put_rows(even_ref, last - 1, last)
-        put_rows(odd_ref, 1, 0)
-
-    @pl.when(jnp.logical_not(even))
-    def _():
-        put_rows(even_ref, 1, 0)
-        put_rows(odd_ref, last - 1, last)
+    for index, (north, south) in enumerate(zip(to_north, to_south)):
+        here = slice(index * levels, (index + 1) * levels)
+        even_ref[here] = jnp.where(even, north, south)
+        odd_ref[here] = jnp.where(even, south, north)
 
     put_diffs.wait()
     put_head.wait()
@@ -246,7 +268,7 @@
 
 def select_kernel(
     levels, rows, devices, recv_ref, owner_ref, slot_ref, diff_ref, active_ref, shear_ref,
-    after_ref, mine_ref, start_ref, arrived_ref,
+    after_ref, mine_ref,
 ):
     faces = levels - 1
     half = levels // 2
@@ -257,35 +279,34 @@
     owner = owner_ref[...]
     slot = slot_ref[...]
     span = slot // LANES
-    start_ref[...] = jnp.zeros((rows, LANES), jnp.float32)
-
-    def look_up(source):
+
+    def look_up(source, start):
         table = jnp.broadcast_to(recv_ref[source, 1:2, :], (rows, LANES))
-        start_ref[...] = jnp.where(
-            owner == source, jnp.take_along_axis(table, span, axis=1), start_ref[...]
-        )
-
-    loop_over(devices, look_up)
-    place = start_ref[...].astype(jnp.int32) + (slot - span * LANES)
+        return jnp.where(owner == source, jnp.take_along_axis(table, span, axis=1), start)
+
+    start = fold(devices, look_up, jnp.zeros((rows, LANES), jnp.float32))
+    place = start.astype(jnp.int32) + (slot - span * LANES)
     group_of = owner * rows + place // LANES
     position = place & (LANES - 1)
 
-    mine_ref[:, 0:cols] = jnp.zeros((half, cols), jnp.float32)
-
-    def gather(source):
+    def gather(source, found):
+        result = []
         for j in range(rows):
             spot = jnp.broadcast_to(position[j : j + 1], (half, LANES))
-            found = mine_ref[:, j * LANES : (j + 1) * LANES]
+            value = found[j]
             for group in range(rows):
                 held = recv_ref[source, MISC + half * (group + 1) : MISC + half * (group + 2), :]
                 taken = jnp.take_along_axis(held, spot, axis=1)
-                found = jnp.where(group_of[j : j + 1] == source * rows + group, taken, found)
-            mine_ref[:, j * LANES : (j + 1) * LANES] = found
-
-    loop_over(devices, gather)
-    mine_ref[:, 0:cols] = 0.5 * mine_ref[:, 0:cols] + source_term(shear_ref[...])
-
-    def place(slot_row, values):
+                value = jnp.where(group_of[j : j + 1] == source * rows + group, taken, value)
+            result.append(value)
+        return tuple(result)
+
+    found = fold(devices, gather, (jnp.zeros((half, LANES), jnp.float32),) * rows)
+    for j in range(rows):
+        here = slice(j * LANES, (j + 1) * LANES)
+        mine_ref[:, here] = 0.5 * found[j] + source_term(shear_ref[:, here])
+
+    def place_columns(slot_row, values):
         split = split3(values)
         masked = [only_where(split, slot_row >> 7, index) for index in range(spans)]
         hot = hot_matrix(slot_row & (LANES - 1), LANES)
@@ -300,19 +321,19 @@
         return recv_ref[source, MISC : MISC + half, :]
 
     if devices <= 8:
-        arrived_ref[...] = place(
+        arrived = place_columns(
             jnp.concatenate([slots_of(source) for source in range(devices)], axis=1),
             jnp.concatenate([shears_of(source) for source in range(devices)], axis=1),
         )
     else:
-        arrived_ref[...] = jnp.zeros((half, slot_total), jnp.float32)
-
-        @pl.loop(0, devices)
-        def _(source):
-            arrived_ref[...] += place(slots_of(source), shears_of(source))
-
+        arrived = lax.fori_loop(
+            0,
+            devices,
+            lambda source, total: total + place_columns(slots_of(source), shears_of(source)),
+            jnp.zeros((half, slot_total), jnp.float32),
+        )
     old = half_levels(diff_ref[0:half], diff_ref[faces - half :])
-    new = 0.5 * old + source_term(arrived_ref[...])
+    new = 0.5 * old + source_term(arrived)
     mine_ref[:, cols:] = jnp.where(active_ref[...] > 0.0, new, old)
 
 
@@ -324,10 +345,6 @@
     lat, lon = lax.axis_index("lat"), lax.axis_index("lon")
     first, final = lat == 0, lat == lat_count - 1
     lane_row = lane_iota((1, LANES))
-
-    def block(lat_index, lon_index):
-        return lat_index * lon_count + lon_index
-
     west_lon = lax.rem(lon + lon_count - 1, lon_count)
     east_lon = lax.rem(lon + 1, lon_count)
     south_lat = jnp.maximum(lat - 1, 0)
@@ -337,16 +354,13 @@
         return ref[group * rows : (group + 1) * rows, :]
 
     def corner(lat_index, lon_index, row):
-        return recv_ref[block(lat_index, lon_index), row : row + 1, :]
+        return recv_ref[lat_index * lon_count + lon_index, row : row + 1, :]
 
     def east_of(row):
         return jnp.where(lane_row < lev, pltpu.roll(row, 2 * lev, 1), pltpu.roll(row, 3 * lev, 1))
 
     def north_of(row):
         return jnp.where(lane_row < lev, pltpu.roll(row, lev, 1), pltpu.roll(row, 2 * lev, 1))
-
-    def upwind(wind, here, ahead):
-        return jnp.maximum(wind, 0.0) * here + jnp.minimum(wind, 0.0) * ahead
 
     def beside(column, west_east, west_value, here_east, east_value, mass):
         fluxes = upwind(north_of(column[: rows + 1]), column[: rows + 1], column[1:])
@@ -359,80 +373,86 @@
 
     far_west, far_east = edge(west_ref, 0), edge(east_ref, 3)
     own_first, own_last = edge(own_ref, 2), edge(own_ref, 1)
-    west = jnp.concatenate(
-        [corner(south_lat, west_lon, 2), edge(west_ref, 1), corner(north_lat, west_lon, 4)], axis=0
-    )
-    east = jnp.concatenate(
-        [corner(south_lat, east_lon, 3), edge(east_ref, 2), corner(north_lat, east_lon, 5)], axis=0
-    )
-    west_mid, east_mid = west[1 : rows + 1], east[1 : rows + 1]
+    west_mid, east_mid = edge(west_ref, 1), edge(east_ref, 2)
+    south_west, south_east = corner(south_lat, west_lon, 2), corner(south_lat, east_lon, 3)
+    north_west, north_east = corner(north_lat, west_lon, 4), corner(north_lat, east_lon, 5)
     west_new = beside(
-        west, east_of(far_west), far_west, east_of(west_mid), own_first, north_of(far_west)
+        jnp.concatenate([south_west, west_mid, north_west], axis=0),
+        east_of(far_west), far_west, east_of(west_mid), own_first, north_of(far_west),
     )
     east_new = beside(
-        east, east_of(own_last), own_last, east_of(east_mid), far_east, east_of(far_east)
-    )
-    filler = jnp.zeros((LANES - 2 * (rows + 2) - 2 * rows, LANES), jnp.float32)
-    turned = jnp.transpose(jnp.concatenate([west, east, west_new, east_new, filler], axis=0))
+        jnp.concatenate([south_east, east_mid, north_east], axis=0),
+        east_of(own_last), own_last, east_of(east_mid), far_east, east_of(far_east),
+    )
+
+    def end_fluxes(lat_index, row, west_cell, east_cell):
+        own_end, own_start = corner(lat_index, lon, row), corner(lat_index, lon, row + 1)
+        return [
+            upwind(east_of(west_cell), west_cell, own_start),
+            jnp.minimum(east_of(own_end), 0.0) * east_cell,
+        ]
+
+    ends = end_fluxes(south_lat, 2, south_west, south_east)
+    ends += end_fluxes(north_lat, 4, north_west, north_east)
+    used = [west_mid, east_mid, west_new, east_new] + ends
+    filler = jnp.zeros((LANES - 4 * rows - 4, LANES), jnp.float32)
+    turned = jnp.transpose(jnp.concatenate(used + [filler], axis=0))
 
     def column(index, start, size):
         return jnp.broadcast_to(turned[start : start + size, index : index + 1], (size, LANES))
 
-    def place(value, lane, index, start, size):
-        return jnp.where(lane_row == lane, column(index, start, size), value)
+    def put(value, lane, index, start):
+        return jnp.where(lane_row == lane, column(index, start, lev), value)
 
     even = lax.rem(lat, 2) == 0
 
-    def low(start, size):
-        return jnp.where(even, odd_ref[start : start + size], even_ref[start : start + size])
-
-    def high(start, size):
-        return jnp.where(even, even_ref[start : start + size], odd_ref[start : start + size])
-
-    tracer = {-2: low(0, two), -1: low(two, two)}
-    east_wind = {-1: low(2 * two, lev)}
-    north_wind = {-2: low(2 * two + lev, lev), -1: low(2 * two + 2 * lev, lev)}
-    mass = {-1: low(2 * two + 3 * lev, lev)}
-    for j in range(rows):
-        tracer[j] = tr_ref[pl.ds(j, two, stride=rows), :]
-        east_wind[j] = wind_ref[pl.ds(j, lev, stride=rows), :]
-        north_wind[j] = wind_ref[pl.ds(levels * rows + j, lev, stride=rows), :]
-        mass[j] = mass_ref[pl.ds(j, lev, stride=rows), :]
-    tracer[rows], tracer[rows + 1] = high(two, two), high(0, two)
-    east_wind[rows] = high(2 * two, lev)
-    north_wind[rows] = high(2 * two + 2 * lev, lev)
-    mass[rows] = high(2 * two + 3 * lev, lev)
-
-    west_wind = {
-        j: place(pltpu.roll(east_wind[j], 1, 1), 0, j + 1, two, lev) for j in range(-1, rows + 1)
-    }
-
-    def substep(field, row_range, west_index, east_index, start):
-        fluxes = {}
-        for j in range(row_range[0] - 1, row_range[-1] + 1):
-            flux = upwind(north_wind[j], field[j], field[j + 1])
-            if j == -1:
-                flux = jnp.where(first, 0.0, flux)
-            if j == rows - 1:
-                flux = jnp.where(final, 0.0, flux)
-            fluxes[j] = flux
-        result = {}
-        for j in row_range:
+    def low(index):
+        here = slice(index * lev, (index + 1) * lev)
+        return jnp.where(even, odd_ref[here], even_ref[here])
+
+    def high(index):
+        here = slice(index * lev, (index + 1) * lev)
+        return jnp.where(even, even_ref[here], odd_ref[here])
+
+    east_wind = [wind_ref[pl.ds(j, lev, stride=rows), :] for j in range(rows)]
+    north_wind = [wind_ref[pl.ds(lev * rows + j, lev, stride=rows), :] for j in range(rows)]
+    mass = [mass_ref[pl.ds(j, lev, stride=rows), :] for j in range(rows)]
+    west_wind = [put(pltpu.roll(east_wind[j], 1, 1), 0, j, two) for j in range(rows)]
+    low_wind, low_share = jnp.minimum(low(4), 0.0), jnp.maximum(low(4), 0.0)
+    high_mass = high(4)
+
+    def substep(field, west_index, east_index, start, low_flux, high_flux):
+        fluxes = [jnp.where(first, 0.0, low_flux)]
+        for j in range(rows - 1):
+            fluxes.append(upwind(north_wind[j], field[j], field[j + 1]))
+        fluxes.append(jnp.where(final, 0.0, high_flux))
+        result = []
+        for j in range(rows):
             here = field[j]
-            ahead = place(pltpu.roll(here, LANES - 1, 1), LANES - 1, east_index(j), start, lev)
-            behind = place(pltpu.roll(here, 1, 1), 0, west_index(j), start, lev)
+            ahead = put(pltpu.roll(here, LANES - 1, 1), LANES - 1, east_index + j, start)
+            behind = put(pltpu.roll(here, 1, 1), 0, west_index + j, start)
             zonal = upwind(east_wind[j], here, ahead) - upwind(west_wind[j], behind, here)
-            result[j] = here - mass[j] * (zonal + fluxes[j] - fluxes[j - 1])
+            result.append(here - mass[j] * (zonal + fluxes[j + 1] - fluxes[j]))
         return result
 
     for t in range(2):
         start = t * lev
-        field = {j: value[start : start + lev] for j, value in tracer.items()}
-        once = substep(
-            field, range(-1, rows + 1), lambda j: j + 1, lambda j: rows + 2 + j + 1, start
-        )
-        base = 2 * (rows + 2)
-        twice = substep(once, range(rows), lambda j: base + j, lambda j: base + rows + j, start)
+
+        def left_out(index):
+            zero = jnp.zeros((lev, LANES), jnp.float32)
+            return put(put(zero, 0, index, start) * -1.0, LANES - 1, index + 1, start)
+
+        field = [tr_ref[pl.ds(t * lev * rows + j, lev, stride=rows), :] for j in range(rows)]
+        low_flux = low(2 * t) + low_wind * field[0]
+        high_flux = upwind(north_wind[rows - 1], field[rows - 1], high(2 * t))
+        once = substep(field, 0, rows, start, low_flux, high_flux)
+        low_new = low(2 * t + 1) - low_share * (low_flux + left_out(4 * rows))
+        high_new = high(2 * t + 1) - high_mass * (left_out(4 * rows + 2) - high_flux)
+        twice = substep(
+            once, 2 * rows, 3 * rows, start,
+            low_new + low_wind * once[0],
+            upwind(north_wind[rows - 1], once[rows - 1], high_new),
+        )
         for j in range(rows):
             out_ref[pl.ds(t * rows + j, lev, stride=2 * rows), :] = twice[j]
 
@@ -533,8 +553,8 @@
         functools.partial(pack_kernel, levels, rows, devices),
         [
             (devices, block_rows, LANES),
-            (8 * levels, LANES),
-            (8 * levels, LANES),
+            (5 * levels, LANES),
+            (5 * levels, LANES),
             (half, rows * LANES),
             (4 * rows, LANES),
             (1, slot_total),
@@ -572,10 +592,6 @@
         [(half, rows * LANES + slot_total)],
         [vmem] * 6 + [pl.BlockSpec(memory_space=pl.ANY)],
         [vmem],
-        [
-            pltpu.VMEM((rows, LANES), jnp.float32),
-            pltpu.VMEM((half, slot_total), jnp.float32),
-        ],
     )(recv, span_owner, span_slot, diffusivity, active, shear, west_edges)
     other = lax.ppermute(mine, "lev", [(0, 1), (1, 0)])
     (advected,) = call(

time: 25.8 us -> 25.2 us (0.977)
  waiting for transfers between devices: 8.48 us -> 7.91 us
    ppermute x1, waiting for transfers between devices: 2.19 us -> 0.99 us  [on_device(): west_edges = lax.ppermute(edges, 'lon', to_east)]
    all_to_all x1, waiting for transfers between devices: 5.98 us -> 6.61 us  [on_device(): lax.all_to_all(send, ('lat', 'lon'), split_axis=0, concat_axis=0, tiled=T...]
    ppermute x1, starting transfers between devices: 2.02 us -> 1.46 us  [on_device(): lax.ppermute(to_even, 'lat', even_pairs + [(b, a) for a, b in even_pairs])]
    ppermute x1, starting transfers between devices: 1.53 us -> 2.02 us  [on_device(): west_edges = lax.ppermute(edges, 'lon', to_east)]
where the time goes in v4:
time: 25.2 us; the launch traced here: 24.9 us
  starting transfers between devices  11.7 us (46%)
  waiting for transfers between devices  7.91 us (31%)
  Pallas kernels  4.25 us (17%)
  between operations  0.72 us (3%)
  local copies, waits for them, and re-layouts  0.3 us (1%)
    all_to_all x1, starting transfers between devices, on_device(): lax.all_to_all(send, ('lat', 'lon'), split_axis=0, concat_axis=0, tiled=T...  7.4 us
    all_to_all x1, waiting for transfers between devices, on_device(): lax.all_to_all(send, ('lat', 'lon'), split_axis=0, concat_axis=0, tiled=T...  6.61 us
    pallas_call x1, Pallas kernels, on_device(): call(functools.partial(pack_kernel, levels, rows, devices), [(devices, bl...  2.14 us
    ppermute x1, starting transfers between devices, on_device(): west_edges = lax.ppermute(edges, 'lon', to_east)  2.02 us
    ppermute x1, starting transfers between devices, on_device(): lax.ppermute(to_even, 'lat', even_pairs + [(b, a) for a, b in even_pairs])  1.46 us
    ppermute x1, waiting for transfers between devices, on_device(): west_edges = lax.ppermute(edges, 'lon', to_east)  0.99 us
    pallas_call x1, Pallas kernels, on_device(): call(functools.partial(solve_kernel, levels, rows), [(own_count * levels...  0.89 us
    ppermute x1, starting transfers between devices, on_device(): lax.ppermute(to_odd, 'lat', odd_pairs + [(b, a) for a, b in odd_pairs])  0.79 us
  transfers between devices with their start and end apart: 5, of which 3 were waited for; matrix products, arithmetic and copies ran while one was open for 0% of the time, Pallas kernels for 5%

profile of v4, /device:TPU:0, one launch (start us, length us, event | category | flops | bytes accessed | tf_op | source)
XLA Modules:
  0.0 24.9 jit_solution(11138094944031684343)
XLA Ops:
  0.6 2.1 %shard_map.86 = (f32[8,88,128]{2,1,0:T(8,128)}, f32[160,128]{1,0:T(8,128)S(1)}, f32[160,128]{1,0:T(8,128)S(1)}, f32[16,512]{1,0:T(8,128)S(1)}, f32[16,128]{1,0:T(8,128)S(1)}, /*index=5*/f32[1,640]{1,0:T(1,128)S(1)}) custom-call(f32[256,128]{1,0:T(8,128)} %bitcast.4, f32[256,128]{1,0:T(8,128)} %bitcast.6, f32[128,128]{1,0:T(8,128)} %bitcast.8, ...), custom_call_target="tpu_custom_call" | custom-call | tf_op jit(solution)/shard_map/pallas_call | solution.py:552
  2.8 0.0 copy-start.2
  2.8 7.4 %all-to-all-start = ((f32[8,88,128]{2,1,0:T(8,128)}), f32[8,88,128]{2,1,0:T(8,128)S(1)}, u32[]{:S(2)}, u32[]{:S(2)}) async-start(f32[8,88,128]{2,1,0:T(8,128)} %get-tuple-element.12), calls=%async_computation | async-start | bytes 720896 | tf_op jit(solution)/shard_map/all_to_all | solution.py:581
  10.2 2.0 %collective-permute-start.2 = (f32[16,128]{1,0:T(8,128)S(1)}, f32[16,128]{1,0:T(8,128)S(1)}, u32[]{:S(2)}, u32[]{:S(2)}) collective-permute-start(f32[16,128]{1,0:T(8,128)S(1)} %get-tuple-element.13.own_ref), channel_id=1, source_target_pairs={{0,2},{2,0},{1,3},{3,1},{4,6},{6,4},{5,7},{7,5},{8,10},{10,8},{9,1... | collective-permute-start | bytes 24584 | tf_op jit(solution)/shard_map/ppermute | solution.py:588
  12.2 1.5 %collective-permute-start = (f32[160,128]{1,0:T(8,128)S(1)}, f32[160,128]{1,0:T(8,128)S(1)}, u32[]{:S(2)}, u32[]{:S(2)}) collective-permute-start(f32[160,128]{1,0:T(8,128)S(1)} %get-tuple-element.10), channel_id=1, source_target_pairs={{0,4},{8,12},{4,0},{12,8},{1,5},{9,13},{5,1},{13,9},{2,6},{10,14},... | collective-permute-start | bytes 245768 | tf_op jit(solution)/shard_map/ppermute | solution.py:584
  13.7 0.0 copy-start.5
  13.7 0.0 copy-start.4
  13.7 0.8 %collective-permute-start.1 = (f32[160,128]{1,0:T(8,128)S(1)}, f32[160,128]{1,0:T(8,128)S(1)}, u32[]{:S(2)}, u32[]{:S(2)}) collective-permute-start(f32[160,128]{1,0:T(8,128)S(1)} %get-tuple-element.11), channel_id=1, source_target_pairs={{4,8},{8,4},{5,9},{9,5},{6,10},{10,6},{7,11},{11,7},{20,24},{24,20... | collective-permute-start | bytes 245768 | tf_op jit(solution)/shard_map/ppermute | solution.py:585
  14.5 1.0 %collective-permute-done.2.west_ref.east_ref.after_ref = f32[16,128]{1,0:T(8,128)S(1)} collective-permute-done((f32[16,128]{1,0:T(8,128)S(1)}, f32[16,128]{1,0:T(8,128)S(1)}, u32[]{:S(2)}, u32[]{:S(2)}) %collective-permute-start.2) | collective-permute-done | bytes 8224 | tf_op jit(solution)/shard_map/ppermute | solution.py:588
  15.5 6.6 %all-to-all-done.recv_ref = f32[8,88,128]{2,1,0:T(8,128)S(1)} async-done(((f32[8,88,128]{2,1,0:T(8,128)}), f32[8,88,128]{2,1,0:T(8,128)S(1)}, u32[]{:S(2)}, u32[]{:S(2)}) %all-to-all-start) | async-done | bytes 360480 | tf_op jit(solution)/shard_map/all_to_all | solution.py:581
  22.1 0.0 copy-done.2
  22.1 0.0 copy-done.5
  22.1 0.0 copy-done.4
  22.1 0.0 copy-start
  22.1 0.0 copy-start.1
  22.1 0.0 copy-start.3
  22.1 0.6 %shard_map.88.mine_ref = f32[16,1152]{1,0:T(8,128)S(1)} custom-call(f32[8,88,128]{2,1,0:T(8,128)S(1)} %all-to-all-done.recv_ref, s32[4,128]{1,0:T(4,128)S(1)} %copy-done.4, s32[4,128]{1,0:T(4,128)S(1)} %copy-done.5, f32[31,640]{1,0:T(8,128)S(1)} %copy-done.2, f32[1,640]{1,0:T(1,128)S(1)} %get-tuple-element.14.active_ref, ...), custom_call_target="tpu_custom_call" | custom-call | tf_op jit(solution)/shard_map/pallas_call | solution.py:590
  22.7 0.1 collective-permute-start.3
  22.8 0.0 collective-permute-done.even_ref
  22.8 0.0 collective-permute-done.1.odd_ref
  22.8 0.2 copy-done
  23.0 0.1 copy-done.1
  23.1 0.0 copy-done.3
  23.1 0.6 %shard_map.87.adv_ref = f32[256,128]{1,0:T(8,128)S(1)} custom-call(f32[256,128]{1,0:T(8,128)S(1)} %bitcast.5, f32[256,128]{1,0:T(8,128)S(1)} %bitcast.7, f32[128,128]{1,0:T(8,128)S(1)} %bitcast.9, f32[160,128]{1,0:T(8,128)S(1)} %collective-permute-done.even_ref, f32[160,128]{1,0:T(8,128)S(1)} %collective-permute-done.1.odd_ref, ...), custom_call_target="tpu_custom_call" | custom-call | tf_op jit(solution)/shard_map/pallas_call | solution.py:597
  23.7 0.3 %collective-permute-done.3.other_ref = f32[16,1152]{1,0:T(8,128)S(1)} collective-permute-done((f32[16,1152]{1,0:T(8,128)S(1)}, f32[16,1152]{1,0:T(8,128)S(1)}, u32[]{:S(2)}, u32[]{:S(2)}) %collective-permute-start.3) | collective-permute-done | bytes 73760 | tf_op jit(solution)/shard_map/ppermute | solution.py:596
  24.0 0.9 %shard_map.89 = (f32[256,128]{1,0:T(8,128)}, f32[31,640]{1,0:T(8,128)}) custom-call(f32[256,128]{1,0:T(8,128)S(1)} %shard_map.87.adv_ref, f32[16,1152]{1,0:T(8,128)S(1)} %shard_map.88.mine_ref, f32[16,1152]{1,0:T(8,128)S(1)} %collective-permute-done.3.other_ref), custom_call_target="tpu_custom_call" | custom-call | tf_op jit(solution)/shard_map/pallas_call | solution.py:603
Async XLA Ops:
  2.8 19.3 %copy-start.2 = (f32[31,640]{1,0:T(8,128)S(1)}, f32[31,640]{1,0:T(8,128)}, u32[]{:S(2)}) copy-start(f32[31,640]{1,0:T(8,128)} %diff_ref.1) | copy-start | bytes 238084
  2.8 19.3 %all-to-all-start = ((f32[8,88,128]{2,1,0:T(8,128)}), f32[8,88,128]{2,1,0:T(8,128)S(1)}, u32[]{:S(2)}, u32[]{:S(2)}) async-start(f32[8,88,128]{2,1,0:T(8,128)} %get-tuple-element.12), calls=%async_computation | async-start | bytes 720896 | tf_op jit(solution)/shard_map/all_to_all | solution.py:581
  10.2 5.3 %collective-permute-start.2 = (f32[16,128]{1,0:T(8,128)S(1)}, f32[16,128]{1,0:T(8,128)S(1)}, u32[]{:S(2)}, u32[]{:S(2)}) collective-permute-start(f32[16,128]{1,0:T(8,128)S(1)} %get-tuple-element.13.own_ref), channel_id=1, source_target_pairs={{0,2},{2,0},{1,3},{3,1},{4,6},{6,4},{5,7},{7,5},{8,10},{10,8},{9,1... | collective-permute-start | bytes 24584 | tf_op jit(solution)/shard_map/ppermute | solution.py:588
  12.2 10.6 %collective-permute-start = (f32[160,128]{1,0:T(8,128)S(1)}, f32[160,128]{1,0:T(8,128)S(1)}, u32[]{:S(2)}, u32[]{:S(2)}) collective-permute-start(f32[160,128]{1,0:T(8,128)S(1)} %get-tuple-element.10), channel_id=1, source_target_pairs={{0,4},{8,12},{4,0},{12,8},{1,5},{9,13},{5,1},{13,9},{2,6},{10,14},... | collective-permute-start | bytes 245768 | tf_op jit(solution)/shard_map/ppermute | solution.py:584
  13.7 8.4 %copy-start.5 = (s32[4,128]{1,0:T(4,128)S(1)}, s32[4,128]{1,0:T(4,128)}, u32[]{:S(2)}) copy-start(s32[4,128]{1,0:T(4,128)} %slot_ref.1) | copy-start | bytes 6148
  13.7 8.4 %copy-start.4 = (s32[4,128]{1,0:T(4,128)S(1)}, s32[4,128]{1,0:T(4,128)}, u32[]{:S(2)}) copy-start(s32[4,128]{1,0:T(4,128)} %owner_ref.1) | copy-start | bytes 6148
  13.7 9.1 %collective-permute-start.1 = (f32[160,128]{1,0:T(8,128)S(1)}, f32[160,128]{1,0:T(8,128)S(1)}, u32[]{:S(2)}, u32[]{:S(2)}) collective-permute-start(f32[160,128]{1,0:T(8,128)S(1)} %get-tuple-element.11), channel_id=1, source_target_pairs={{4,8},{8,4},{5,9},{9,5},{6,10},{10,6},{7,11},{11,7},{20,24},{24,20... | collective-permute-start | bytes 245768 | tf_op jit(solution)/shard_map/ppermute | solution.py:585
  22.1 0.9 %copy-start = (f32[2,32,4,128]{3,2,1,0:T(4,128)S(1)}, f32[2,32,4,128]{3,2,1,0:T(4,128)}, u32[]{:S(2)}) copy-start(f32[2,32,4,128]{3,2,1,0:T(4,128)} %param.7) | copy-start | bytes 393220
  22.1 1.0 %copy-start.1 = (f32[2,32,4,128]{3,2,1,0:T(4,128)S(1)}, f32[2,32,4,128]{3,2,1,0:T(4,128)}, u32[]{:S(2)}) copy-start(f32[2,32,4,128]{3,2,1,0:T(4,128)} %param.8) | copy-start | bytes 393220
  22.1 1.0 %copy-start.3 = (f32[32,4,128]{2,1,0:T(4,128)S(1)}, f32[32,4,128]{2,1,0:T(4,128)}, u32[]{:S(2)}) copy-start(f32[32,4,128]{2,1,0:T(4,128)} %param.9) | copy-start | bytes 196612
  22.7 1.3 %collective-permute-start.3 = (f32[16,1152]{1,0:T(8,128)S(1)}, f32[16,1152]{1,0:T(8,128)S(1)}, u32[]{:S(2)}, u32[]{:S(2)}) collective-permute-start(f32[16,1152]{1,0:T(8,128)S(1)} %shard_map.88.mine_ref), channel_id=1, source_target_pairs={{0,1},{1,0},{2,3},{3,2},{4,5},{5,4},{6,7},{7,6},{8,9},{9,8},{10,11... | collective-permute-start | bytes 221192 | tf_op jit(solution)/shard_map/ppermute | solution.py:596

commit v5 on v4

--- a/solution.py
+++ b/solution.py
@@ -8,7 +8,6 @@
 from jax.sharding import PartitionSpec as P
 
 LANES = 128
-MISC = 8
 VMEM_LIMIT = 48 * 1024 * 1024
 NT = (((1,), (1,)), ((), ()))
 
@@ -66,19 +65,29 @@
     return jnp.where(lax.axis_index("lev") == 0, first, second)
 
 
+def own_faces(values):
+    middle = values.shape[0] // 2
+    second = jnp.concatenate([values[middle + 1 :], values[middle : middle + 1]], axis=0)
+    return half_levels(values[: middle + 1], second)
+
+
 def pack_kernel(
     levels, rows, devices, tr_hbm, wind_hbm, mass_hbm, owner_hbm, slot_hbm, diff_hbm, count_hbm,
-    send_hbm, even_ref, odd_ref, shear_ref, edge_ref, active_ref,
-    tr_ref, wind_ref, mass_ref, owner_ref, slot_ref, diff_ref, count_ref, send_ref, sems,
+    send_hbm, even_ref, odd_ref, shear_ref, edge_ref, active_ref, asked_ref, rank_ref,
+    owner_ref, old_ref, tr_ref, wind_ref, mass_ref,
+    slot_ref, diff_ref, count_ref, part_ref, send_ref, sems,
 ):
-    faces = levels - 1
     half = levels // 2
     spans = diff_ref.shape[1] // LANES
     last = rows - 1
-    head = MISC + half
+    part = part_ref.shape[1]
+    offset = pl.multiple_of(lax.axis_index("lev") * (levels * rows - part), 8)
     pairs = [
-        (owner_hbm, owner_ref), (slot_hbm, slot_ref), (count_hbm, count_ref), (diff_hbm, diff_ref),
-        (wind_hbm, wind_ref), (tr_hbm, tr_ref), (mass_hbm, mass_ref),
+        (owner_hbm, owner_ref), (slot_hbm, slot_ref),
+        (wind_hbm.at[pl.ds(offset, part)], part_ref.at[0]),
+        (wind_hbm.at[pl.ds(levels * rows + offset, part)], part_ref.at[1]),
+        (count_hbm, count_ref), (diff_hbm, diff_ref),
+        (tr_hbm, tr_ref), (wind_hbm, wind_ref), (mass_hbm, mass_ref),
     ]
     copies = [
         pltpu.make_async_copy(source, target, sems.at[index])
@@ -116,41 +125,63 @@
         ranks.append(jnp.sum(jnp.where(owned[j], count + before, 0.0), axis=0, keepdims=True))
         before = before + count[:, LANES - 1 :]
     rank = jnp.concatenate(ranks, axis=1).astype(jnp.int32)
+    for j in range(rows):
+        rank_ref[j : j + 1, :] = rank[:, j * LANES : (j + 1) * LANES]
     owner = jnp.concatenate([owner_ref[j : j + 1, :] for j in range(rows)], axis=1)
     copies[1].wait()
     slots = jnp.concatenate([slot_ref[j : j + 1, :] for j in range(rows)], axis=1)
 
     copies[2].wait()
     copies[3].wait()
-    diffs = half_levels(diff_ref[0:half], diff_ref[faces - half :])
+    held = part // rows
+    shears = []
+    for j in range(rows):
+        east = part_ref[0, pl.ds(j, held, stride=rows), :]
+        north = part_ref[1, pl.ds(j, held, stride=rows), :]
+        east_step = east[1:] - east[:-1]
+        north_step = north[1:] - north[:-1]
+        shear = east_step * east_step + north_step * north_step
+        second = jnp.concatenate([shear[2 : half + 1], shear[1:2]], axis=0)
+        shears.append(half_levels(shear[:half], second))
+    shear = jnp.concatenate(shears, axis=1)
+    shear_ref[...] = shear
+
+    extra = jnp.concatenate(
+        [slots.astype(jnp.float32) + 1.0, jnp.zeros((7, rows * LANES), jnp.float32)], axis=0
+    )
+    split = split3(jnp.concatenate([shear, extra], axis=0))
+    hot = hot_matrix(rank, LANES)
     lane_half = lane_iota((half, LANES))
     lane_row = lane_iota((1, LANES))
+    middle = lax.broadcasted_iota(jnp.int32, (half, LANES), 0) == half - 1
+    in_half = half_levels(lane_half, LANES - 1 - lane_half) < LANES // 2
+    kept = jnp.logical_or(jnp.logical_not(middle), in_half)
+
+    def fill(dest, grouped):
+        slot_row = grouped[half : half + 1] - 1.0
+        send_ref[dest, 0:half] = jnp.where(kept, grouped[:half], 0.0)
+        send_ref[dest, 2 * half - 1 : 2 * half] = slot_row
+        asked_ref[pl.ds(dest, 1), :] = slot_row.astype(jnp.int32)
+
+    copies[4].wait()
+    copies[5].wait()
+    diffs = own_faces(diff_ref[...])
+    old_ref[...] = diffs
     starts, start = [], 0
     for span in range(spans):
         starts.append(start)
         start = start + count_ref[span]
-    for group in range(rows):
-        if group < last:
-            value = jnp.zeros((half, LANES), jnp.float32)
-            for span in range(spans - 1):
-                spot = lane_half + (group * LANES - starts[span])
-                taken = jnp.take_along_axis(
-                    diffs[:, span * LANES : (span + 1) * LANES], spot & (LANES - 1), axis=1
-                )
-                value = jnp.where((spot >= 0) & (spot < count_ref[span]), taken, value)
-        else:
-            value = diffs[:, (spans - 1) * LANES :]
-
-        def store(dest):
-            send_ref[dest, head + half * group : head + half * (group + 1)] = value
-
-        loop_over(devices, store)
-    put_diffs = pltpu.make_async_copy(
-        send_ref.at[:, pl.ds(head, half * rows)],
-        send_hbm.at[:, pl.ds(head, half * rows)],
-        sems.at[len(pairs)],
-    )
-    put_diffs.start()
+    packed = []
+    for group in range(last):
+        value = jnp.zeros((half, LANES), jnp.float32)
+        for span in range(spans - 1):
+            spot = lane_half + (group * LANES - starts[span])
+            taken = jnp.take_along_axis(
+                diffs[:, span * LANES : (span + 1) * LANES], spot & (LANES - 1), axis=1
+            )
+            value = jnp.where((spot >= 0) & (spot < count_ref[span]), taken, value)
+        packed.append(value)
+    packed.append(diffs[:, (spans - 1) * LANES :])
     start_row = jnp.zeros((1, LANES), jnp.float32)
     for span in range(spans):
         here = lax.convert_element_type(starts[span], jnp.float32)
@@ -158,47 +189,28 @@
         active_ref[:, span * LANES : (span + 1) * LANES] = jnp.where(
             lane_row < count_ref[span], 1.0, 0.0
         )
-
-    copies[4].wait()
-    shears = []
-    for j in range(rows):
-        east, north = east_row(j), north_row(j)
-        east_step = east[1:] - east[:-1]
-        north_step = north[1:] - north[:-1]
-        shear = east_step * east_step + north_step * north_step
-        shears.append(half_levels(shear[:half], shear[faces - half :]))
-    shear = jnp.concatenate(shears, axis=1)
-    shear_ref[...] = shear
-
-    copies[5].wait()
-
-    def turn(j):
-        return jnp.transpose(jnp.concatenate([tracer_row(j), east_row(j), north_row(j)], axis=0))
-
-    turned = {j: turn(j) for j in (0, last)}
-    misc = jnp.concatenate(
-        [
-            start_row,
-            turned[last][LANES - 1 :],
-            turned[last][0:1],
-            turned[0][LANES - 1 :],
-            turned[0][0:1],
-            jnp.zeros((2, LANES), jnp.float32),
-        ],
-        axis=0,
-    )
-
-    extra = jnp.concatenate(
-        [slots.astype(jnp.float32) + 1.0, jnp.zeros((7, rows * LANES), jnp.float32)], axis=0
-    )
-    split = split3(jnp.concatenate([shear, extra], axis=0))
-    hot = hot_matrix(rank, LANES)
-
-    def fill(dest, grouped):
-        send_ref[dest, 0:1] = grouped[half : half + 1] - 1.0
-        send_ref[dest, 1:MISC] = misc
-        send_ref[dest, MISC:head] = grouped[:half]
-
+    last_rows = [packed[0][half - 1 :], start_row]
+    for group in range(rows // 2):
+        last_rows.append(
+            half_levels(packed[group][half - 1 :], packed[group + rows // 2][half - 1 :])
+        )
+    chunks = [
+        jnp.where(middle, last_row, value) for value, last_row in zip(packed, last_rows)
+    ]
+
+    def store(dest):
+        for group, chunk in enumerate(chunks):
+            send_ref[dest, half * (group + 1) : half * (group + 2)] = chunk
+
+    def put(start, size, sem):
+        copy = pltpu.make_async_copy(
+            send_ref.at[:, pl.ds(start, size)], send_hbm.at[:, pl.ds(start, size)], sems.at[sem]
+        )
+        copy.start()
+        return copy
+
+    loop_over(devices, store)
+    put_tail = put(2 * half, half * (rows - 1), len(pairs))
     if devices <= 8:
         masked = [only_where(split, owner, dest) for dest in range(devices)]
         for dest, grouped in enumerate(
@@ -209,14 +221,33 @@
         pl.loop(0, devices)(
             lambda dest: fill(dest, pick_columns(only_where(split, owner, dest), hot, half + 8)[0])
         )
-    put_head = pltpu.make_async_copy(
-        send_ref.at[:, pl.ds(0, head)], send_hbm.at[:, pl.ds(0, head)], sems.at[len(pairs) + 1]
-    )
-    put_head.start()
+    put_head = put(0, 2 * half, len(pairs) + 1)
 
     copies[6].wait()
+    copies[7].wait()
+    turned = [
+        jnp.transpose(jnp.concatenate([tracer_row(j), east_row(j), north_row(j)], axis=0))
+        for j in range(rows)
+    ]
+    corners = jnp.concatenate(
+        [
+            turned[last][LANES - 1 :],
+            turned[last][0:1],
+            turned[0][LANES - 1 :],
+            turned[0][0:1],
+            jnp.zeros((4, LANES), jnp.float32),
+        ],
+        axis=0,
+    )
+    corner_at = half * (rows + 1)
+
+    def add_corners(dest):
+        send_ref[dest, corner_at : corner_at + 8] = corners
+
+    loop_over(devices, add_corners)
+    put_corners = put(corner_at, 8, len(pairs) + 2)
+    copies[8].wait()
     masses = jnp.transpose(jnp.concatenate([mass_row(j) for j in range(rows)], axis=0))
-    turned.update({j: turn(j) for j in range(1, last)})
     edge_rows = [[], [], [], []]
     for j in range(rows):
         west_mass = pltpu.roll(masses[0:1], (2 * levels - j * levels) % LANES, 1)
@@ -258,8 +289,16 @@
         even_ref[here] = jnp.where(even, north, south)
         odd_ref[here] = jnp.where(even, south, north)
 
-    put_diffs.wait()
+    put_tail.wait()
     put_head.wait()
+    put_corners.wait()
+
+
+def from_side(lat, south, even_round, odd_round, here):
+    even = lax.rem(lat, 2) == 0
+    if south:
+        return jnp.where(even, odd_round[here], even_round[here])
+    return jnp.where(even, even_round[here], odd_round[here])
 
 
 def source_term(shear):
@@ -267,44 +306,55 @@
 
 
 def select_kernel(
-    levels, rows, devices, recv_ref, owner_ref, slot_ref, diff_ref, active_ref, shear_ref,
-    after_ref, mine_ref,
+    levels, rows, devices, recv_ref, owner_ref, rank_ref, asked_ref, old_ref, active_ref, shear_ref,
+    after_ref, mine_ref, lane_ref, group_ref, middle_ref,
 ):
-    faces = levels - 1
     half = levels // 2
-    slot_total = diff_ref.shape[1]
+    slot_total = old_ref.shape[1]
     spans = slot_total // LANES
     cols = rows * LANES
-
-    owner = owner_ref[...]
-    slot = slot_ref[...]
-    span = slot // LANES
-
-    def look_up(source, start):
-        table = jnp.broadcast_to(recv_ref[source, 1:2, :], (rows, LANES))
-        return jnp.where(owner == source, jnp.take_along_axis(table, span, axis=1), start)
-
-    start = fold(devices, look_up, jnp.zeros((rows, LANES), jnp.float32))
-    place = start.astype(jnp.int32) + (slot - span * LANES)
-    group_of = owner * rows + place // LANES
-    position = place & (LANES - 1)
+    row_index = lax.broadcasted_iota(jnp.int32, (half, 1), 0)
+    shared = row_index == half - 1
+    counts = jnp.where(shared, half_levels(1.0, 0.0), 1.0)
+
+    asked = asked_ref[...]
+    span = jnp.maximum(asked >> 7, 0)
+    start = jnp.take_along_axis(recv_ref[:, 3 * half - 1, :], span, axis=1).astype(jnp.int32)
+    place = start + (asked & (LANES - 1))
+    lane = place & (LANES - 1)
+    group = jnp.where(asked < 0, -1, place >> 7)
+    middle = jnp.zeros((devices, LANES), jnp.float32)
+    for index in range(rows // 2):
+        held = recv_ref[:, half * (index + 4) - 1, :]
+        wanted = half_levels(index, index + rows // 2)
+        middle = jnp.where(group == wanted, jnp.take_along_axis(held, lane, axis=1), middle)
+    lane_ref[...] = lane
+    group_ref[...] = group
+    middle_ref[...] = middle
 
     def gather(source, found):
-        result = []
-        for j in range(rows):
-            spot = jnp.broadcast_to(position[j : j + 1], (half, LANES))
-            value = found[j]
-            for group in range(rows):
-                held = recv_ref[source, MISC + half * (group + 1) : MISC + half * (group + 2), :]
-                taken = jnp.take_along_axis(held, spot, axis=1)
-                value = jnp.where(group_of[j : j + 1] == source * rows + group, taken, value)
-            result.append(value)
-        return tuple(result)
+        spot = jnp.broadcast_to(lane_ref[pl.ds(source, 1), :], (half, LANES))
+        kind = group_ref[pl.ds(source, 1), :]
+        value = jnp.zeros((half, LANES), jnp.float32)
+        for index in range(rows):
+            held = recv_ref[source, half * (index + 1) : half * (index + 2), :]
+            value = jnp.where(kind == index, jnp.take_along_axis(held, spot, axis=1), value)
+        value = jnp.where(shared, middle_ref[pl.ds(source, 1), :], value)
+        return tuple(
+            jnp.where(
+                owner_ref[j : j + 1, :] == source,
+                jnp.take_along_axis(
+                    value, jnp.broadcast_to(rank_ref[j : j + 1, :], (half, LANES)), axis=1
+                ),
+                found[j],
+            )
+            for j in range(rows)
+        )
 
     found = fold(devices, gather, (jnp.zeros((half, LANES), jnp.float32),) * rows)
     for j in range(rows):
         here = slice(j * LANES, (j + 1) * LANES)
-        mine_ref[:, here] = 0.5 * found[j] + source_term(shear_ref[:, here])
+        mine_ref[:, here] = 0.5 * found[j] + counts * source_term(shear_ref[:, here])
 
     def place_columns(slot_row, values):
         split = split3(values)
@@ -315,10 +365,10 @@
         )
 
     def slots_of(source):
-        return recv_ref[source, 0:1, :].astype(jnp.int32)
+        return recv_ref[source, 2 * half - 1 : 2 * half, :].astype(jnp.int32)
 
     def shears_of(source):
-        return recv_ref[source, MISC : MISC + half, :]
+        return recv_ref[source, 0:half, :]
 
     if devices <= 8:
         arrived = place_columns(
@@ -332,7 +382,7 @@
             lambda source, total: total + place_columns(slots_of(source), shears_of(source)),
             jnp.zeros((half, slot_total), jnp.float32),
         )
-    old = half_levels(diff_ref[0:half], diff_ref[faces - half :])
+    old = counts * old_ref[...]
     new = 0.5 * old + source_term(arrived)
     mine_ref[:, cols:] = jnp.where(active_ref[...] > 0.0, new, old)
 
@@ -344,17 +394,24 @@
     lev, two = levels, 2 * levels
     lat, lon = lax.axis_index("lat"), lax.axis_index("lon")
     first, final = lat == 0, lat == lat_count - 1
-    lane_row = lane_iota((1, LANES))
     west_lon = lax.rem(lon + lon_count - 1, lon_count)
     east_lon = lax.rem(lon + 1, lon_count)
     south_lat = jnp.maximum(lat - 1, 0)
     north_lat = jnp.minimum(lat + 1, lat_count - 1)
+    lane_row = lane_iota((1, LANES))
 
     def edge(ref, group):
         return ref[group * rows : (group + 1) * rows, :]
 
-    def corner(lat_index, lon_index, row):
-        return recv_ref[lat_index * lon_count + lon_index, row : row + 1, :]
+    def corner(lat_index, lon_index, row, size=1):
+        at = recv_ref.shape[1] - 8 + row
+        return recv_ref[lat_index * lon_count + lon_index, at : at + size, :]
+
+    def from_south(here):
+        return from_side(lat, True, even_ref, odd_ref, here)
+
+    def from_north(here):
+        return from_side(lat, False, even_ref, odd_ref, here)
 
     def east_of(row):
         return jnp.where(lane_row < lev, pltpu.roll(row, 2 * lev, 1), pltpu.roll(row, 3 * lev, 1))
@@ -374,8 +431,8 @@
     far_west, far_east = edge(west_ref, 0), edge(east_ref, 3)
     own_first, own_last = edge(own_ref, 2), edge(own_ref, 1)
     west_mid, east_mid = edge(west_ref, 1), edge(east_ref, 2)
-    south_west, south_east = corner(south_lat, west_lon, 2), corner(south_lat, east_lon, 3)
-    north_west, north_east = corner(north_lat, west_lon, 4), corner(north_lat, east_lon, 5)
+    south_west, south_east = corner(south_lat, west_lon, 0), corner(south_lat, east_lon, 1)
+    north_west, north_east = corner(north_lat, west_lon, 2), corner(north_lat, east_lon, 3)
     west_new = beside(
         jnp.concatenate([south_west, west_mid, north_west], axis=0),
         east_of(far_west), far_west, east_of(west_mid), own_first, north_of(far_west),
@@ -385,15 +442,16 @@
         east_of(own_last), own_last, east_of(east_mid), far_east, east_of(far_east),
     )
 
-    def end_fluxes(lat_index, row, west_cell, east_cell):
-        own_end, own_start = corner(lat_index, lon, row), corner(lat_index, lon, row + 1)
+    def end_fluxes(own_ends, west_cell, east_cell):
         return [
-            upwind(east_of(west_cell), west_cell, own_start),
-            jnp.minimum(east_of(own_end), 0.0) * east_cell,
+            upwind(east_of(west_cell), west_cell, own_ends[1:]),
+            jnp.minimum(east_of(own_ends[:1]), 0.0) * east_cell,
         ]
 
-    ends = end_fluxes(south_lat, 2, south_west, south_east)
-    ends += end_fluxes(north_lat, 4, north_west, north_east)
+    south_ends = corner(south_lat, lon, 0, 2)
+    north_ends = corner(north_lat, lon, 2, 2)
+    ends = end_fluxes(south_ends, south_west, south_east)
+    ends += end_fluxes(north_ends, north_west, north_east)
     used = [west_mid, east_mid, west_new, east_new] + ends
     filler = jnp.zeros((LANES - 4 * rows - 4, LANES), jnp.float32)
     turned = jnp.transpose(jnp.concatenate(used + [filler], axis=0))
@@ -404,15 +462,11 @@
     def put(value, lane, index, start):
         return jnp.where(lane_row == lane, column(index, start, lev), value)
 
-    even = lax.rem(lat, 2) == 0
-
     def low(index):
-        here = slice(index * lev, (index + 1) * lev)
-        return jnp.where(even, odd_ref[here], even_ref[here])
+        return from_south(slice(index * lev, (index + 1) * lev))
 
     def high(index):
-        here = slice(index * lev, (index + 1) * lev)
-        return jnp.where(even, even_ref[here], odd_ref[here])
+        return from_north(slice(index * lev, (index + 1) * lev))
 
     east_wind = [wind_ref[pl.ds(j, lev, stride=rows), :] for j in range(rows)]
     north_wind = [wind_ref[pl.ds(lev * rows + j, lev, stride=rows), :] for j in range(rows)]
@@ -460,21 +514,24 @@
 def solve_kernel(
     levels, rows, adv_ref, mine_ref, other_ref, out_hbm, diff_hbm, out_ref, diff_ref, kv_ref, sems
 ):
-    faces = levels - 1
     half = levels // 2
     cols = rows * LANES
     width = 2 * rows
     low = half_levels(mine_ref[...], other_ref[...])
     high = half_levels(other_ref[...], mine_ref[...])
-    diff_ref[0:half] = low[:, cols:]
-    diff_ref[half:] = high[1:, cols:]
+    shared = low[half - 1 :] + high[half - 1 :]
+    diff_ref[0 : half - 1] = low[: half - 1, cols:]
+    diff_ref[half - 1 : half] = shared[:, cols:]
+    diff_ref[half:] = high[: half - 1, cols:]
     put_diff = pltpu.make_async_copy(diff_ref, diff_hbm, sems.at[0])
     put_diff.start()
     for j in range(rows):
         here = slice(j * LANES, (j + 1) * LANES)
         for t in range(2):
-            kv_ref[pl.ds(t * rows + j, half, stride=width), :] = low[:, here]
-            kv_ref[pl.ds((faces - half) * width + t * rows + j, half, stride=width), :] = high[:, here]
+            at = t * rows + j
+            kv_ref[pl.ds(at, half - 1, stride=width), :] = low[: half - 1, here]
+            kv_ref[pl.ds((half - 1) * width + at, 1), :] = shared[:, here]
+            kv_ref[pl.ds(half * width + at, half - 1, stride=width), :] = high[: half - 1, here]
 
     def face(level):
         return kv_ref[level * width : (level + 1) * width]
@@ -522,13 +579,17 @@
     put_out.wait()
 
 
-def call(kernel, outs, in_specs, out_specs, scratch=()):
+def call(kernel, outs, in_specs, out_specs, scratch=(), aliases=None):
     return pl.pallas_call(
         kernel,
-        out_shape=[jax.ShapeDtypeStruct(shape, jnp.float32) for shape in outs],
+        out_shape=[
+            jax.ShapeDtypeStruct(out, jnp.float32) if isinstance(out, tuple) else out
+            for out in outs
+        ],
         in_specs=in_specs,
         out_specs=out_specs,
         scratch_shapes=list(scratch),
+        input_output_aliases=aliases or {},
         compiler_params=pltpu.CompilerParams(vmem_limit_bytes=VMEM_LIMIT),
     )
 
@@ -541,7 +602,7 @@
     devices = lat_count * lon_count
     half = levels // 2
     slot_total = diffusivity.shape[1]
-    block_rows = MISC + half * (1 + rows)
+    block_rows = half * (1 + rows) + 8
     vmem = pl.BlockSpec(memory_space=pltpu.VMEM)
     hbm = pl.BlockSpec(memory_space=pltpu.HBM)
 
@@ -549,28 +610,33 @@
     winds = face_winds.reshape(2 * levels * rows, cols)
     mass = inverse_mass.reshape(levels * rows, cols)
 
-    send, to_even, to_odd, shear, edges, active = call(
+    outs = [
+        (devices, block_rows, LANES),
+        (5 * levels, LANES),
+        (5 * levels, LANES),
+        (half, rows * LANES),
+        (4 * rows, LANES),
+        (1, slot_total),
+        jax.ShapeDtypeStruct((devices, LANES), jnp.int32),
+        jax.ShapeDtypeStruct((rows, LANES), jnp.int32),
+        jax.ShapeDtypeStruct((rows, LANES), jnp.int32),
+        (half, slot_total),
+        tr.shape,
+        winds.shape,
+        mass.shape,
+    ]
+    send, to_even, to_odd, shear, edges, active, asked, rank, owner, old, tr, winds, mass = call(
         functools.partial(pack_kernel, levels, rows, devices),
+        outs,
+        [hbm] * 7,
+        [hbm] + [vmem] * (len(outs) - 1),
         [
-            (devices, block_rows, LANES),
-            (5 * levels, LANES),
-            (5 * levels, LANES),
-            (half, rows * LANES),
-            (4 * rows, LANES),
-            (1, slot_total),
-        ],
-        [hbm] * 7,
-        [hbm] + [vmem] * 5,
-        [
-            pltpu.VMEM(tr.shape, jnp.float32),
-            pltpu.VMEM(winds.shape, jnp.float32),
-            pltpu.VMEM(mass.shape, jnp.float32),
-            pltpu.VMEM(span_owner.shape, jnp.int32),
             pltpu.VMEM(span_slot.shape, jnp.int32),
             pltpu.VMEM(diffusivity.shape, jnp.float32),
             pltpu.SMEM(span_column_count.shape, jnp.int32),
+            pltpu.VMEM((2, (half + 2) * rows, LANES), jnp.float32),
             pltpu.VMEM((devices, block_rows, LANES), jnp.float32),
-            pltpu.SemaphoreType.DMA((9,)),
+            pltpu.SemaphoreType.DMA((12,)),
         ],
     )(
         *(
@@ -579,27 +645,32 @@
         )
     )
     recv = lax.all_to_all(send, ("lat", "lon"), split_axis=0, concat_axis=0, tiled=True)
-    even_pairs = [(i, i + 1) for i in range(0, lat_count - 1, 2)]
-    odd_pairs = [(i, i + 1) for i in range(1, lat_count - 1, 2)]
-    from_even = lax.ppermute(to_even, "lat", even_pairs + [(b, a) for a, b in even_pairs])
-    from_odd = lax.ppermute(to_odd, "lat", odd_pairs + [(b, a) for a, b in odd_pairs])
+    from_lat = []
+    for first, values in enumerate((to_even, to_odd)):
+        pairs = [(i, i + 1) for i in range(first, lat_count - 1, 2)]
+        from_lat.append(lax.ppermute(values, "lat", pairs + [(b, a) for a, b in pairs]))
     to_east = [(i, (i + 1) % lon_count) for i in range(lon_count)]
     to_west = [(target, source) for source, target in to_east]
-    west_edges = lax.ppermute(edges, "lon", to_east)
-    east_edges = west_edges if lon_count == 2 else lax.ppermute(edges, "lon", to_west)
+    from_west = lax.ppermute(edges, "lon", to_east)
+    from_east = from_west if lon_count == 2 else lax.ppermute(edges, "lon", to_west)
     (mine,) = call(
         functools.partial(select_kernel, levels, rows, devices),
         [(half, rows * LANES + slot_total)],
-        [vmem] * 6 + [pl.BlockSpec(memory_space=pl.ANY)],
+        [vmem] * 7 + [pl.BlockSpec(memory_space=pl.ANY)],
         [vmem],
-    )(recv, span_owner, span_slot, diffusivity, active, shear, west_edges)
+        [
+            pltpu.VMEM((devices, LANES), jnp.int32),
+            pltpu.VMEM((devices, LANES), jnp.int32),
+            pltpu.VMEM((devices, LANES), jnp.float32),
+        ],
+    )(recv, owner, rank, asked, old, active, shear, from_west)
     other = lax.ppermute(mine, "lev", [(0, 1), (1, 0)])
     (advected,) = call(
         functools.partial(advect_kernel, levels, rows, lat_count, lon_count),
         [(levels * own_count * rows, LANES)],
         [vmem] * 9,
         [vmem],
-    )(tr, winds, mass, from_even, from_odd, recv, edges, west_edges, east_edges)
+    )(tr, winds, mass, *from_lat, recv, edges, from_west, from_east)
     out, diff_out = call(
         functools.partial(solve_kernel, levels, rows),
         [(own_count * levels * rows, cols), (levels - 1, slot_total)],

time: 25.2 us -> 24.9 us (0.988)
  waiting for transfers between devices: 7.91 us -> 8.31 us
  local copies, waits for them, and re-layouts: 0.3 us -> 0 us
    unnamed x12 -> x0, local copies, waits for them, and re-layouts: 0.3 us -> none
    ppermute x1, waiting for transfers between devices: 0.31 us -> 0.57 us  [on_device(): other = lax.ppermute(mine, 'lev', [(0, 1), (1, 0)])]
  transfers between devices with their start and end apart: 5 -> 5, of which waited for: 3 -> 3; matrix products, arithmetic and copies ran while one was open for 0% -> 0% of each run, Pallas kernels for 5% -> 4%
where the time goes in v5:
time: 24.9 us; the launch traced here: 24.6 us
  starting transfers between devices  11.5 us (46%)
  waiting for transfers between devices  8.31 us (33%)
  Pallas kernels  4.17 us (17%)
  between operations  0.69 us (3%)
    all_to_all x1, starting transfers between devices, on_device(): lax.all_to_all(send, ('lat', 'lon'), split_axis=0, concat_axis=0, tiled=T...  7.27 us
    all_to_all x1, waiting for transfers between devices, on_device(): lax.all_to_all(send, ('lat', 'lon'), split_axis=0, concat_axis=0, tiled=T...  6.61 us
    pallas_call x1, Pallas kernels, on_device(): call(functools.partial(pack_kernel, levels, rows, devices), outs, [hbm] *...  2.17 us
    ppermute x2, starting transfers between devices, on_device(): lax.ppermute(values, 'lat', pairs + [(b, a) for a, b in pairs])  2.12 us
    ppermute x1, starting transfers between devices, on_device(): from_west = lax.ppermute(edges, 'lon', to_east)  2.02 us
    ppermute x1, waiting for transfers between devices, on_device(): from_west = lax.ppermute(edges, 'lon', to_east)  1.12 us
    pallas_call x1, Pallas kernels, on_device(): call(functools.partial(solve_kernel, levels, rows), [(own_count * levels...  0.89 us
    pallas_call x1, Pallas kernels, on_device(): call(functools.partial(advect_kernel, levels, rows, lat_count, lon_count)...  0.66 us
  transfers between devices with their start and end apart: 5, of which 3 were waited for; matrix products, arithmetic and copies ran while one was open for 0% of the time, Pallas kernels for 4%

profile of v5, /device:TPU:0, one launch (start us, length us, event | category | flops | bytes accessed | tf_op | source)
XLA Modules:
  0.0 24.6 jit_solution(14721378690987076872)
XLA Ops:
  0.6 2.2 %shard_map.86 = (f32[8,88,128]{2,1,0:T(8,128)}, f32[160,128]{1,0:T(8,128)S(1)}, f32[160,128]{1,0:T(8,128)S(1)}, f32[16,512]{1,0:T(8,128)S(1)}, f32[16,128]{1,0:T...) custom-call(f32[256,128]{1,0:T(8,128)} %bitcast.4, ...), custom_call_target="tpu_custom_call" | custom-call | tf_op jit(solution)/shard_map/pallas_call | solution.py:628
  2.8 7.3 %all-to-all-start = ((f32[8,88,128]{2,1,0:T(8,128)}), f32[8,88,128]{2,1,0:T(8,128)S(1)}, u32[]{:S(2)}, u32[]{:S(2)}) async-start(f32[8,88,128]{2,1,0:T(8,128)} %get-tuple-element.22), calls=%async_computation | async-start | bytes 720896 | tf_op jit(solution)/shard_map/all_to_all | solution.py:647
  10.1 2.0 %collective-permute-start.2 = (f32[16,128]{1,0:T(8,128)S(1)}, f32[16,128]{1,0:T(8,128)S(1)}, u32[]{:S(2)}, u32[]{:S(2)}) collective-permute-start(f32[16,128]{1,0:T(8,128)S(1)} %get-tuple-element.23.own_ref), channel_id=1, source_target_pairs={{0,2},{2,0},{1,3},{3,1},{4,6},{6,4},{5,7},{7,5},{8,10},{10,8},{9,1... | collective-permute-start | bytes 24584 | tf_op jit(solution)/shard_map/ppermute | solution.py:654
  12.1 1.5 %collective-permute-start = (f32[160,128]{1,0:T(8,128)S(1)}, f32[160,128]{1,0:T(8,128)S(1)}, u32[]{:S(2)}, u32[]{:S(2)}) collective-permute-start(f32[160,128]{1,0:T(8,128)S(1)} %get-tuple-element.20), channel_id=1, source_target_pairs={{0,4},{8,12},{4,0},{12,8},{1,5},{9,13},{5,1},{13,9},{2,6},{10,14},... | collective-permute-start | bytes 245768 | tf_op jit(solution)/shard_map/ppermute | solution.py:651
  13.6 0.7 %collective-permute-start.1 = (f32[160,128]{1,0:T(8,128)S(1)}, f32[160,128]{1,0:T(8,128)S(1)}, u32[]{:S(2)}, u32[]{:S(2)}) collective-permute-start(f32[160,128]{1,0:T(8,128)S(1)} %get-tuple-element.21), channel_id=1, source_target_pairs={{4,8},{8,4},{5,9},{9,5},{6,10},{10,6},{7,11},{11,7},{20,24},{24,20... | collective-permute-start | bytes 245768 | tf_op jit(solution)/shard_map/ppermute | solution.py:651
  14.2 1.1 %collective-permute-done.2.west_ref.east_ref.after_ref = f32[16,128]{1,0:T(8,128)S(1)} collective-permute-done((f32[16,128]{1,0:T(8,128)S(1)}, f32[16,128]{1,0:T(8,128)S(1)}, u32[]{:S(2)}, u32[]{:S(2)}) %collective-permute-start.2) | collective-permute-done | bytes 8224 | tf_op jit(solution)/shard_map/ppermute | solution.py:654
  15.4 6.6 %all-to-all-done.recv_ref = f32[8,88,128]{2,1,0:T(8,128)S(1)} async-done(((f32[8,88,128]{2,1,0:T(8,128)}), f32[8,88,128]{2,1,0:T(8,128)S(1)}, u32[]{:S(2)}, u32[]{:S(2)}) %all-to-all-start) | async-done | bytes 360480 | tf_op jit(solution)/shard_map/all_to_all | solution.py:647
  22.0 0.4 %shard_map.88.mine_ref = f32[16,1152]{1,0:T(8,128)S(1)} custom-call(f32[8,88,128]{2,1,0:T(8,128)S(1)} %all-to-all-done.recv_ref, s32[4,128]{1,0:T(4,128)S(1)} %get-tuple-element.24.owner_ref, s32[4,128]{1,0:T(4,128)S(1)} %get-tuple-element.25.rank_ref, s32[8,128]{1,0:T(8,128)S(1)} %get-tuple-element.26.asked_ref, f32[16,640]{1,0:T(8,128)S(1)} %get-tuple-element.27.old_ref, ...), custom_call_target="tpu_custom_call" | custom-call | tf_op jit(solution)/shard_map/pallas_call | solution.py:656
  22.4 0.1 collective-permute-start.3
  22.5 0.0 collective-permute-done.even_ref
  22.5 0.0 collective-permute-done.1.odd_ref
  22.5 0.7 %shard_map.87.adv_ref = f32[256,128]{1,0:T(8,128)S(1)} custom-call(f32[256,128]{1,0:T(8,128)S(1)} %get-tuple-element.17.tr_ref, f32[256,128]{1,0:T(8,128)S(1)} %get-tuple-element.18.wind_ref, f32[128,128]{1,0:T(8,128)S(1)} %get-tuple-element.19.mass_ref, f32[160,128]{1,0:T(8,128)S(1)} %collective-permute-done.even_ref, ...), custom_call_target="tpu_custom_call" | custom-call | tf_op jit(solution)/shard_map/pallas_call | solution.py:668
  23.2 0.6 %collective-permute-done.3.other_ref = f32[16,1152]{1,0:T(8,128)S(1)} collective-permute-done((f32[16,1152]{1,0:T(8,128)S(1)}, f32[16,1152]{1,0:T(8,128)S(1)}, u32[]{:S(2)}, u32[]{:S(2)}) %collective-permute-start.3) | collective-permute-done | bytes 73760 | tf_op jit(solution)/shard_map/ppermute | solution.py:667
  23.7 0.9 %shard_map.89 = (f32[256,128]{1,0:T(8,128)}, f32[31,640]{1,0:T(8,128)}) custom-call(f32[256,128]{1,0:T(8,128)S(1)} %shard_map.87.adv_ref, f32[16,1152]{1,0:T(8,128)S(1)} %shard_map.88.mine_ref, f32[16,1152]{1,0:T(8,128)S(1)} %collective-permute-done.3.other_ref), custom_call_target="tpu_custom_call" | custom-call | tf_op jit(solution)/shard_map/pallas_call | solution.py:674
Async XLA Ops:
  2.8 19.1 %all-to-all-start = ((f32[8,88,128]{2,1,0:T(8,128)}), f32[8,88,128]{2,1,0:T(8,128)S(1)}, u32[]{:S(2)}, u32[]{:S(2)}) async-start(f32[8,88,128]{2,1,0:T(8,128)} %get-tuple-element.22), calls=%async_computation | async-start | bytes 720896 | tf_op jit(solution)/shard_map/all_to_all | solution.py:647
  10.1 5.3 %collective-permute-start.2 = (f32[16,128]{1,0:T(8,128)S(1)}, f32[16,128]{1,0:T(8,128)S(1)}, u32[]{:S(2)}, u32[]{:S(2)}) collective-permute-start(f32[16,128]{1,0:T(8,128)S(1)} %get-tuple-element.23.own_ref), channel_id=1, source_target_pairs={{0,2},{2,0},{1,3},{3,1},{4,6},{6,4},{5,7},{7,5},{8,10},{10,8},{9,1... | collective-permute-start | bytes 24584 | tf_op jit(solution)/shard_map/ppermute | solution.py:654
  12.1 10.4 %collective-permute-start = (f32[160,128]{1,0:T(8,128)S(1)}, f32[160,128]{1,0:T(8,128)S(1)}, u32[]{:S(2)}, u32[]{:S(2)}) collective-permute-start(f32[160,128]{1,0:T(8,128)S(1)} %get-tuple-element.20), channel_id=1, source_target_pairs={{0,4},{8,12},{4,0},{12,8},{1,5},{9,13},{5,1},{13,9},{2,6},{10,14},... | collective-permute-start | bytes 245768 | tf_op jit(solution)/shard_map/ppermute | solution.py:651
  13.6 8.9 %collective-permute-start.1 = (f32[160,128]{1,0:T(8,128)S(1)}, f32[160,128]{1,0:T(8,128)S(1)}, u32[]{:S(2)}, u32[]{:S(2)}) collective-permute-start(f32[160,128]{1,0:T(8,128)S(1)} %get-tuple-element.21), channel_id=1, source_target_pairs={{4,8},{8,4},{5,9},{9,5},{6,10},{10,6},{7,11},{11,7},{20,24},{24,20... | collective-permute-start | bytes 245768 | tf_op jit(solution)/shard_map/ppermute | solution.py:651
  22.4 1.3 %collective-permute-start.3 = (f32[16,1152]{1,0:T(8,128)S(1)}, f32[16,1152]{1,0:T(8,128)S(1)}, u32[]{:S(2)}, u32[]{:S(2)}) collective-permute-start(f32[16,1152]{1,0:T(8,128)S(1)} %shard_map.88.mine_ref), channel_id=1, source_target_pairs={{0,1},{1,0},{2,3},{3,2},{4,5},{5,4},{6,7},{7,6},{8,9},{9,8},{10,11... | collective-permute-start | bytes 221192 | tf_op jit(solution)/shard_map/ppermute | solution.py:667

commit v6 on v5

--- a/solution.py
+++ b/solution.py
@@ -71,23 +71,30 @@
     return half_levels(values[: middle + 1], second)
 
 
+def turn(levels, rows, tr_ref, wind_ref, j):
+    fields = [
+        tr_ref[pl.ds(j, 2 * levels, stride=rows), :],
+        wind_ref[pl.ds(j, levels, stride=rows), :],
+        wind_ref[pl.ds(levels * rows + j, levels, stride=rows), :],
+    ]
+    return jnp.transpose(jnp.concatenate(fields, axis=0))
+
+
 def pack_kernel(
-    levels, rows, devices, tr_hbm, wind_hbm, mass_hbm, owner_hbm, slot_hbm, diff_hbm, count_hbm,
-    send_hbm, even_ref, odd_ref, shear_ref, edge_ref, active_ref, asked_ref, rank_ref,
-    owner_ref, old_ref, tr_ref, wind_ref, mass_ref,
-    slot_ref, diff_ref, count_ref, part_ref, send_ref, sems,
+    levels, rows, devices, lon_count,
+    tr_hbm, wind_hbm, mass_hbm, owner_hbm, slot_hbm, diff_hbm, count_hbm,
+    send_hbm, shear_ref, active_ref, rank_ref, owner_ref, slot_ref, diff_ref, tr_ref, wind_ref, mass_ref,
+    count_ref, send_ref, sems,
 ):
     half = levels // 2
     spans = diff_ref.shape[1] // LANES
     last = rows - 1
-    part = part_ref.shape[1]
-    offset = pl.multiple_of(lax.axis_index("lev") * (levels * rows - part), 8)
+    lane_half = lane_iota((half, LANES))
+    lane_row = lane_iota((1, LANES))
+    bottom = lax.broadcasted_iota(jnp.int32, (half, LANES), 0) == half - 1
     pairs = [
-        (owner_hbm, owner_ref), (slot_hbm, slot_ref),
-        (wind_hbm.at[pl.ds(offset, part)], part_ref.at[0]),
-        (wind_hbm.at[pl.ds(levels * rows + offset, part)], part_ref.at[1]),
-        (count_hbm, count_ref), (diff_hbm, diff_ref),
-        (tr_hbm, tr_ref), (wind_hbm, wind_ref), (mass_hbm, mass_ref),
+        (owner_hbm, owner_ref), (slot_hbm, slot_ref), (wind_hbm, wind_ref), (count_hbm, count_ref),
+        (diff_hbm, diff_ref), (tr_hbm, tr_ref), (mass_hbm, mass_ref),
     ]
     copies = [
         pltpu.make_async_copy(source, target, sems.at[index])
@@ -96,17 +103,12 @@
     for copy in copies:
         copy.start()
 
-    def tracer_row(j):
-        return tr_ref[pl.ds(j, 2 * levels, stride=rows), :]
-
-    def east_row(j):
-        return wind_ref[pl.ds(j, levels, stride=rows), :]
-
-    def north_row(j):
-        return wind_ref[pl.ds(levels * rows + j, levels, stride=rows), :]
-
-    def mass_row(j):
-        return mass_ref[pl.ds(j, levels, stride=rows), :]
+    def put(start, size, sem):
+        copy = pltpu.make_async_copy(
+            send_ref.at[:, pl.ds(start, size)], send_hbm.at[:, pl.ds(start, size)], sems.at[sem]
+        )
+        copy.start()
+        return copy
 
     copies[0].wait()
     owner_index = lax.broadcasted_iota(jnp.int32, (devices, LANES), 0)
@@ -122,51 +124,37 @@
     ranks = []
     for j in range(rows):
         count = counted[j * devices : (j + 1) * devices]
-        ranks.append(jnp.sum(jnp.where(owned[j], count + before, 0.0), axis=0, keepdims=True))
+        rank = jnp.sum(jnp.where(owned[j], count + before, 0.0), axis=0, keepdims=True)
+        ranks.append(rank.astype(jnp.int32))
+        rank_ref[j : j + 1, :] = ranks[j]
         before = before + count[:, LANES - 1 :]
-    rank = jnp.concatenate(ranks, axis=1).astype(jnp.int32)
+    owner = jnp.concatenate([owner_ref[j : j + 1, :] for j in range(rows)] * 2, axis=1)
+
+    part = LANES // 2
+    place = jnp.concatenate(ranks, axis=1) - half_levels(0, part)
+    inside = (place >= 0) & (place < part)
+    hot = hot_matrix(
+        jnp.concatenate([jnp.where(inside, place, -1), jnp.where(inside, place + part, -1)], axis=1),
+        LANES,
+    )
+    copies[1].wait()
+    copies[2].wait()
+    lower, upper = [], []
     for j in range(rows):
-        rank_ref[j : j + 1, :] = rank[:, j * LANES : (j + 1) * LANES]
-    owner = jnp.concatenate([owner_ref[j : j + 1, :] for j in range(rows)], axis=1)
-    copies[1].wait()
-    slots = jnp.concatenate([slot_ref[j : j + 1, :] for j in range(rows)], axis=1)
-
-    copies[2].wait()
-    copies[3].wait()
-    held = part // rows
-    shears = []
-    for j in range(rows):
-        east = part_ref[0, pl.ds(j, held, stride=rows), :]
-        north = part_ref[1, pl.ds(j, held, stride=rows), :]
+        east = wind_ref[pl.ds(j, levels, stride=rows), :]
+        north = wind_ref[pl.ds(levels * rows + j, levels, stride=rows), :]
         east_step = east[1:] - east[:-1]
         north_step = north[1:] - north[:-1]
         shear = east_step * east_step + north_step * north_step
-        second = jnp.concatenate([shear[2 : half + 1], shear[1:2]], axis=0)
-        shears.append(half_levels(shear[:half], second))
-    shear = jnp.concatenate(shears, axis=1)
-    shear_ref[...] = shear
-
-    extra = jnp.concatenate(
-        [slots.astype(jnp.float32) + 1.0, jnp.zeros((7, rows * LANES), jnp.float32)], axis=0
-    )
-    split = split3(jnp.concatenate([shear, extra], axis=0))
-    hot = hot_matrix(rank, LANES)
-    lane_half = lane_iota((half, LANES))
-    lane_row = lane_iota((1, LANES))
-    middle = lax.broadcasted_iota(jnp.int32, (half, LANES), 0) == half - 1
-    in_half = half_levels(lane_half, LANES - 1 - lane_half) < LANES // 2
-    kept = jnp.logical_or(jnp.logical_not(middle), in_half)
-
-    def fill(dest, grouped):
-        slot_row = grouped[half : half + 1] - 1.0
-        send_ref[dest, 0:half] = jnp.where(kept, grouped[:half], 0.0)
-        send_ref[dest, 2 * half - 1 : 2 * half] = slot_row
-        asked_ref[pl.ds(dest, 1), :] = slot_row.astype(jnp.int32)
-
+        slot = slot_ref[j : j + 1, :].astype(jnp.float32) + 1.0
+        lower.append(shear[:half])
+        upper.append(jnp.concatenate([shear[half:], slot], axis=0))
+        shear_ref[:, j * LANES : (j + 1) * LANES] = own_faces(shear)
+    split = split3(jnp.concatenate(lower + upper, axis=1))
+
+    copies[3].wait()
     copies[4].wait()
-    copies[5].wait()
     diffs = own_faces(diff_ref[...])
-    old_ref[...] = diffs
     starts, start = [], 0
     for span in range(spans):
         starts.append(start)
@@ -185,68 +173,95 @@
     start_row = jnp.zeros((1, LANES), jnp.float32)
     for span in range(spans):
         here = lax.convert_element_type(starts[span], jnp.float32)
-        start_row = jnp.where(lane_row == span, here, start_row)
+        start_row = jnp.where(lane_row == 3 * levels + span, here, start_row)
         active_ref[:, span * LANES : (span + 1) * LANES] = jnp.where(
             lane_row < count_ref[span], 1.0, 0.0
         )
-    last_rows = [packed[0][half - 1 :], start_row]
+    chunks = packed[:2]
     for group in range(rows // 2):
-        last_rows.append(
-            half_levels(packed[group][half - 1 :], packed[group + rows // 2][half - 1 :])
-        )
-    chunks = [
-        jnp.where(middle, last_row, value) for value, last_row in zip(packed, last_rows)
-    ]
-
-    def store(dest):
-        for group, chunk in enumerate(chunks):
-            send_ref[dest, half * (group + 1) : half * (group + 2)] = chunk
-
-    def put(start, size, sem):
-        copy = pltpu.make_async_copy(
-            send_ref.at[:, pl.ds(start, size)], send_hbm.at[:, pl.ds(start, size)], sems.at[sem]
-        )
-        copy.start()
-        return copy
-
-    loop_over(devices, store)
-    put_tail = put(2 * half, half * (rows - 1), len(pairs))
+        shared = half_levels(packed[group][half - 1 :], packed[group + rows // 2][half - 1 :])
+        chunks.append(jnp.where(bottom, shared, packed[group + 2]))
+
+    def store_late(dest):
+        for group in range(2, rows):
+            send_ref[dest, half * (group + 1) : half * (group + 2)] = chunks[group]
+
+    loop_over(devices, store_late)
+    puts = [put(3 * half, half * (rows - 2), len(pairs))]
+
+    copies[5].wait()
+    ends = []
+    for j in (0, last):
+        turned = turn(levels, rows, tr_ref, wind_ref, j)
+        east_end, west_end = turned[LANES - 1 :], turned[0:1]
+        tracers = jnp.where(lane_row < part, east_end, pltpu.roll(west_end, part, 1))
+        winds = jnp.where(
+            lane_row < part,
+            pltpu.roll(east_end, part, 1),
+            jnp.where(lane_row < 3 * levels, pltpu.roll(west_end, 3 * levels, 1), start_row),
+        )
+        ends.append(
+            [jnp.where(bottom, row, chunk) for row, chunk in zip((tracers, winds), chunks)]
+        )
+
+    def store_early(dest):
+        northward = dest // lon_count > lax.axis_index("lat")
+        for group in range(2):
+            send_ref[dest, half * (group + 1) : half * (group + 2)] = jnp.where(
+                northward, ends[1][group], ends[0][group]
+            )
+
+    loop_over(devices, store_early)
+    puts.append(put(half, 2 * half, len(pairs) + 1))
+    unasked = jnp.where(bottom & (lane_half >= part), 1.0, 0.0)
+
+    def fill(dest, grouped):
+        send_ref[dest, 0:half] = grouped - unasked
+
     if devices <= 8:
         masked = [only_where(split, owner, dest) for dest in range(devices)]
-        for dest, grouped in enumerate(
-            pick_columns(jnp.concatenate(masked, axis=0), hot, half + 8)
-        ):
+        for dest, grouped in enumerate(pick_columns(jnp.concatenate(masked, axis=0), hot, half)):
             fill(dest, grouped)
     else:
         pl.loop(0, devices)(
-            lambda dest: fill(dest, pick_columns(only_where(split, owner, dest), hot, half + 8)[0])
-        )
-    put_head = put(0, 2 * half, len(pairs) + 1)
-
+            lambda dest: fill(dest, pick_columns(only_where(split, owner, dest), hot, half)[0])
+        )
+    puts.append(put(0, half, len(pairs) + 2))
     copies[6].wait()
-    copies[7].wait()
-    turned = [
-        jnp.transpose(jnp.concatenate([tracer_row(j), east_row(j), north_row(j)], axis=0))
-        for j in range(rows)
-    ]
-    corners = jnp.concatenate(
-        [
-            turned[last][LANES - 1 :],
-            turned[last][0:1],
-            turned[0][LANES - 1 :],
-            turned[0][0:1],
-            jnp.zeros((4, LANES), jnp.float32),
-        ],
-        axis=0,
-    )
-    corner_at = half * (rows + 1)
-
-    def add_corners(dest):
-        send_ref[dest, corner_at : corner_at + 8] = corners
-
-    loop_over(devices, add_corners)
-    put_corners = put(corner_at, 8, len(pairs) + 2)
-    copies[8].wait()
+    for copy in puts:
+        copy.wait()
+
+
+def halo_kernel(
+    levels, rows, devices, tr_ref, wind_ref, mass_ref, owner_ref, slot_ref, rank_ref,
+    even_ref, odd_ref, edge_ref, asked_ref,
+):
+    last = rows - 1
+
+    def flat(ref):
+        return jnp.concatenate([ref[j : j + 1, :] for j in range(rows)], axis=1)
+
+    owner, hot = flat(owner_ref), hot_matrix(flat(rank_ref), LANES)
+    filler = jnp.zeros((7, rows * LANES), jnp.float32)
+    split = split3(jnp.concatenate([flat(slot_ref).astype(jnp.float32) + 1.0, filler], axis=0))
+
+    def ask(dest):
+        (found,) = pick_columns(only_where(split, owner, dest), hot, 8)
+        asked_ref[pl.ds(dest, 1), :] = found[0:1].astype(jnp.int32) - 1
+
+    loop_over(devices, ask)
+    lane_row = lane_iota((1, LANES))
+
+    def east_row(j):
+        return wind_ref[pl.ds(j, levels, stride=rows), :]
+
+    def north_row(j):
+        return wind_ref[pl.ds(levels * rows + j, levels, stride=rows), :]
+
+    def mass_row(j):
+        return mass_ref[pl.ds(j, levels, stride=rows), :]
+
+    turned = [turn(levels, rows, tr_ref, wind_ref, j) for j in range(rows)]
     masses = jnp.transpose(jnp.concatenate([mass_row(j) for j in range(rows)], axis=0))
     edge_rows = [[], [], [], []]
     for j in range(rows):
@@ -289,9 +304,12 @@
         even_ref[here] = jnp.where(even, north, south)
         odd_ref[here] = jnp.where(even, south, north)
 
-    put_tail.wait()
-    put_head.wait()
-    put_corners.wait()
+
+def neighbour_blocks(lat_count, lon_count):
+    lat, lon = lax.axis_index("lat"), lax.axis_index("lon")
+    west, east = lax.rem(lon + lon_count - 1, lon_count), lax.rem(lon + 1, lon_count)
+    south, north = jnp.maximum(lat - 1, 0), jnp.minimum(lat + 1, lat_count - 1)
+    return [at * lon_count + index for at in (south, north) for index in (west, lon, east)]
 
 
 def from_side(lat, south, even_round, odd_round, here):
@@ -306,20 +324,21 @@
 
 
 def select_kernel(
-    levels, rows, devices, recv_ref, owner_ref, rank_ref, asked_ref, old_ref, active_ref, shear_ref,
-    after_ref, mine_ref, lane_ref, group_ref, middle_ref,
+    levels, rows, devices, recv_ref, owner_ref, rank_ref, asked_ref, shear_ref,
+    side_ref, even_ref, odd_ref, mine_ref, lane_ref, group_ref, middle_ref,
 ):
     half = levels // 2
-    slot_total = old_ref.shape[1]
+    cols = rows * LANES
+    slot_total = (mine_ref.shape[1] - cols) // 2
     spans = slot_total // LANES
-    cols = rows * LANES
     row_index = lax.broadcasted_iota(jnp.int32, (half, 1), 0)
     shared = row_index == half - 1
     counts = jnp.where(shared, half_levels(1.0, 0.0), 1.0)
 
     asked = asked_ref[...]
     span = jnp.maximum(asked >> 7, 0)
-    start = jnp.take_along_axis(recv_ref[:, 3 * half - 1, :], span, axis=1).astype(jnp.int32)
+    start = jnp.take_along_axis(recv_ref[:, 3 * half - 1, :], span + 3 * levels, axis=1)
+    start = start.astype(jnp.int32)
     place = start + (asked & (LANES - 1))
     lane = place & (LANES - 1)
     group = jnp.where(asked < 0, -1, place >> 7)
@@ -356,35 +375,38 @@
         here = slice(j * LANES, (j + 1) * LANES)
         mine_ref[:, here] = 0.5 * found[j] + counts * source_term(shear_ref[:, here])
 
-    def place_columns(slot_row, values):
+    bottom = lax.broadcasted_iota(jnp.int32, (half, LANES), 0) == half - 1
+    first_half = lane_iota((1, LANES)) < LANES // 2
+
+    def arrived(source):
+        slots = recv_ref[source, half - 1 : half, :]
+        slots = jnp.where(first_half, pltpu.roll(slots, LANES // 2, 1), slots).astype(jnp.int32)
+        shears = recv_ref[source, 0:half, :]
+        lower = jnp.where(first_half, shears, 0.0)
+        upper = jnp.where(jnp.logical_or(first_half, bottom), 0.0, shears)
+        return slots, jnp.concatenate([lower, upper], axis=0)
+
+    def place_columns(slots, values):
         split = split3(values)
-        masked = [only_where(split, slot_row >> 7, index) for index in range(spans)]
-        hot = hot_matrix(slot_row & (LANES - 1), LANES)
+        masked = [only_where(split, slots >> 7, index) for index in range(spans)]
+        hot = hot_matrix(slots & (LANES - 1), LANES)
+        placed = pick_columns(jnp.concatenate(masked, axis=0), hot, levels)
         return jnp.concatenate(
-            pick_columns(jnp.concatenate(masked, axis=0), hot, half), axis=1
-        )
-
-    def slots_of(source):
-        return recv_ref[source, 2 * half - 1 : 2 * half, :].astype(jnp.int32)
-
-    def shears_of(source):
-        return recv_ref[source, 0:half, :]
+            [value[:half] for value in placed] + [value[half:] for value in placed], axis=1
+        )
 
     if devices <= 8:
-        arrived = place_columns(
-            jnp.concatenate([slots_of(source) for source in range(devices)], axis=1),
-            jnp.concatenate([shears_of(source) for source in range(devices)], axis=1),
+        slots, values = zip(*(arrived(source) for source in range(devices)))
+        mine_ref[:, cols:] = place_columns(
+            jnp.concatenate(slots, axis=1), jnp.concatenate(values, axis=1)
         )
     else:
-        arrived = lax.fori_loop(
+        mine_ref[:, cols:] = lax.fori_loop(
             0,
             devices,
-            lambda source, total: total + place_columns(slots_of(source), shears_of(source)),
-            jnp.zeros((half, slot_total), jnp.float32),
-        )
-    old = counts * old_ref[...]
-    new = 0.5 * old + source_term(arrived)
-    mine_ref[:, cols:] = jnp.where(active_ref[...] > 0.0, new, old)
+            lambda source, total: total + place_columns(*arrived(source)),
+            jnp.zeros((half, 2 * slot_total), jnp.float32),
+        )
 
 
 def advect_kernel(
@@ -392,20 +414,21 @@
     own_ref, west_ref, east_ref, out_ref,
 ):
     lev, two = levels, 2 * levels
-    lat, lon = lax.axis_index("lat"), lax.axis_index("lon")
+    lat = lax.axis_index("lat")
     first, final = lat == 0, lat == lat_count - 1
-    west_lon = lax.rem(lon + lon_count - 1, lon_count)
-    east_lon = lax.rem(lon + 1, lon_count)
-    south_lat = jnp.maximum(lat - 1, 0)
-    north_lat = jnp.minimum(lat + 1, lat_count - 1)
     lane_row = lane_iota((1, LANES))
 
     def edge(ref, group):
         return ref[group * rows : (group + 1) * rows, :]
 
-    def corner(lat_index, lon_index, row, size=1):
-        at = recv_ref.shape[1] - 8 + row
-        return recv_ref[lat_index * lon_count + lon_index, at : at + size, :]
+    blocks = neighbour_blocks(lat_count, lon_count)
+    tracers, winds = (
+        jnp.concatenate([recv_ref[block, row : row + 1, :] for block in blocks], axis=0)
+        for row in (lev - 1, 3 * (lev // 2) - 1)
+    )
+    in_first = lane_iota((len(blocks), LANES)) < two
+    last_cells = jnp.where(in_first, tracers, pltpu.roll(winds, two, 1))
+    first_cells = jnp.where(in_first, pltpu.roll(tracers, two, 1), pltpu.roll(winds, lev, 1))
 
     def from_south(here):
         return from_side(lat, True, even_ref, odd_ref, here)
@@ -431,8 +454,8 @@
     far_west, far_east = edge(west_ref, 0), edge(east_ref, 3)
     own_first, own_last = edge(own_ref, 2), edge(own_ref, 1)
     west_mid, east_mid = edge(west_ref, 1), edge(east_ref, 2)
-    south_west, south_east = corner(south_lat, west_lon, 0), corner(south_lat, east_lon, 1)
-    north_west, north_east = corner(north_lat, west_lon, 2), corner(north_lat, east_lon, 3)
+    south_west, south_east = last_cells[0:1], first_cells[2:3]
+    north_west, north_east = last_cells[3:4], first_cells[5:6]
     west_new = beside(
         jnp.concatenate([south_west, west_mid, north_west], axis=0),
         east_of(far_west), far_west, east_of(west_mid), own_first, north_of(far_west),
@@ -442,16 +465,14 @@
         east_of(own_last), own_last, east_of(east_mid), far_east, east_of(far_east),
     )
 
-    def end_fluxes(own_ends, west_cell, east_cell):
+    def end_fluxes(index, west_cell, east_cell):
+        own_end, own_start = last_cells[index : index + 1], first_cells[index : index + 1]
         return [
-            upwind(east_of(west_cell), west_cell, own_ends[1:]),
-            jnp.minimum(east_of(own_ends[:1]), 0.0) * east_cell,
+            upwind(east_of(west_cell), west_cell, own_start),
+            jnp.minimum(east_of(own_end), 0.0) * east_cell,
         ]
 
-    south_ends = corner(south_lat, lon, 0, 2)
-    north_ends = corner(north_lat, lon, 2, 2)
-    ends = end_fluxes(south_ends, south_west, south_east)
-    ends += end_fluxes(north_ends, north_west, north_east)
+    ends = end_fluxes(1, south_west, south_east) + end_fluxes(4, north_west, north_east)
     used = [west_mid, east_mid, west_new, east_new] + ends
     filler = jnp.zeros((LANES - 4 * rows - 4, LANES), jnp.float32)
     turned = jnp.transpose(jnp.concatenate(used + [filler], axis=0))
@@ -512,19 +533,28 @@
 
 
 def solve_kernel(
-    levels, rows, adv_ref, mine_ref, other_ref, out_hbm, diff_hbm, out_ref, diff_ref, kv_ref, sems
+    levels, rows, adv_ref, mine_ref, other_ref, old_ref, active_ref, out_hbm, diff_hbm,
+    out_ref, diff_ref, kv_ref, sems,
 ):
     half = levels // 2
     cols = rows * LANES
     width = 2 * rows
-    low = half_levels(mine_ref[...], other_ref[...])
-    high = half_levels(other_ref[...], mine_ref[...])
-    shared = low[half - 1 :] + high[half - 1 :]
-    diff_ref[0 : half - 1] = low[: half - 1, cols:]
-    diff_ref[half - 1 : half] = shared[:, cols:]
-    diff_ref[half:] = high[: half - 1, cols:]
+    slot_total = old_ref.shape[1]
+    active = active_ref[...] > 0.0
+    shear = mine_ref[:, cols:] + other_ref[:, cols:]
+
+    def update(start, size, shear):
+        old = old_ref[start : start + size]
+        new = 0.5 * old + source_term(shear)
+        diff_ref[start : start + size] = jnp.where(active, new, old)
+
+    update(0, half, shear[:, :slot_total])
+    update(half, half - 1, shear[: half - 1, slot_total:])
     put_diff = pltpu.make_async_copy(diff_ref, diff_hbm, sems.at[0])
     put_diff.start()
+    low = half_levels(mine_ref[:, :cols], other_ref[:, :cols])
+    high = half_levels(other_ref[:, :cols], mine_ref[:, :cols])
+    shared = low[half - 1 :] + high[half - 1 :]
     for j in range(rows):
         here = slice(j * LANES, (j + 1) * LANES)
         for t in range(2):
@@ -602,7 +632,7 @@
     devices = lat_count * lon_count
     half = levels // 2
     slot_total = diffusivity.shape[1]
-    block_rows = half * (1 + rows) + 8
+    block_rows = half * (1 + rows)
     vmem = pl.BlockSpec(memory_space=pltpu.VMEM)
     hbm = pl.BlockSpec(memory_space=pltpu.HBM)
 
@@ -612,31 +642,25 @@
 
     outs = [
         (devices, block_rows, LANES),
-        (5 * levels, LANES),
-        (5 * levels, LANES),
         (half, rows * LANES),
-        (4 * rows, LANES),
         (1, slot_total),
-        jax.ShapeDtypeStruct((devices, LANES), jnp.int32),
         jax.ShapeDtypeStruct((rows, LANES), jnp.int32),
         jax.ShapeDtypeStruct((rows, LANES), jnp.int32),
-        (half, slot_total),
+        jax.ShapeDtypeStruct((rows, LANES), jnp.int32),
+        diffusivity.shape,
         tr.shape,
         winds.shape,
         mass.shape,
     ]
-    send, to_even, to_odd, shear, edges, active, asked, rank, owner, old, tr, winds, mass = call(
-        functools.partial(pack_kernel, levels, rows, devices),
+    send, shear, active, rank, owner, slot, old, tr, winds, mass = call(
+        functools.partial(pack_kernel, levels, rows, devices, lon_count),
         outs,
         [hbm] * 7,
         [hbm] + [vmem] * (len(outs) - 1),
         [
-            pltpu.VMEM(span_slot.shape, jnp.int32),
-            pltpu.VMEM(diffusivity.shape, jnp.float32),
             pltpu.SMEM(span_column_count.shape, jnp.int32),
-            pltpu.VMEM((2, (half + 2) * rows, LANES), jnp.float32),
             pltpu.VMEM((devices, block_rows, LANES), jnp.float32),
-            pltpu.SemaphoreType.DMA((12,)),
+            pltpu.SemaphoreType.DMA((10,)),
         ],
     )(
         *(
@@ -645,6 +669,17 @@
         )
     )
     recv = lax.all_to_all(send, ("lat", "lon"), split_axis=0, concat_axis=0, tiled=True)
+    to_even, to_odd, edges, asked = call(
+        functools.partial(halo_kernel, levels, rows, devices),
+        [
+            (5 * levels, LANES),
+            (5 * levels, LANES),
+            (4 * rows, LANES),
+            jax.ShapeDtypeStruct((devices, LANES), jnp.int32),
+        ],
+        [vmem] * 6,
+        [vmem] * 4,
+    )(tr, winds, mass, owner, slot, rank)
     from_lat = []
     for first, values in enumerate((to_even, to_odd)):
         pairs = [(i, i + 1) for i in range(first, lat_count - 1, 2)]
@@ -655,15 +690,15 @@
     from_east = from_west if lon_count == 2 else lax.ppermute(edges, "lon", to_west)
     (mine,) = call(
         functools.partial(select_kernel, levels, rows, devices),
-        [(half, rows * LANES + slot_total)],
-        [vmem] * 7 + [pl.BlockSpec(memory_space=pl.ANY)],
+        [(half, rows * LANES + 2 * slot_total)],
+        [vmem] * 5 + [pl.BlockSpec(memory_space=pl.ANY)] * 3,
         [vmem],
         [
             pltpu.VMEM((devices, LANES), jnp.int32),
             pltpu.VMEM((devices, LANES), jnp.int32),
             pltpu.VMEM((devices, LANES), jnp.float32),
         ],
-    )(recv, owner, rank, asked, old, active, shear, from_west)
+    )(recv, owner, rank, asked, shear, from_west, *from_lat)
     other = lax.ppermute(mine, "lev", [(0, 1), (1, 0)])
     (advected,) = call(
         functools.partial(advect_kernel, levels, rows, lat_count, lon_count),
@@ -674,7 +709,7 @@
     out, diff_out = call(
         functools.partial(solve_kernel, levels, rows),
         [(own_count * levels * rows, cols), (levels - 1, slot_total)],
-        [vmem] * 3,
+        [vmem] * 5,
         [hbm] * 2,
         [
             pltpu.VMEM((own_count * levels * rows, cols), jnp.float32),
@@ -682,7 +717,7 @@
             pltpu.VMEM((levels * 2 * rows, LANES), jnp.float32),
             pltpu.SemaphoreType.DMA((2,)),
         ],
-    )(advected, mine, other)
+    )(advected, mine, other, old, active)
     return out.reshape(own_count, levels, rows, cols), diff_out
 
 

time: 24.9 us -> 24.5 us (0.984)
  waiting for transfers between devices: 8.31 us -> 7.01 us
  Pallas kernels: 4.17 us -> 4.99 us
    all_to_all x1, waiting for transfers between devices: 6.61 us -> 3.14 us  [on_device(): lax.all_to_all(send, ('lat', 'lon'), split_axis=0, concat_axis=0, tiled=T...]
    ppermute x2, waiting for transfers between devices: 0.01 us -> 1.11 us  [on_device(): lax.ppermute(values, 'lat', pairs + [(b, a) for a, b in pairs])]
    ppermute x1, waiting for transfers between devices: 1.12 us -> 2.2 us  [on_device(): from_west = lax.ppermute(edges, 'lon', to_east)]
    pallas_call x1 -> x2, Pallas kernels: 2.17 us -> 2.82 us  [the longest x1 2.37 us: on_device(): call(functools.partial(pack_kernel, levels, rows, devices, lon_count), ou...]
    ppermute x2, starting transfers between devices: 2.12 us -> 2.74 us  [on_device(): lax.ppermute(values, 'lat', pairs + [(b, a) for a, b in pairs])]
    ppermute x1, starting transfers between devices: 2.02 us -> 1.53 us  [on_device(): from_west = lax.ppermute(edges, 'lon', to_east)]
  transfers between devices with their start and end apart: 5 -> 5, of which waited for: 3 -> 4; matrix products, arithmetic and copies ran while one was open for 0% -> 0% of each run, Pallas kernels for 4% -> 5%
where the time goes in v6:
time: 24.5 us; the launch traced here: 24.3 us
  starting transfers between devices  11.6 us (47%)
  waiting for transfers between devices  7.01 us (29%)
  Pallas kernels  4.99 us (20%)
  between operations  0.69 us (3%)
    all_to_all x1, starting transfers between devices, on_device(): lax.all_to_all(send, ('lat', 'lon'), split_axis=0, concat_axis=0, tiled=T...  7.26 us
    all_to_all x1, waiting for transfers between devices, on_device(): lax.all_to_all(send, ('lat', 'lon'), split_axis=0, concat_axis=0, tiled=T...  3.14 us
    ppermute x2, starting transfers between devices, on_device(): lax.ppermute(values, 'lat', pairs + [(b, a) for a, b in pairs])  2.74 us
    pallas_call x1, Pallas kernels, on_device(): call(functools.partial(pack_kernel, levels, rows, devices, lon_count), ou...  2.37 us
    ppermute x1, waiting for transfers between devices, on_device(): from_west = lax.ppermute(edges, 'lon', to_east)  2.2 us
    ppermute x1, starting transfers between devices, on_device(): from_west = lax.ppermute(edges, 'lon', to_east)  1.53 us
    ppermute x2, waiting for transfers between devices, on_device(): lax.ppermute(values, 'lat', pairs + [(b, a) for a, b in pairs])  1.11 us
    pallas_call x1, Pallas kernels, on_device(): call(functools.partial(solve_kernel, levels, rows), [(own_count * levels...  0.91 us
  transfers between devices with their start and end apart: 5, of which 4 were waited for; matrix products, arithmetic and copies ran while one was open for 0% of the time, Pallas kernels for 5%

profile of v6, /device:TPU:0, one launch (start us, length us, event | category | flops | bytes accessed | tf_op | source)
XLA Modules:
  0.0 24.3 jit_solution(9115081026789442960)
XLA Ops:
  0.6 2.4 %shard_map.86 = (f32[8,80,128]{2,1,0:T(8,128)}, f32[16,512]{1,0:T(8,128)S(1)}, f32[1,640]{1,0:T(1,128)S(1)}, s32[4,128]{1,0:T(4,128)S(1)}, s32[4,128]{1,0:T(4,12...) custom-call(f32[256,128]{1,0:T(8,128)} %bitcast.4, ...), custom_call_target="tpu_custom_call" | custom-call | tf_op jit(solution)/shard_map/pallas_call | solution.py:655
  3.0 7.3 %all-to-all-start = ((f32[8,80,128]{2,1,0:T(8,128)}), f32[8,80,128]{2,1,0:T(8,128)S(1)}, u32[]{:S(2)}, u32[]{:S(2)}) async-start(f32[8,80,128]{2,1,0:T(8,128)} %get-tuple-element.26), calls=%async_computation | async-start | bytes 655360 | tf_op jit(solution)/shard_map/all_to_all | solution.py:671
  10.3 0.4 %shard_map.87 = (f32[160,128]{1,0:T(8,128)S(1)}, f32[160,128]{1,0:T(8,128)S(1)}, f32[16,128]{1,0:T(8,128)S(1)}, s32[8,128]{1,0:T(8,128)S(1)}) custom-call(f32[256,128]{1,0:T(8,128)S(1)} %get-tuple-element.18.tr_ref, f32[256,128]{1,0:T(8,128)S(1)} %get-tuple-element.19.wind_ref, f32[128,128]{1,0:T(8,128)S(1)} %get-tuple-element.20.mass_ref, ...), custom_call_target="tpu_custom_call" | custom-call | tf_op jit(solution)/shard_map/pallas_call | solution.py:672
  10.7 2.1 %collective-permute-start = (f32[160,128]{1,0:T(8,128)S(1)}, f32[160,128]{1,0:T(8,128)S(1)}, u32[]{:S(2)}, u32[]{:S(2)}) collective-permute-start(f32[160,128]{1,0:T(8,128)S(1)} %get-tuple-element.24), channel_id=1, source_target_pairs={{0,4},{8,12},{4,0},{12,8},{1,5},{9,13},{5,1},{13,9},{2,6},{10,14},... | collective-permute-start | bytes 245768 | tf_op jit(solution)/shard_map/ppermute | solution.py:686
  12.8 0.7 %collective-permute-start.1 = (f32[160,128]{1,0:T(8,128)S(1)}, f32[160,128]{1,0:T(8,128)S(1)}, u32[]{:S(2)}, u32[]{:S(2)}) collective-permute-start(f32[160,128]{1,0:T(8,128)S(1)} %get-tuple-element.25), channel_id=1, source_target_pairs={{4,8},{8,4},{5,9},{9,5},{6,10},{10,6},{7,11},{11,7},{20,24},{24,20... | collective-permute-start | bytes 245768 | tf_op jit(solution)/shard_map/ppermute | solution.py:686
  13.5 1.5 %collective-permute-start.2 = (f32[16,128]{1,0:T(8,128)S(1)}, f32[16,128]{1,0:T(8,128)S(1)}, u32[]{:S(2)}, u32[]{:S(2)}) collective-permute-start(f32[16,128]{1,0:T(8,128)S(1)} %get-tuple-element.27.own_ref), channel_id=1, source_target_pairs={{0,2},{2,0},{1,3},{3,1},{4,6},{6,4},{5,7},{7,5},{8,10},{10,8},{9,1... | collective-permute-start | bytes 24584 | tf_op jit(solution)/shard_map/ppermute | solution.py:689
  15.0 2.2 %collective-permute-done.2.west_ref.east_ref.side_ref = f32[16,128]{1,0:T(8,128)S(1)} collective-permute-done((f32[16,128]{1,0:T(8,128)S(1)}, f32[16,128]{1,0:T(8,128)S(1)}, u32[]{:S(2)}, u32[]{:S(2)}) %collective-permute-start.2) | collective-permute-done | bytes 8224 | tf_op jit(solution)/shard_map/ppermute | solution.py:689
  17.2 1.1 %collective-permute-done.even_ref = f32[160,128]{1,0:T(8,128)S(1)} collective-permute-done((f32[160,128]{1,0:T(8,128)S(1)}, f32[160,128]{1,0:T(8,128)S(1)}, u32[]{:S(2)}, u32[]{:S(2)}) %collective-permute-start) | collective-permute-done | bytes 81952 | tf_op jit(solution)/shard_map/ppermute | solution.py:686
  18.3 0.0 collective-permute-done.1.odd_ref
  18.3 3.1 %all-to-all-done.recv_ref = f32[8,80,128]{2,1,0:T(8,128)S(1)} async-done(((f32[8,80,128]{2,1,0:T(8,128)}), f32[8,80,128]{2,1,0:T(8,128)S(1)}, u32[]{:S(2)}, u32[]{:S(2)}) %all-to-all-start) | async-done | bytes 327712 | tf_op jit(solution)/shard_map/all_to_all | solution.py:671
  21.5 0.5 %shard_map.89.mine_ref = f32[16,1792]{1,0:T(8,128)S(1)} custom-call(f32[8,80,128]{2,1,0:T(8,128)S(1)} %all-to-all-done.recv_ref, s32[4,128]{1,0:T(4,128)S(1)} %get-tuple-element.21.owner_ref, s32[4,128]{1,0:T(4,128)S(1)} %get-tuple-element.23.rank_ref, s32[8,128]{1,0:T(8,128)S(1)} %get-tuple-element.28.asked_ref, f32[16,512]{1,0:T(8,128)S(1)} %get-tuple-element.29.shear_ref, ...), custom_call_target="tpu_custom_call" | custom-call | tf_op jit(solution)/shard_map/pallas_call | solution.py:691
  22.0 0.1 collective-permute-start.3
  22.1 0.8 %shard_map.88.adv_ref = f32[256,128]{1,0:T(8,128)S(1)} custom-call(f32[256,128]{1,0:T(8,128)S(1)} %get-tuple-element.18.tr_ref, f32[256,128]{1,0:T(8,128)S(1)} %get-tuple-element.19.wind_ref, f32[128,128]{1,0:T(8,128)S(1)} %get-tuple-element.20.mass_ref, f32[160,128]{1,0:T(8,128)S(1)} %collective-permute-done.even_ref, ...), custom_call_target="tpu_custom_call" | custom-call | tf_op jit(solution)/shard_map/pallas_call | solution.py:703
  22.8 0.6 %collective-permute-done.3.other_ref = f32[16,1792]{1,0:T(8,128)S(1)} collective-permute-done((f32[16,1792]{1,0:T(8,128)S(1)}, f32[16,1792]{1,0:T(8,128)S(1)}, u32[]{:S(2)}, u32[]{:S(2)}) %collective-permute-start.3) | collective-permute-done | bytes 114720 | tf_op jit(solution)/shard_map/ppermute | solution.py:702
  23.4 0.9 %shard_map.90 = (f32[256,128]{1,0:T(8,128)}, f32[31,640]{1,0:T(8,128)}) custom-call(f32[256,128]{1,0:T(8,128)S(1)} %shard_map.88.adv_ref, f32[16,1792]{1,0:T(8,128)S(1)} %shard_map.89.mine_ref, f32[16,1792]{1,0:T(8,128)S(1)} %collective-permute-done.3.other_ref, f32[31,640]{1,0:T(8,128)S(1)} %get-tuple-element.30.old_ref, ...), custom_call_target="tpu_custom_call" | custom-call | tf_op jit(solution)/shard_map/pallas_call | solution.py:709
Async XLA Ops:
  3.0 18.5 %all-to-all-start = ((f32[8,80,128]{2,1,0:T(8,128)}), f32[8,80,128]{2,1,0:T(8,128)S(1)}, u32[]{:S(2)}, u32[]{:S(2)}) async-start(f32[8,80,128]{2,1,0:T(8,128)} %get-tuple-element.26), calls=%async_computation | async-start | bytes 655360 | tf_op jit(solution)/shard_map/all_to_all | solution.py:671
  10.7 7.6 %collective-permute-start = (f32[160,128]{1,0:T(8,128)S(1)}, f32[160,128]{1,0:T(8,128)S(1)}, u32[]{:S(2)}, u32[]{:S(2)}) collective-permute-start(f32[160,128]{1,0:T(8,128)S(1)} %get-tuple-element.24), channel_id=1, source_target_pairs={{0,4},{8,12},{4,0},{12,8},{1,5},{9,13},{5,1},{13,9},{2,6},{10,14},... | collective-permute-start | bytes 245768 | tf_op jit(solution)/shard_map/ppermute | solution.py:686
  12.8 5.5 %collective-permute-start.1 = (f32[160,128]{1,0:T(8,128)S(1)}, f32[160,128]{1,0:T(8,128)S(1)}, u32[]{:S(2)}, u32[]{:S(2)}) collective-permute-start(f32[160,128]{1,0:T(8,128)S(1)} %get-tuple-element.25), channel_id=1, source_target_pairs={{4,8},{8,4},{5,9},{9,5},{6,10},{10,6},{7,11},{11,7},{20,24},{24,20... | collective-permute-start | bytes 245768 | tf_op jit(solution)/shard_map/ppermute | solution.py:686
  13.5 3.7 %collective-permute-start.2 = (f32[16,128]{1,0:T(8,128)S(1)}, f32[16,128]{1,0:T(8,128)S(1)}, u32[]{:S(2)}, u32[]{:S(2)}) collective-permute-start(f32[16,128]{1,0:T(8,128)S(1)} %get-tuple-element.27.own_ref), channel_id=1, source_target_pairs={{0,2},{2,0},{1,3},{3,1},{4,6},{6,4},{5,7},{7,5},{8,10},{10,8},{9,1... | collective-permute-start | bytes 24584 | tf_op jit(solution)/shard_map/ppermute | solution.py:689
  22.0 1.4 %collective-permute-start.3 = (f32[16,1792]{1,0:T(8,128)S(1)}, f32[16,1792]{1,0:T(8,128)S(1)}, u32[]{:S(2)}, u32[]{:S(2)}) collective-permute-start(f32[16,1792]{1,0:T(8,128)S(1)} %shard_map.89.mine_ref), channel_id=1, source_target_pairs={{0,1},{1,0},{2,3},{3,2},{4,5},{5,4},{6,7},{7,6},{8,9},{9,8},{10,11... | collective-permute-start | bytes 344072 | tf_op jit(solution)/shard_map/ppermute | solution.py:702

commit v7 on v6

--- a/solution.py
+++ b/solution.py
@@ -8,8 +8,19 @@
 from jax.sharding import PartitionSpec as P
 
 LANES = 128
+ORDERS = {8: (4, 6, 1, 0, 7, 5, 2, 3)}
 VMEM_LIMIT = 48 * 1024 * 1024
 NT = (((1,), (1,)), ((), ()))
+
+
+def device_of(devices, block):
+    return ORDERS[devices][block] if devices in ORDERS else block
+
+
+def block_of(devices, device):
+    if devices not in ORDERS:
+        return device
+    return sum(jnp.where(device == held, block, 0) for block, held in enumerate(ORDERS[devices]))
 
 
 def lane_iota(shape):
@@ -137,8 +148,8 @@
         jnp.concatenate([jnp.where(inside, place, -1), jnp.where(inside, place + part, -1)], axis=1),
         LANES,
     )
-    copies[1].wait()
-    copies[2].wait()
+    for index in range(1, 6):
+        copies[index].wait()
     lower, upper = [], []
     for j in range(rows):
         east = wind_ref[pl.ds(j, levels, stride=rows), :]
@@ -152,8 +163,6 @@
         shear_ref[:, j * LANES : (j + 1) * LANES] = own_faces(shear)
     split = split3(jnp.concatenate(lower + upper, axis=1))
 
-    copies[3].wait()
-    copies[4].wait()
     diffs = own_faces(diff_ref[...])
     starts, start = [], 0
     for span in range(spans):
@@ -189,7 +198,6 @@
     loop_over(devices, store_late)
     puts = [put(3 * half, half * (rows - 2), len(pairs))]
 
-    copies[5].wait()
     ends = []
     for j in (0, last):
         turned = turn(levels, rows, tr_ref, wind_ref, j)
@@ -205,7 +213,7 @@
         )
 
     def store_early(dest):
-        northward = dest // lon_count > lax.axis_index("lat")
+        northward = device_of(devices, dest) // lon_count > lax.axis_index("lat")
         for group in range(2):
             send_ref[dest, half * (group + 1) : half * (group + 2)] = jnp.where(
                 northward, ends[1][group], ends[0][group]
@@ -219,12 +227,14 @@
         send_ref[dest, 0:half] = grouped - unasked
 
     if devices <= 8:
-        masked = [only_where(split, owner, dest) for dest in range(devices)]
+        masked = [only_where(split, owner, device_of(devices, dest)) for dest in range(devices)]
         for dest, grouped in enumerate(pick_columns(jnp.concatenate(masked, axis=0), hot, half)):
             fill(dest, grouped)
     else:
         pl.loop(0, devices)(
-            lambda dest: fill(dest, pick_columns(only_where(split, owner, dest), hot, half)[0])
+            lambda dest: fill(
+                dest, pick_columns(only_where(split, owner, device_of(devices, dest)), hot, half)[0]
+            )
         )
     puts.append(put(0, half, len(pairs) + 2))
     copies[6].wait()
@@ -246,7 +256,7 @@
     split = split3(jnp.concatenate([flat(slot_ref).astype(jnp.float32) + 1.0, filler], axis=0))
 
     def ask(dest):
-        (found,) = pick_columns(only_where(split, owner, dest), hot, 8)
+        (found,) = pick_columns(only_where(split, owner, device_of(devices, dest)), hot, 8)
         asked_ref[pl.ds(dest, 1), :] = found[0:1].astype(jnp.int32) - 1
 
     loop_over(devices, ask)
@@ -309,7 +319,11 @@
     lat, lon = lax.axis_index("lat"), lax.axis_index("lon")
     west, east = lax.rem(lon + lon_count - 1, lon_count), lax.rem(lon + 1, lon_count)
     south, north = jnp.maximum(lat - 1, 0), jnp.minimum(lat + 1, lat_count - 1)
-    return [at * lon_count + index for at in (south, north) for index in (west, lon, east)]
+    return [
+        block_of(lat_count * lon_count, at * lon_count + index)
+        for at in (south, north)
+        for index in (west, lon, east)
+    ]
 
 
 def from_side(lat, south, even_round, odd_round, here):
@@ -361,7 +375,7 @@
         value = jnp.where(shared, middle_ref[pl.ds(source, 1), :], value)
         return tuple(
             jnp.where(
-                owner_ref[j : j + 1, :] == source,
+                owner_ref[j : j + 1, :] == device_of(devices, source),
                 jnp.take_along_axis(
                     value, jnp.broadcast_to(rank_ref[j : j + 1, :], (half, LANES)), axis=1
                 ),
@@ -378,13 +392,12 @@
     bottom = lax.broadcasted_iota(jnp.int32, (half, LANES), 0) == half - 1
     first_half = lane_iota((1, LANES)) < LANES // 2
 
-    def arrived(source):
-        slots = recv_ref[source, half - 1 : half, :]
-        slots = jnp.where(first_half, pltpu.roll(slots, LANES // 2, 1), slots).astype(jnp.int32)
-        shears = recv_ref[source, 0:half, :]
-        lower = jnp.where(first_half, shears, 0.0)
-        upper = jnp.where(jnp.logical_or(first_half, bottom), 0.0, shears)
-        return slots, jnp.concatenate([lower, upper], axis=0)
+    def arrived(pair):
+        left, right = (recv_ref[2 * pair + index, 0:half, :] for index in range(2))
+        lower = jnp.where(first_half, left, pltpu.roll(right, LANES // 2, 1))
+        upper = jnp.where(first_half, pltpu.roll(left, LANES // 2, 1), right)
+        slots = upper[half - 1 :].astype(jnp.int32)
+        return slots, jnp.concatenate([lower, jnp.where(bottom, 0.0, upper)], axis=0)
 
     def place_columns(slots, values):
         split = split3(values)
@@ -396,15 +409,15 @@
         )
 
     if devices <= 8:
-        slots, values = zip(*(arrived(source) for source in range(devices)))
+        slots, values = zip(*(arrived(pair) for pair in range(devices // 2)))
         mine_ref[:, cols:] = place_columns(
             jnp.concatenate(slots, axis=1), jnp.concatenate(values, axis=1)
         )
     else:
         mine_ref[:, cols:] = lax.fori_loop(
             0,
-            devices,
-            lambda source, total: total + place_columns(*arrived(source)),
+            devices // 2,
+            lambda pair, total: total + place_columns(*arrived(pair)),
             jnp.zeros((half, 2 * slot_total), jnp.float32),
         )
 
@@ -668,7 +681,14 @@
             for value in (tr, winds, mass, span_owner, span_slot, diffusivity, span_column_count)
         )
     )
-    recv = lax.all_to_all(send, ("lat", "lon"), split_axis=0, concat_axis=0, tiled=True)
+    recv = lax.all_to_all(
+        send,
+        ("lat", "lon"),
+        split_axis=0,
+        concat_axis=0,
+        tiled=True,
+        axis_index_groups=[list(ORDERS[devices])] if devices in ORDERS else None,
+    )
     to_even, to_odd, edges, asked = call(
         functools.partial(halo_kernel, levels, rows, devices),
         [

time: 24.5 us -> 21.3 us (0.87)
  the two profiles are of different devices: /device:TPU:0 before, /device:TPU:13 now
where the time goes in v7:
time: 21.3 us; the launch traced here: 21.1 us
  starting transfers between devices  11.2 us (53%)
  Pallas kernels  4.87 us (23%)
  waiting for transfers between devices  4.27 us (20%)
  between operations  0.69 us (3%)
    all_to_all x1, starting transfers between devices, on_device(): lax.all_to_all(send, ('lat', 'lon'), split_axis=0, concat_axis=0, tiled=T...  4.81 us
    ppermute x2, starting transfers between devices, on_device(): lax.ppermute(values, 'lat', pairs + [(b, a) for a, b in pairs])  3.43 us
    ppermute x2, waiting for transfers between devices, on_device(): lax.ppermute(values, 'lat', pairs + [(b, a) for a, b in pairs])  2.38 us
    pallas_call x1, Pallas kernels, on_device(): call(functools.partial(pack_kernel, levels, rows, devices, lon_count), ou...  2.24 us
    ppermute x1, starting transfers between devices, on_device(): other = lax.ppermute(mine, 'lev', [(0, 1), (1, 0)])  1.75 us
    ppermute x1, waiting for transfers between devices, on_device(): from_west = lax.ppermute(edges, 'lon', to_east)  1.69 us
    ppermute x1, starting transfers between devices, on_device(): from_west = lax.ppermute(edges, 'lon', to_east)  1.25 us
    pallas_call x1, Pallas kernels, on_device(): call(functools.partial(solve_kernel, levels, rows), [(own_count * levels...  0.91 us
  transfers between devices with their start and end apart: 5, of which 4 were waited for; matrix products, arithmetic and copies ran while one was open for 0% of the time, Pallas kernels for 6%

profile of v7, /device:TPU:13, one launch (start us, length us, event | category | flops | bytes accessed | tf_op | source)
XLA Modules:
  0.0 21.1 jit_solution(10937868478444489731)
XLA Ops:
  0.6 2.2 %shard_map.86 = (f32[8,80,128]{2,1,0:T(8,128)}, f32[16,512]{1,0:T(8,128)S(1)}, f32[1,640]{1,0:T(1,128)S(1)}, s32[4,128]{1,0:T(4,128)S(1)}, s32[4,128]{1,0:T(4,12...) custom-call(f32[256,128]{1,0:T(8,128)} %bitcast.4, ...), custom_call_target="tpu_custom_call" | custom-call | tf_op jit(solution)/shard_map/pallas_call | solution.py:668
  2.9 4.8 %all-to-all-start = ((f32[8,80,128]{2,1,0:T(8,128)}), f32[8,80,128]{2,1,0:T(8,128)S(1)}, u32[]{:S(2)}, u32[]{:S(2)}) async-start(f32[8,80,128]{2,1,0:T(8,128)} %get-tuple-element.26), calls=%async_computation | async-start | bytes 655360 | tf_op jit(solution)/shard_map/all_to_all | solution.py:684
  7.7 0.4 %shard_map.87 = (f32[160,128]{1,0:T(8,128)S(1)}, f32[160,128]{1,0:T(8,128)S(1)}, f32[16,128]{1,0:T(8,128)S(1)}, s32[8,128]{1,0:T(8,128)S(1)}) custom-call(f32[256,128]{1,0:T(8,128)S(1)} %get-tuple-element.18.tr_ref, f32[256,128]{1,0:T(8,128)S(1)} %get-tuple-element.19.wind_ref, f32[128,128]{1,0:T(8,128)S(1)} %get-tuple-element.20.mass_ref, ...), custom_call_target="tpu_custom_call" | custom-call | tf_op jit(solution)/shard_map/pallas_call | solution.py:692
  8.2 1.2 %collective-permute-start = (f32[160,128]{1,0:T(8,128)S(1)}, f32[160,128]{1,0:T(8,128)S(1)}, u32[]{:S(2)}, u32[]{:S(2)}) collective-permute-start(f32[160,128]{1,0:T(8,128)S(1)} %get-tuple-element.24), channel_id=1, source_target_pairs={{0,4},{8,12},{4,0},{12,8},{1,5},{9,13},{5,1},{13,9},{2,6},{10,14},... | collective-permute-start | bytes 245768 | tf_op jit(solution)/shard_map/ppermute | solution.py:706
  9.4 2.2 %collective-permute-start.1 = (f32[160,128]{1,0:T(8,128)S(1)}, f32[160,128]{1,0:T(8,128)S(1)}, u32[]{:S(2)}, u32[]{:S(2)}) collective-permute-start(f32[160,128]{1,0:T(8,128)S(1)} %get-tuple-element.25), channel_id=1, source_target_pairs={{4,8},{8,4},{5,9},{9,5},{6,10},{10,6},{7,11},{11,7},{20,24},{24,20... | collective-permute-start | bytes 245768 | tf_op jit(solution)/shard_map/ppermute | solution.py:706
  11.6 1.2 %collective-permute-start.2 = (f32[16,128]{1,0:T(8,128)S(1)}, f32[16,128]{1,0:T(8,128)S(1)}, u32[]{:S(2)}, u32[]{:S(2)}) collective-permute-start(f32[16,128]{1,0:T(8,128)S(1)} %get-tuple-element.27.own_ref), channel_id=1, source_target_pairs={{0,2},{2,0},{1,3},{3,1},{4,6},{6,4},{5,7},{7,5},{8,10},{10,8},{9,1... | collective-permute-start | bytes 24584 | tf_op jit(solution)/shard_map/ppermute | solution.py:709
  12.8 1.7 %collective-permute-done.2.west_ref.east_ref.side_ref = f32[16,128]{1,0:T(8,128)S(1)} collective-permute-done((f32[16,128]{1,0:T(8,128)S(1)}, f32[16,128]{1,0:T(8,128)S(1)}, u32[]{:S(2)}, u32[]{:S(2)}) %collective-permute-start.2) | collective-permute-done | bytes 8224 | tf_op jit(solution)/shard_map/ppermute | solution.py:709
  14.5 1.4 %collective-permute-done.even_ref = f32[160,128]{1,0:T(8,128)S(1)} collective-permute-done((f32[160,128]{1,0:T(8,128)S(1)}, f32[160,128]{1,0:T(8,128)S(1)}, u32[]{:S(2)}, u32[]{:S(2)}) %collective-permute-start) | collective-permute-done | bytes 81952 | tf_op jit(solution)/shard_map/ppermute | solution.py:706
  15.9 1.0 %collective-permute-done.1.odd_ref = f32[160,128]{1,0:T(8,128)S(1)} collective-permute-done((f32[160,128]{1,0:T(8,128)S(1)}, f32[160,128]{1,0:T(8,128)S(1)}, u32[]{:S(2)}, u32[]{:S(2)}) %collective-permute-start.1) | collective-permute-done | bytes 81952 | tf_op jit(solution)/shard_map/ppermute | solution.py:706
  16.9 0.0 all-to-all-done.recv_ref
  16.9 0.5 %shard_map.89.mine_ref = f32[16,1792]{1,0:T(8,128)S(1)} custom-call(f32[8,80,128]{2,1,0:T(8,128)S(1)} %all-to-all-done.recv_ref, s32[4,128]{1,0:T(4,128)S(1)} %get-tuple-element.21.owner_ref, s32[4,128]{1,0:T(4,128)S(1)} %get-tuple-element.23.rank_ref, s32[8,128]{1,0:T(8,128)S(1)} %get-tuple-element.28.asked_ref, f32[16,512]{1,0:T(8,128)S(1)} %get-tuple-element.29.shear_ref, ...), custom_call_target="tpu_custom_call" | custom-call | tf_op jit(solution)/shard_map/pallas_call | solution.py:711
  17.4 1.8 %collective-permute-start.3 = (f32[16,1792]{1,0:T(8,128)S(1)}, f32[16,1792]{1,0:T(8,128)S(1)}, u32[]{:S(2)}, u32[]{:S(2)}) collective-permute-start(f32[16,1792]{1,0:T(8,128)S(1)} %shard_map.89.mine_ref), channel_id=1, source_target_pairs={{0,1},{1,0},{2,3},{3,2},{4,5},{5,4},{6,7},{7,6},{8,9},{9,8},{10,11... | collective-permute-start | bytes 344072 | tf_op jit(solution)/shard_map/ppermute | solution.py:722
  19.2 0.8 %shard_map.88.adv_ref = f32[256,128]{1,0:T(8,128)S(1)} custom-call(f32[256,128]{1,0:T(8,128)S(1)} %get-tuple-element.18.tr_ref, f32[256,128]{1,0:T(8,128)S(1)} %get-tuple-element.19.wind_ref, f32[128,128]{1,0:T(8,128)S(1)} %get-tuple-element.20.mass_ref, f32[160,128]{1,0:T(8,128)S(1)} %collective-permute-done.even_ref, ...), custom_call_target="tpu_custom_call" | custom-call | tf_op jit(solution)/shard_map/pallas_call | solution.py:723
  20.0 0.2 collective-permute-done.3.other_ref
  20.2 0.9 %shard_map.90 = (f32[256,128]{1,0:T(8,128)}, f32[31,640]{1,0:T(8,128)}) custom-call(f32[256,128]{1,0:T(8,128)S(1)} %shard_map.88.adv_ref, f32[16,1792]{1,0:T(8,128)S(1)} %shard_map.89.mine_ref, f32[16,1792]{1,0:T(8,128)S(1)} %collective-permute-done.3.other_ref, f32[31,640]{1,0:T(8,128)S(1)} %get-tuple-element.30.old_ref, ...), custom_call_target="tpu_custom_call" | custom-call | tf_op jit(solution)/shard_map/pallas_call | solution.py:729
Async XLA Ops:
  2.9 14.0 %all-to-all-start = ((f32[8,80,128]{2,1,0:T(8,128)}), f32[8,80,128]{2,1,0:T(8,128)S(1)}, u32[]{:S(2)}, u32[]{:S(2)}) async-start(f32[8,80,128]{2,1,0:T(8,128)} %get-tuple-element.26), calls=%async_computation | async-start | bytes 655360 | tf_op jit(solution)/shard_map/all_to_all | solution.py:684
  8.2 7.8 %collective-permute-start = (f32[160,128]{1,0:T(8,128)S(1)}, f32[160,128]{1,0:T(8,128)S(1)}, u32[]{:S(2)}, u32[]{:S(2)}) collective-permute-start(f32[160,128]{1,0:T(8,128)S(1)} %get-tuple-element.24), channel_id=1, source_target_pairs={{0,4},{8,12},{4,0},{12,8},{1,5},{9,13},{5,1},{13,9},{2,6},{10,14},... | collective-permute-start | bytes 245768 | tf_op jit(solution)/shard_map/ppermute | solution.py:706
  9.4 7.5 %collective-permute-start.1 = (f32[160,128]{1,0:T(8,128)S(1)}, f32[160,128]{1,0:T(8,128)S(1)}, u32[]{:S(2)}, u32[]{:S(2)}) collective-permute-start(f32[160,128]{1,0:T(8,128)S(1)} %get-tuple-element.25), channel_id=1, source_target_pairs={{4,8},{8,4},{5,9},{9,5},{6,10},{10,6},{7,11},{11,7},{20,24},{24,20... | collective-permute-start | bytes 245768 | tf_op jit(solution)/shard_map/ppermute | solution.py:706
  11.6 2.9 %collective-permute-start.2 = (f32[16,128]{1,0:T(8,128)S(1)}, f32[16,128]{1,0:T(8,128)S(1)}, u32[]{:S(2)}, u32[]{:S(2)}) collective-permute-start(f32[16,128]{1,0:T(8,128)S(1)} %get-tuple-element.27.own_ref), channel_id=1, source_target_pairs={{0,2},{2,0},{1,3},{3,1},{4,6},{6,4},{5,7},{7,5},{8,10},{10,8},{9,1... | collective-permute-start | bytes 24584 | tf_op jit(solution)/shard_map/ppermute | solution.py:709
  17.4 2.7 %collective-permute-start.3 = (f32[16,1792]{1,0:T(8,128)S(1)}, f32[16,1792]{1,0:T(8,128)S(1)}, u32[]{:S(2)}, u32[]{:S(2)}) collective-permute-start(f32[16,1792]{1,0:T(8,128)S(1)} %shard_map.89.mine_ref), channel_id=1, source_target_pairs={{0,1},{1,0},{2,3},{3,2},{4,5},{5,4},{6,7},{7,6},{8,9},{9,8},{10,11... | collective-permute-start | bytes 344072 | tf_op jit(solution)/shard_map/ppermute | solution.py:722

commit v8 on v7

--- a/solution.py
+++ b/solution.py
@@ -27,12 +27,10 @@
     return lax.broadcasted_iota(jnp.int32, shape, len(shape) - 1)
 
 
-def split3(values):
+def split2(values):
     top = values.astype(jnp.bfloat16)
-    rest = values - top.astype(jnp.float32)
-    mid = rest.astype(jnp.bfloat16)
-    low = (rest - mid.astype(jnp.float32)).astype(jnp.bfloat16)
-    return jnp.concatenate([top, mid, low], axis=0)
+    rest = (values - top.astype(jnp.float32)).astype(jnp.bfloat16)
+    return jnp.concatenate([top, rest], axis=0)
 
 
 def hot_matrix(row_of, size):
@@ -43,8 +41,8 @@
 def pick_columns(masked, hot, rows):
     out = lax.dot_general(masked, hot, NT, preferred_element_type=jnp.float32)
     return [
-        out[at : at + rows] + out[at + rows : at + 2 * rows] + out[at + 2 * rows : at + 3 * rows]
-        for at in range(0, masked.shape[0], 3 * rows)
+        out[at : at + rows] + out[at + rows : at + 2 * rows]
+        for at in range(0, masked.shape[0], 2 * rows)
     ]
 
 
@@ -161,7 +159,7 @@
         lower.append(shear[:half])
         upper.append(jnp.concatenate([shear[half:], slot], axis=0))
         shear_ref[:, j * LANES : (j + 1) * LANES] = own_faces(shear)
-    split = split3(jnp.concatenate(lower + upper, axis=1))
+    split = split2(jnp.concatenate(lower + upper, axis=1))
 
     diffs = own_faces(diff_ref[...])
     starts, start = [], 0
@@ -242,25 +240,12 @@
         copy.wait()
 
 
-def halo_kernel(
-    levels, rows, devices, tr_ref, wind_ref, mass_ref, owner_ref, slot_ref, rank_ref,
-    even_ref, odd_ref, edge_ref, asked_ref,
-):
+def mass_rows(levels, rows, mass_ref, j):
+    return mass_ref[pl.ds(j, levels, stride=rows), :]
+
+
+def lat_kernel(levels, rows, tr_ref, wind_ref, mass_ref, even_ref, odd_ref):
     last = rows - 1
-
-    def flat(ref):
-        return jnp.concatenate([ref[j : j + 1, :] for j in range(rows)], axis=1)
-
-    owner, hot = flat(owner_ref), hot_matrix(flat(rank_ref), LANES)
-    filler = jnp.zeros((7, rows * LANES), jnp.float32)
-    split = split3(jnp.concatenate([flat(slot_ref).astype(jnp.float32) + 1.0, filler], axis=0))
-
-    def ask(dest):
-        (found,) = pick_columns(only_where(split, owner, device_of(devices, dest)), hot, 8)
-        asked_ref[pl.ds(dest, 1), :] = found[0:1].astype(jnp.int32) - 1
-
-    loop_over(devices, ask)
-    lane_row = lane_iota((1, LANES))
 
     def east_row(j):
         return wind_ref[pl.ds(j, levels, stride=rows), :]
@@ -269,21 +254,7 @@
         return wind_ref[pl.ds(levels * rows + j, levels, stride=rows), :]
 
     def mass_row(j):
-        return mass_ref[pl.ds(j, levels, stride=rows), :]
-
-    turned = [turn(levels, rows, tr_ref, wind_ref, j) for j in range(rows)]
-    masses = jnp.transpose(jnp.concatenate([mass_row(j) for j in range(rows)], axis=0))
-    edge_rows = [[], [], [], []]
-    for j in range(rows):
-        west_mass = pltpu.roll(masses[0:1], (2 * levels - j * levels) % LANES, 1)
-        east_mass = pltpu.roll(masses[LANES - 1 :], (3 * levels - j * levels) % LANES, 1)
-        edge_rows[0].append(
-            jnp.where(lane_row >= 3 * levels, east_mass, turned[j][LANES - 2 : LANES - 1])
-        )
-        edge_rows[1].append(turned[j][LANES - 1 :])
-        edge_rows[2].append(turned[j][0:1])
-        edge_rows[3].append(jnp.where(lane_row >= 2 * levels, west_mass, turned[j][1:2]))
-    edge_ref[...] = jnp.concatenate([row for group in edge_rows for row in group], axis=0)
+        return mass_rows(levels, rows, mass_ref, j)
 
     lane_level = lane_iota((levels, LANES))
 
@@ -313,6 +284,42 @@
         here = slice(index * levels, (index + 1) * levels)
         even_ref[here] = jnp.where(even, north, south)
         odd_ref[here] = jnp.where(even, south, north)
+
+
+def edge_kernel(
+    levels, rows, devices, tr_ref, wind_ref, mass_ref, owner_ref, slot_ref, rank_ref,
+    edge_ref, asked_ref,
+):
+    lane_row = lane_iota((1, LANES))
+
+    def mass_row(j):
+        return mass_rows(levels, rows, mass_ref, j)
+
+    def flat(ref):
+        return jnp.concatenate([ref[j : j + 1, :] for j in range(rows)], axis=1)
+
+    owner, hot = flat(owner_ref), hot_matrix(flat(rank_ref), LANES)
+    filler = jnp.zeros((7, rows * LANES), jnp.float32)
+    split = split2(jnp.concatenate([flat(slot_ref).astype(jnp.float32) + 1.0, filler], axis=0))
+
+    def ask(dest):
+        (found,) = pick_columns(only_where(split, owner, device_of(devices, dest)), hot, 8)
+        asked_ref[pl.ds(dest, 1), :] = found[0:1].astype(jnp.int32) - 1
+
+    loop_over(devices, ask)
+    turned = [turn(levels, rows, tr_ref, wind_ref, j) for j in range(rows)]
+    masses = jnp.transpose(jnp.concatenate([mass_row(j) for j in range(rows)], axis=0))
+    edge_rows = [[], [], [], []]
+    for j in range(rows):
+        west_mass = pltpu.roll(masses[0:1], (2 * levels - j * levels) % LANES, 1)
+        east_mass = pltpu.roll(masses[LANES - 1 :], (3 * levels - j * levels) % LANES, 1)
+        edge_rows[0].append(
+            jnp.where(lane_row >= 3 * levels, east_mass, turned[j][LANES - 2 : LANES - 1])
+        )
+        edge_rows[1].append(turned[j][LANES - 1 :])
+        edge_rows[2].append(turned[j][0:1])
+        edge_rows[3].append(jnp.where(lane_row >= 2 * levels, west_mass, turned[j][1:2]))
+    edge_ref[...] = jnp.concatenate([row for group in edge_rows for row in group], axis=0)
 
 
 def neighbour_blocks(lat_count, lon_count):
@@ -400,7 +407,7 @@
         return slots, jnp.concatenate([lower, jnp.where(bottom, 0.0, upper)], axis=0)
 
     def place_columns(slots, values):
-        split = split3(values)
+        split = split2(values)
         masked = [only_where(split, slots >> 7, index) for index in range(spans)]
         hot = hot_matrix(slots & (LANES - 1), LANES)
         placed = pick_columns(jnp.concatenate(masked, axis=0), hot, levels)
@@ -689,16 +696,17 @@
         tiled=True,
         axis_index_groups=[list(ORDERS[devices])] if devices in ORDERS else None,
     )
-    to_even, to_odd, edges, asked = call(
-        functools.partial(halo_kernel, levels, rows, devices),
-        [
-            (5 * levels, LANES),
-            (5 * levels, LANES),
-            (4 * rows, LANES),
-            jax.ShapeDtypeStruct((devices, LANES), jnp.int32),
-        ],
+    to_even, to_odd = call(
+        functools.partial(lat_kernel, levels, rows),
+        [(5 * levels, LANES), (5 * levels, LANES)],
+        [vmem] * 3,
+        [vmem] * 2,
+    )(tr, winds, mass)
+    edges, asked = call(
+        functools.partial(edge_kernel, levels, rows, devices),
+        [(4 * rows, LANES), jax.ShapeDtypeStruct((devices, LANES), jnp.int32)],
         [vmem] * 6,
-        [vmem] * 4,
+        [vmem] * 2,
     )(tr, winds, mass, owner, slot, rank)
     from_lat = []
     for first, values in enumerate((to_even, to_odd)):

time: 21.3 us -> 21.2 us (level)
    pallas_call x1 -> x2, Pallas kernels: 0.45 us -> 0.53 us  [the longest x1 0.37 us: on_device(): call(functools.partial(edge_kernel, levels, rows, devices), [(4 * rows, L...]
where the time goes in v8:
time: 21.2 us; the launch traced here: 20.9 us
  starting transfers between devices  11.3 us (53%)
  Pallas kernels  4.81 us (23%)
  waiting for transfers between devices  4.09 us (19%)
  between operations  0.67 us (3%)
    all_to_all x1, starting transfers between devices, on_device(): lax.all_to_all(send, ('lat', 'lon'), split_axis=0, concat_axis=0, tiled=T...  4.81 us
    ppermute x2, starting transfers between devices, on_device(): lax.ppermute(values, 'lat', pairs + [(b, a) for a, b in pairs])  3.42 us
    ppermute x2, waiting for transfers between devices, on_device(): lax.ppermute(values, 'lat', pairs + [(b, a) for a, b in pairs])  2.2 us
    pallas_call x1, Pallas kernels, on_device(): call(functools.partial(pack_kernel, levels, rows, devices, lon_count), ou...  2.11 us
    ppermute x1, starting transfers between devices, on_device(): other = lax.ppermute(mine, 'lev', [(0, 1), (1, 0)])  1.91 us
    ppermute x1, waiting for transfers between devices, on_device(): from_west = lax.ppermute(edges, 'lon', to_east)  1.7 us
    ppermute x1, starting transfers between devices, on_device(): from_west = lax.ppermute(edges, 'lon', to_east)  1.21 us
    pallas_call x1, Pallas kernels, on_device(): call(functools.partial(solve_kernel, levels, rows), [(own_count * levels...  0.91 us
  transfers between devices with their start and end apart: 5, of which 4 were waited for; matrix products, arithmetic and copies ran while one was open for 0% of the time, Pallas kernels for 6%

profile of v8, /device:TPU:13, one launch (start us, length us, event | category | flops | bytes accessed | tf_op | source)
XLA Modules:
  0.0 20.9 jit_solution(7660963558057915188)
XLA Ops:
  0.6 2.1 %shard_map.86 = (f32[8,80,128]{2,1,0:T(8,128)}, f32[16,512]{1,0:T(8,128)S(1)}, f32[1,640]{1,0:T(1,128)S(1)}, s32[4,128]{1,0:T(4,128)S(1)}, s32[4,128]{1,0:T(4,12...) custom-call(f32[256,128]{1,0:T(8,128)} %bitcast.4, ...), custom_call_target="tpu_custom_call" | custom-call | tf_op jit(solution)/shard_map/pallas_call | solution.py:675
  2.7 4.8 %all-to-all-start = ((f32[8,80,128]{2,1,0:T(8,128)}), f32[8,80,128]{2,1,0:T(8,128)S(1)}, u32[]{:S(2)}, u32[]{:S(2)}) async-start(f32[8,80,128]{2,1,0:T(8,128)} %get-tuple-element.23), calls=%async_computation | async-start | bytes 655360 | tf_op jit(solution)/shard_map/all_to_all | solution.py:691
  7.6 0.2 shard_map.87
  7.7 1.2 %collective-permute-start = (f32[160,128]{1,0:T(8,128)S(1)}, f32[160,128]{1,0:T(8,128)S(1)}, u32[]{:S(2)}, u32[]{:S(2)}) collective-permute-start(f32[160,128]{1,0:T(8,128)S(1)} %get-tuple-element.21), channel_id=1, source_target_pairs={{0,4},{8,12},{4,0},{12,8},{1,5},{9,13},{5,1},{13,9},{2,6},{10,14},... | collective-permute-start | bytes 245768 | tf_op jit(solution)/shard_map/ppermute | solution.py:714
  9.0 2.2 %collective-permute-start.1 = (f32[160,128]{1,0:T(8,128)S(1)}, f32[160,128]{1,0:T(8,128)S(1)}, u32[]{:S(2)}, u32[]{:S(2)}) collective-permute-start(f32[160,128]{1,0:T(8,128)S(1)} %get-tuple-element.22), channel_id=1, source_target_pairs={{4,8},{8,4},{5,9},{9,5},{6,10},{10,6},{7,11},{11,7},{20,24},{24,20... | collective-permute-start | bytes 245768 | tf_op jit(solution)/shard_map/ppermute | solution.py:714
  11.2 0.4 %shard_map.88 = (f32[16,128]{1,0:T(8,128)S(1)}, s32[8,128]{1,0:T(8,128)S(1)}) custom-call(f32[256,128]{1,0:T(8,128)S(1)} %get-tuple-element.18.tr_ref, f32[256,128]{1,0:T(8,128)S(1)} %get-tuple-element.19.wind_ref, f32[128,128]{1,0:T(8,128)S(1)} %get-tuple-element.20.mass_ref, s32[4,128]{1,0:T(4,128)S(1)} %get-tuple-element.24.owner_ref, ...), custom_call_target="tpu_custom_call" | custom-call | tf_op jit(solution)/shard_map/pallas_call | solution.py:705
  11.5 1.2 %collective-permute-start.2 = (f32[16,128]{1,0:T(8,128)S(1)}, f32[16,128]{1,0:T(8,128)S(1)}, u32[]{:S(2)}, u32[]{:S(2)}) collective-permute-start(f32[16,128]{1,0:T(8,128)S(1)} %get-tuple-element.27.own_ref), channel_id=1, source_target_pairs={{0,2},{2,0},{1,3},{3,1},{4,6},{6,4},{5,7},{7,5},{8,10},{10,8},{9,1... | collective-permute-start | bytes 24584 | tf_op jit(solution)/shard_map/ppermute | solution.py:717
  12.7 1.7 %collective-permute-done.2.west_ref.east_ref.side_ref = f32[16,128]{1,0:T(8,128)S(1)} collective-permute-done((f32[16,128]{1,0:T(8,128)S(1)}, f32[16,128]{1,0:T(8,128)S(1)}, u32[]{:S(2)}, u32[]{:S(2)}) %collective-permute-start.2) | collective-permute-done | bytes 8224 | tf_op jit(solution)/shard_map/ppermute | solution.py:717
  14.4 1.4 %collective-permute-done.even_ref = f32[160,128]{1,0:T(8,128)S(1)} collective-permute-done((f32[160,128]{1,0:T(8,128)S(1)}, f32[160,128]{1,0:T(8,128)S(1)}, u32[]{:S(2)}, u32[]{:S(2)}) %collective-permute-start) | collective-permute-done | bytes 81952 | tf_op jit(solution)/shard_map/ppermute | solution.py:714
  15.8 0.8 %collective-permute-done.1.odd_ref = f32[160,128]{1,0:T(8,128)S(1)} collective-permute-done((f32[160,128]{1,0:T(8,128)S(1)}, f32[160,128]{1,0:T(8,128)S(1)}, u32[]{:S(2)}, u32[]{:S(2)}) %collective-permute-start.1) | collective-permute-done | bytes 81952 | tf_op jit(solution)/shard_map/ppermute | solution.py:714
  16.6 0.0 all-to-all-done.recv_ref
  16.6 0.5 %shard_map.90.mine_ref = f32[16,1792]{1,0:T(8,128)S(1)} custom-call(f32[8,80,128]{2,1,0:T(8,128)S(1)} %all-to-all-done.recv_ref, s32[4,128]{1,0:T(4,128)S(1)} %get-tuple-element.24.owner_ref, s32[4,128]{1,0:T(4,128)S(1)} %get-tuple-element.26.rank_ref, s32[8,128]{1,0:T(8,128)S(1)} %get-tuple-element.28.asked_ref, f32[16,512]{1,0:T(8,128)S(1)} %get-tuple-element.29.shear_ref, ...), custom_call_target="tpu_custom_call" | custom-call | tf_op jit(solution)/shard_map/pallas_call | solution.py:719
  17.1 1.9 %collective-permute-start.3 = (f32[16,1792]{1,0:T(8,128)S(1)}, f32[16,1792]{1,0:T(8,128)S(1)}, u32[]{:S(2)}, u32[]{:S(2)}) collective-permute-start(f32[16,1792]{1,0:T(8,128)S(1)} %shard_map.90.mine_ref), channel_id=1, source_target_pairs={{0,1},{1,0},{2,3},{3,2},{4,5},{5,4},{6,7},{7,6},{8,9},{9,8},{10,11... | collective-permute-start | bytes 344072 | tf_op jit(solution)/shard_map/ppermute | solution.py:730
  19.0 0.8 %shard_map.89.adv_ref = f32[256,128]{1,0:T(8,128)S(1)} custom-call(f32[256,128]{1,0:T(8,128)S(1)} %get-tuple-element.18.tr_ref, f32[256,128]{1,0:T(8,128)S(1)} %get-tuple-element.19.wind_ref, f32[128,128]{1,0:T(8,128)S(1)} %get-tuple-element.20.mass_ref, f32[160,128]{1,0:T(8,128)S(1)} %collective-permute-done.even_ref, ...), custom_call_target="tpu_custom_call" | custom-call | tf_op jit(solution)/shard_map/pallas_call | solution.py:731
  19.8 0.2 collective-permute-done.3.other_ref
  20.0 0.9 %shard_map.91 = (f32[256,128]{1,0:T(8,128)}, f32[31,640]{1,0:T(8,128)}) custom-call(f32[256,128]{1,0:T(8,128)S(1)} %shard_map.89.adv_ref, f32[16,1792]{1,0:T(8,128)S(1)} %shard_map.90.mine_ref, f32[16,1792]{1,0:T(8,128)S(1)} %collective-permute-done.3.other_ref, f32[31,640]{1,0:T(8,128)S(1)} %get-tuple-element.30.old_ref, ...), custom_call_target="tpu_custom_call" | custom-call | tf_op jit(solution)/shard_map/pallas_call | solution.py:737
Async XLA Ops:
  2.7 13.9 %all-to-all-start = ((f32[8,80,128]{2,1,0:T(8,128)}), f32[8,80,128]{2,1,0:T(8,128)S(1)}, u32[]{:S(2)}, u32[]{:S(2)}) async-start(f32[8,80,128]{2,1,0:T(8,128)} %get-tuple-element.23), calls=%async_computation | async-start | bytes 655360 | tf_op jit(solution)/shard_map/all_to_all | solution.py:691
  7.7 8.1 %collective-permute-start = (f32[160,128]{1,0:T(8,128)S(1)}, f32[160,128]{1,0:T(8,128)S(1)}, u32[]{:S(2)}, u32[]{:S(2)}) collective-permute-start(f32[160,128]{1,0:T(8,128)S(1)} %get-tuple-element.21), channel_id=1, source_target_pairs={{0,4},{8,12},{4,0},{12,8},{1,5},{9,13},{5,1},{13,9},{2,6},{10,14},... | collective-permute-start | bytes 245768 | tf_op jit(solution)/shard_map/ppermute | solution.py:714
  9.0 7.7 %collective-permute-start.1 = (f32[160,128]{1,0:T(8,128)S(1)}, f32[160,128]{1,0:T(8,128)S(1)}, u32[]{:S(2)}, u32[]{:S(2)}) collective-permute-start(f32[160,128]{1,0:T(8,128)S(1)} %get-tuple-element.22), channel_id=1, source_target_pairs={{4,8},{8,4},{5,9},{9,5},{6,10},{10,6},{7,11},{11,7},{20,24},{24,20... | collective-permute-start | bytes 245768 | tf_op jit(solution)/shard_map/ppermute | solution.py:714
  11.5 2.9 %collective-permute-start.2 = (f32[16,128]{1,0:T(8,128)S(1)}, f32[16,128]{1,0:T(8,128)S(1)}, u32[]{:S(2)}, u32[]{:S(2)}) collective-permute-start(f32[16,128]{1,0:T(8,128)S(1)} %get-tuple-element.27.own_ref), channel_id=1, source_target_pairs={{0,2},{2,0},{1,3},{3,1},{4,6},{6,4},{5,7},{7,5},{8,10},{10,8},{9,1... | collective-permute-start | bytes 24584 | tf_op jit(solution)/shard_map/ppermute | solution.py:717
  17.1 2.9 %collective-permute-start.3 = (f32[16,1792]{1,0:T(8,128)S(1)}, f32[16,1792]{1,0:T(8,128)S(1)}, u32[]{:S(2)}, u32[]{:S(2)}) collective-permute-start(f32[16,1792]{1,0:T(8,128)S(1)} %shard_map.90.mine_ref), channel_id=1, source_target_pairs={{0,1},{1,0},{2,3},{3,2},{4,5},{5,4},{6,7},{7,6},{8,9},{9,8},{10,11... | collective-permute-start | bytes 344072 | tf_op jit(solution)/shard_map/ppermute | solution.py:730

commit v9 on v8

--- a/solution.py
+++ b/solution.py
@@ -8,7 +8,7 @@
 from jax.sharding import PartitionSpec as P
 
 LANES = 128
-ORDERS = {8: (4, 6, 1, 0, 7, 5, 2, 3)}
+ORDERS = {8: (4, 3, 1, 0, 7, 5, 6, 2)}
 VMEM_LIMIT = 48 * 1024 * 1024
 NT = (((1,), (1,)), ((), ()))
 
@@ -346,7 +346,7 @@
 
 def select_kernel(
     levels, rows, devices, recv_ref, owner_ref, rank_ref, asked_ref, shear_ref,
-    side_ref, even_ref, odd_ref, mine_ref, lane_ref, group_ref, middle_ref,
+    side_ref, mine_ref, lane_ref, group_ref, middle_ref,
 ):
     half = levels // 2
     cols = rows * LANES
@@ -641,6 +641,7 @@
         scratch_shapes=list(scratch),
         input_output_aliases=aliases or {},
         compiler_params=pltpu.CompilerParams(vmem_limit_bytes=VMEM_LIMIT),
+        cost_estimate=pl.CostEstimate(flops=10**9, bytes_accessed=1000, transcendentals=0),
     )
 
 
@@ -709,7 +710,7 @@
         [vmem] * 2,
     )(tr, winds, mass, owner, slot, rank)
     from_lat = []
-    for first, values in enumerate((to_even, to_odd)):
+    for first, values in ((1, to_odd), (0, to_even)):
         pairs = [(i, i + 1) for i in range(first, lat_count - 1, 2)]
         from_lat.append(lax.ppermute(values, "lat", pairs + [(b, a) for a, b in pairs]))
     to_east = [(i, (i + 1) % lon_count) for i in range(lon_count)]
@@ -719,21 +720,21 @@
     (mine,) = call(
         functools.partial(select_kernel, levels, rows, devices),
         [(half, rows * LANES + 2 * slot_total)],
-        [vmem] * 5 + [pl.BlockSpec(memory_space=pl.ANY)] * 3,
+        [vmem] * 5 + [pl.BlockSpec(memory_space=pl.ANY)],
         [vmem],
         [
             pltpu.VMEM((devices, LANES), jnp.int32),
             pltpu.VMEM((devices, LANES), jnp.int32),
             pltpu.VMEM((devices, LANES), jnp.float32),
         ],
-    )(recv, owner, rank, asked, shear, from_west, *from_lat)
+    )(recv, owner, rank, asked, shear, from_west)
     other = lax.ppermute(mine, "lev", [(0, 1), (1, 0)])
     (advected,) = call(
         functools.partial(advect_kernel, levels, rows, lat_count, lon_count),
         [(levels * own_count * rows, LANES)],
         [vmem] * 9,
         [vmem],
-    )(tr, winds, mass, *from_lat, recv, edges, from_west, from_east)
+    )(tr, winds, mass, *from_lat[::-1], recv, edges, from_west, from_east)
     out, diff_out = call(
         functools.partial(solve_kernel, levels, rows),
         [(own_count * levels * rows, cols), (levels - 1, slot_total)],

time: 21.2 us -> 20.5 us (0.967)
  the two profiles are of different devices: /device:TPU:13 before, /device:TPU:0 now
where the time goes in v9:
time: 20.5 us; the launch traced here: 20.2 us
  starting transfers between devices  10.7 us (52%)
  Pallas kernels  4.8 us (23%)
  waiting for transfers between devices  4.01 us (20%)
  between operations  0.68 us (3%)
    all_to_all x1, starting transfers between devices, on_device(): lax.all_to_all(send, ('lat', 'lon'), split_axis=0, concat_axis=0, tiled=T...  7.83 us
    pallas_call x1, Pallas kernels, on_device(): call(functools.partial(pack_kernel, levels, rows, devices, lon_count), ou...  2.11 us
    all_to_all x1, waiting for transfers between devices, on_device(): lax.all_to_all(send, ('lat', 'lon'), split_axis=0, concat_axis=0, tiled=T...  1.92 us
    ppermute x1, waiting for transfers between devices, on_device(): from_west = lax.ppermute(edges, 'lon', to_east)  1.56 us
    ppermute x1, starting transfers between devices, on_device(): from_west = lax.ppermute(edges, 'lon', to_east)  1.49 us
    ppermute x2, starting transfers between devices, on_device(): lax.ppermute(values, 'lat', pairs + [(b, a) for a, b in pairs])  1.28 us
    pallas_call x1, Pallas kernels, on_device(): call(functools.partial(solve_kernel, levels, rows), [(own_count * levels...  0.91 us
    pallas_call x1, Pallas kernels, on_device(): call(functools.partial(advect_kernel, levels, rows, lat_count, lon_count)...  0.77 us
  transfers between devices with their start and end apart: 5, of which 4 were waited for; matrix products, arithmetic and copies ran while one was open for 0% of the time, Pallas kernels for 9%

profile of v9, /device:TPU:0, one launch (start us, length us, event | category | flops | bytes accessed | tf_op | source)
XLA Modules:
  0.0 20.2 jit_solution(16351294106780333111)
XLA Ops:
  0.6 2.1 %shard_map.86 = (f32[8,80,128]{2,1,0:T(8,128)}, f32[16,512]{1,0:T(8,128)S(1)}, f32[1,640]{1,0:T(1,128)S(1)}, s32[4,128]{1,0:T(4,128)S(1)}, s32[4,128]{1,0:T(4,12...) custom-call(f32[256,128]{1,0:T(8,128)} %bitcast.4, ...), custom_call_target="tpu_custom_call" | custom-call | flops 1000000000 | bytes 1000 | tf_op jit(solution)/shard_map/pallas_call | solution.py:676
  2.7 7.8 %all-to-all-start = ((f32[8,80,128]{2,1,0:T(8,128)}), f32[8,80,128]{2,1,0:T(8,128)S(1)}, u32[]{:S(2)}, u32[]{:S(2)}) async-start(f32[8,80,128]{2,1,0:T(8,128)} %get-tuple-element.23), calls=%async_computation | async-start | bytes 655360 | tf_op jit(solution)/shard_map/all_to_all | solution.py:692
  10.6 0.4 %shard_map.88 = (f32[16,128]{1,0:T(8,128)S(1)}, s32[8,128]{1,0:T(8,128)S(1)}) custom-call(f32[256,128]{1,0:T(8,128)S(1)} %get-tuple-element.18.tr_ref, f32[256,128]{1,0:T(8,128)S(1)} %get-tuple-element.19.wind_ref, f32[128,128]{1,0:T(8,128)S(1)} %get-tuple-element.20.mass_ref, s32[4,128]{1,0:T(4,128)S(1)} %get-tuple-element.24.owner_ref, ...), custom_call_target="tpu_custom_call" | custom-call | flops 1000000000 | bytes 1000 | tf_op jit(solution)/shard_map/pallas_call | solution.py:706
  10.9 1.5 %collective-permute-start.2 = (f32[16,128]{1,0:T(8,128)S(1)}, f32[16,128]{1,0:T(8,128)S(1)}, u32[]{:S(2)}, u32[]{:S(2)}) collective-permute-start(f32[16,128]{1,0:T(8,128)S(1)} %get-tuple-element.27.own_ref), channel_id=1, source_target_pairs={{0,2},{2,0},{1,3},{3,1},{4,6},{6,4},{5,7},{7,5},{8,10},{10,8},{9,1... | collective-permute-start | bytes 24584 | tf_op jit(solution)/shard_map/ppermute | solution.py:718
  12.4 0.2 shard_map.87
  12.6 0.6 %collective-permute-start = (f32[160,128]{1,0:T(8,128)S(1)}, f32[160,128]{1,0:T(8,128)S(1)}, u32[]{:S(2)}, u32[]{:S(2)}) collective-permute-start(f32[160,128]{1,0:T(8,128)S(1)} %get-tuple-element.21), channel_id=1, source_target_pairs={{0,4},{8,12},{4,0},{12,8},{1,5},{9,13},{5,1},{13,9},{2,6},{10,14},... | collective-permute-start | bytes 245768 | tf_op jit(solution)/shard_map/ppermute | solution.py:715
  13.2 0.7 %collective-permute-start.1 = (f32[160,128]{1,0:T(8,128)S(1)}, f32[160,128]{1,0:T(8,128)S(1)}, u32[]{:S(2)}, u32[]{:S(2)}) collective-permute-start(f32[160,128]{1,0:T(8,128)S(1)} %get-tuple-element.22), channel_id=1, source_target_pairs={{4,8},{8,4},{5,9},{9,5},{6,10},{10,6},{7,11},{11,7},{20,24},{24,20... | collective-permute-start | bytes 245768 | tf_op jit(solution)/shard_map/ppermute | solution.py:715
  13.9 1.6 %collective-permute-done.2.west_ref.east_ref.side_ref = f32[16,128]{1,0:T(8,128)S(1)} collective-permute-done((f32[16,128]{1,0:T(8,128)S(1)}, f32[16,128]{1,0:T(8,128)S(1)}, u32[]{:S(2)}, u32[]{:S(2)}) %collective-permute-start.2) | collective-permute-done | bytes 8224 | tf_op jit(solution)/shard_map/ppermute | solution.py:718
  15.4 1.9 %all-to-all-done.recv_ref = f32[8,80,128]{2,1,0:T(8,128)S(1)} async-done(((f32[8,80,128]{2,1,0:T(8,128)}), f32[8,80,128]{2,1,0:T(8,128)S(1)}, u32[]{:S(2)}, u32[]{:S(2)}) %all-to-all-start) | async-done | bytes 327712 | tf_op jit(solution)/shard_map/all_to_all | solution.py:692
  17.4 0.5 %shard_map.90.mine_ref = f32[16,1792]{1,0:T(8,128)S(1)} custom-call(f32[8,80,128]{2,1,0:T(8,128)S(1)} %all-to-all-done.recv_ref, s32[4,128]{1,0:T(4,128)S(1)} %get-tuple-element.24.owner_ref, s32[4,128]{1,0:T(4,128)S(1)} %get-tuple-element.26.rank_ref, s32[8,128]{1,0:T(8,128)S(1)} %get-tuple-element.28.asked_ref, f32[16,512]{1,0:T(8,128)S(1)} %get-tuple-element.29.shear_ref, ...), custom_call_target="tpu_custom_call" | custom-call | flops 1000000000 | bytes 1000 | tf_op jit(solution)/shard_map/pallas_call | solution.py:720
  17.9 0.1 collective-permute-start.3
  17.9 0.1 collective-permute-done.even_ref
  18.1 0.0 collective-permute-done.1.odd_ref
  18.1 0.8 %shard_map.89.adv_ref = f32[256,128]{1,0:T(8,128)S(1)} custom-call(f32[256,128]{1,0:T(8,128)S(1)} %get-tuple-element.18.tr_ref, f32[256,128]{1,0:T(8,128)S(1)} %get-tuple-element.19.wind_ref, f32[128,128]{1,0:T(8,128)S(1)} %get-tuple-element.20.mass_ref, f32[160,128]{1,0:T(8,128)S(1)} %collective-permute-done.even_ref, ...), custom_call_target="tpu_custom_call" | custom-call | flops 1000000000 | bytes 1000 | tf_op jit(solution)/shard_map/pallas_call | solution.py:732
  18.8 0.4 %collective-permute-done.3.other_ref = f32[16,1792]{1,0:T(8,128)S(1)} collective-permute-done((f32[16,1792]{1,0:T(8,128)S(1)}, f32[16,1792]{1,0:T(8,128)S(1)}, u32[]{:S(2)}, u32[]{:S(2)}) %collective-permute-start.3) | collective-permute-done | bytes 114720 | tf_op jit(solution)/shard_map/ppermute | solution.py:731
  19.3 0.9 %shard_map.91 = (f32[256,128]{1,0:T(8,128)}, f32[31,640]{1,0:T(8,128)}) custom-call(f32[256,128]{1,0:T(8,128)S(1)} %shard_map.89.adv_ref, f32[16,1792]{1,0:T(8,128)S(1)} %shard_map.90.mine_ref, f32[16,1792]{1,0:T(8,128)S(1)} %collective-permute-done.3.other_ref, f32[31,640]{1,0:T(8,128)S(1)} %get-tuple-element.30.old_ref, ...), custom_call_target="tpu_custom_call" | custom-call | flops 1000000000 | bytes 1000 | tf_op jit(solution)/shard_map/pallas_call | solution.py:738
Async XLA Ops:
  2.7 14.6 %all-to-all-start = ((f32[8,80,128]{2,1,0:T(8,128)}), f32[8,80,128]{2,1,0:T(8,128)S(1)}, u32[]{:S(2)}, u32[]{:S(2)}) async-start(f32[8,80,128]{2,1,0:T(8,128)} %get-tuple-element.23), calls=%async_computation | async-start | bytes 655360 | tf_op jit(solution)/shard_map/all_to_all | solution.py:692
  10.9 4.5 %collective-permute-start.2 = (f32[16,128]{1,0:T(8,128)S(1)}, f32[16,128]{1,0:T(8,128)S(1)}, u32[]{:S(2)}, u32[]{:S(2)}) collective-permute-start(f32[16,128]{1,0:T(8,128)S(1)} %get-tuple-element.27.own_ref), channel_id=1, source_target_pairs={{0,2},{2,0},{1,3},{3,1},{4,6},{6,4},{5,7},{7,5},{8,10},{10,8},{9,1... | collective-permute-start | bytes 24584 | tf_op jit(solution)/shard_map/ppermute | solution.py:718
  12.6 5.5 %collective-permute-start = (f32[160,128]{1,0:T(8,128)S(1)}, f32[160,128]{1,0:T(8,128)S(1)}, u32[]{:S(2)}, u32[]{:S(2)}) collective-permute-start(f32[160,128]{1,0:T(8,128)S(1)} %get-tuple-element.21), channel_id=1, source_target_pairs={{0,4},{8,12},{4,0},{12,8},{1,5},{9,13},{5,1},{13,9},{2,6},{10,14},... | collective-permute-start | bytes 245768 | tf_op jit(solution)/shard_map/ppermute | solution.py:715
  13.2 4.8 %collective-permute-start.1 = (f32[160,128]{1,0:T(8,128)S(1)}, f32[160,128]{1,0:T(8,128)S(1)}, u32[]{:S(2)}, u32[]{:S(2)}) collective-permute-start(f32[160,128]{1,0:T(8,128)S(1)} %get-tuple-element.22), channel_id=1, source_target_pairs={{4,8},{8,4},{5,9},{9,5},{6,10},{10,6},{7,11},{11,7},{20,24},{24,20... | collective-permute-start | bytes 245768 | tf_op jit(solution)/shard_map/ppermute | solution.py:715
  17.9 1.4 %collective-permute-start.3 = (f32[16,1792]{1,0:T(8,128)S(1)}, f32[16,1792]{1,0:T(8,128)S(1)}, u32[]{:S(2)}, u32[]{:S(2)}) collective-permute-start(f32[16,1792]{1,0:T(8,128)S(1)} %shard_map.90.mine_ref), channel_id=1, source_target_pairs={{0,1},{1,0},{2,3},{3,2},{4,5},{5,4},{6,7},{7,6},{8,9},{9,8},{10,11... | collective-permute-start | bytes 344072 | tf_op jit(solution)/shard_map/ppermute | solution.py:731
